TPU v7x, 512 devices: a whole 4x4x16 slice. The times are simulated.
512 devices in a mesh: ta: 16 (over z), aa: 32 (over y, x, core).
Axes of the slice: x: 4, y: 4, z: 16, core: 2. Of those that a mesh axis runs over, the one named last changes fastest.
Arguments:
- voltages: float32 [6144, 2, 2, 4096], P('ta', None, None, 'aa'), may hold values from -6 to 6
- taps: float32 [4, 16], replicated, may hold values from -3 to 3
- tile_map: int32 [32, 17], P('aa'), may hold values from 0 to 16, each once within a row
Outputs:
- visibilities: float32 [544, 32, 2, 128, 128], P('aa', 'ta')
Inputs may be any that keep to these rules, and one draw needn't show every extreme that they name: `tile_map`: each row holds every number 0 to 16 exactly once.
All inputs are finite; a program needn't handle non-finite values.
Results may differ from a plain program's by a relative error of at most 0.0003.
Values sent between devices are 32-bit elements; how exact they have to be, the bound alone decides.
No kernel may reach another device: no remote copies, remote signals or barrier semaphores. Data moves between devices by JAX's collectives and lax.ppermute only.
A program may use at most 128 MiB of HBM per device.

v0:
```python
import math

import jax
import jax.numpy as jnp
from jax import lax
from jax.sharding import PartitionSpec as P

TAPS = 4
FINE = 16
COARSE = 2


def shifted(block, axis, distance):
    devices = range(lax.axis_size(axis))
    route = [(i - distance, i) for i in devices if i - distance in devices]
    return lax.ppermute(block, axis, route)


def from_behind(block, axis, distance):
    devices = range(lax.axis_size(axis))
    route = [((i - distance) % len(devices), i) for i in devices]
    return lax.ppermute(block, axis, route)


def transform(summed):
    count = summed.shape[1]
    steps = jnp.arange(count, dtype=jnp.int32)
    phase = steps[:, None] * steps[None, :] % count
    theta = phase.astype(jnp.float32) * (2.0 * math.pi / count)
    cosine = jnp.cos(theta)
    sine = jnp.sin(theta)
    scale = 1.0 / math.sqrt(count)
    highest = lax.Precision.HIGHEST
    real_in = summed[:, :, :, 0]
    imag_in = summed[:, :, :, 1]
    real_out = (
        jnp.einsum("mjcb,jf->mcfb", real_in, cosine, precision=highest)
        + jnp.einsum("mjcb,jf->mcfb", imag_in, sine, precision=highest)
    ) * scale
    imag_out = (
        jnp.einsum("mjcb,jf->mcfb", imag_in, cosine, precision=highest)
        - jnp.einsum("mjcb,jf->mcfb", real_in, sine, precision=highest)
    ) * scale
    stacked = jnp.stack([real_out, imag_out], axis=3)
    array_shape = stacked.shape
    return stacked.reshape(array_shape[0], array_shape[1] * array_shape[2], 2, array_shape[4])


def correlate(left_block, right_block, total):
    block_width = left_block.shape[3]
    left_flat = left_block.reshape(left_block.shape[0], left_block.shape[1], 2 * block_width)
    right_flat = right_block.reshape(right_block.shape[0], right_block.shape[1], 2 * block_width)
    product = jnp.einsum("tcx,tcy->cxy", left_flat, right_flat, precision=lax.Precision.HIGHEST)
    real_part = product[:, :block_width, :block_width] + product[:, block_width:, block_width:]
    imag_part = product[:, block_width:, :block_width] - product[:, :block_width, block_width:]
    return jnp.stack([real_part, imag_part], axis=1) / total


def local(voltages, taps, tile_map):
    nframes = voltages.shape[0] // FINE
    block_width = voltages.shape[3]
    lead = (TAPS - 1) * FINE
    carried = shifted(voltages[voltages.shape[0] - lead :], "ta", 1)
    padded = jnp.concatenate([carried, voltages], axis=0)
    framed = padded.reshape(nframes + TAPS - 1, FINE, COARSE, 2, block_width)
    filtered = jnp.zeros((nframes, FINE, COARSE, 2, block_width), jnp.float32)
    for tap in range(TAPS):
        first = TAPS - 1 - tap
        filtered = filtered + taps[tap][None, :, None, None, None] * framed[first : first + nframes]
    spectra = transform(filtered)
    local_block = lax.all_to_all(spectra, "ta", split_axis=1, concat_axis=0, tiled=True)
    total = float(local_block.shape[0])
    block_list = lax.axis_size("aa")
    slot_count = block_list // 2 + 1
    slot_row = tile_map[0]
    slot_positions = jnp.arange(slot_count, dtype=jnp.int32)

    def place_tile(block_holder, distance, partner):
        target = jnp.sum(jnp.where(slot_row == distance, slot_positions, 0))
        tile = correlate(local_block, partner, total)
        return lax.dynamic_update_index_in_dim(block_holder, tile, target, 0)

    empty_buffer = jnp.zeros(
        (slot_count, local_block.shape[1], 2, block_width, block_width), jnp.float32
    )
    block_holder = place_tile(empty_buffer, 0, local_block)

    def advance_step(distance, state):
        travel, current = state
        travel = from_behind(travel, "aa", -1)
        return (travel, place_tile(current, distance, travel))

    closing_state = lax.fori_loop(1, slot_count, advance_step, (local_block, block_holder))
    return closing_state[1]


def solution(mesh):
    in_specs = (P("ta", None, None, "aa"), P(), P("aa", None))
    out_specs = P("aa", "ta", None, None, None)
    return jax.shard_map(local, mesh=mesh, in_specs=in_specs, out_specs=out_specs, check_vma=False)
```

profile of v0, /device:TPU:31, one launch (start us, length us, event | category | flops | bytes accessed | tf_op | source)
XLA Modules:
  0.0 379.5 jit_solution(9020434079283392916)
XLA Ops:
  0.0 1.0 slice.109
  1.0 3.5 collective-permute-start.1
  4.5 0.8 slice_bitcast_fusion.9
  5.4 0.8 collective-permute-done.1
  6.2 1.2 constant_dynamic-update-slice_fusion
  10.4 0.9 pad_maximum_fusion
  11.3 16.3 %all-to-all-start = ((f32[24,32,2,128]{3,0,2,1:T(8,128)}), f32[24,32,2,128]{3,0,2,1:T(8,128)S(1)}, u32[]{:S(2)}, u32[]{:S(2)}) async-start(f32[24,32,2,128]{3,0,2,1:T(8,128)} %pad_maximum_fusion), calls=%async_computation | async-start | bytes 1572864 | tf_op jit(solution)/shard_map/all_to_all | solution.py:71
  30.5 31.9 %all-to-all-done = f32[24,32,2,128]{3,0,2,1:T(8,128)S(1)} async-done(((f32[24,32,2,128]{3,0,2,1:T(8,128)}), f32[24,32,2,128]{3,0,2,1:T(8,128)S(1)}, u32[]{:S(2)}, u32[]{:S(2)}) %all-to-all-start) | async-done | bytes 786464 | tf_op jit(solution)/shard_map/all_to_all | solution.py:71
  63.4 1.5 fusion.51
  66.0 2.0 copy-done
  68.0 306.7 %while.16 = (s32[]{:T(128)}, f32[384,2,2,128]{3,2,0,1:T(2,128)S(1)}, f32[17,2,2,128,128]{4,3,1,2,0:T(8,128)}, f32[384,2,2,128]{0,3,2,1:T(8,128)S(1)}, s32[17]{0:T(128)S(1)}, /*index=5*/s32[]{:T(128)}, s32[]{:T(128)}, s32[]{:T(128)}) while((s32[]{:T(128)}, f32[384,2,2,128]{3,2,0,1:T(2,128)S(1)}, f32[17,2,2,128,128]{4,3,1,2,0:T(8,128)}, ...), condition=%wide.region_3.4_spmd.clone, body=%wide.region_1.3_spmd.clone.sunk | while | flops 604176448 | bytes 9699567 | solution.py:93
  68.0 6.7 %collective-permute-start = (f32[384,2,2,128]{3,2,0,1:T(2,128)S(1)}, f32[384,2,2,128]{3,2,0,1:T(2,128)S(1)}, u32[]{:S(2)}, u32[]{:S(2)}) collective-permute-start(f32[384,2,2,128]{3,2,0,1:T(2,128)S(1)} %get-tuple-element.209), channel_id=1, source_target_pairs={{1,0},{2,1},{3,2},{4,3},{5,4},{6,5},{7,6},{8,7},{9,8},{10,9},{11,1... | collective-permute-start | bytes 2359304 | tf_op jit(solution)/shard_map/while/body/eval_jaxpr/ppermute | solution.py:22
  77.3 7.3 %collective-permute-done = f32[384,2,2,128]{3,2,0,1:T(2,128)S(1)} collective-permute-done((f32[384,2,2,128]{3,2,0,1:T(2,128)S(1)}, f32[384,2,2,128]{3,2,0,1:T(2,128)S(1)}, u32[]{:S(2)}, u32[]{:S(2)}) %collective-permute-start) | collective-permute-done | bytes 786464 | tf_op jit(solution)/shard_map/while/body/eval_jaxpr/ppermute | solution.py:22
  85.2 1.1 fusion.65
  86.3 0.8 fusion.67
  87.1 1.9 collective-permute-start
  91.6 12.1 %collective-permute-done = f32[384,2,2,128]{3,2,0,1:T(2,128)S(1)} collective-permute-done((f32[384,2,2,128]{3,2,0,1:T(2,128)S(1)}, f32[384,2,2,128]{3,2,0,1:T(2,128)S(1)}, u32[]{:S(2)}, u32[]{:S(2)}) %collective-permute-start) | collective-permute-done | bytes 786464 | tf_op jit(solution)/shard_map/while/body/eval_jaxpr/ppermute | solution.py:22
  104.4 1.1 fusion.65
  106.3 1.9 collective-permute-start
  110.8 12.1 %collective-permute-done = f32[384,2,2,128]{3,2,0,1:T(2,128)S(1)} collective-permute-done((f32[384,2,2,128]{3,2,0,1:T(2,128)S(1)}, f32[384,2,2,128]{3,2,0,1:T(2,128)S(1)}, u32[]{:S(2)}, u32[]{:S(2)}) %collective-permute-start) | collective-permute-done | bytes 786464 | tf_op jit(solution)/shard_map/while/body/eval_jaxpr/ppermute | solution.py:22
  123.6 1.1 fusion.65
  125.5 1.9 collective-permute-start
  130.0 12.1 %collective-permute-done = f32[384,2,2,128]{3,2,0,1:T(2,128)S(1)} collective-permute-done((f32[384,2,2,128]{3,2,0,1:T(2,128)S(1)}, f32[384,2,2,128]{3,2,0,1:T(2,128)S(1)}, u32[]{:S(2)}, u32[]{:S(2)}) %collective-permute-start) | collective-permute-done | bytes 786464 | tf_op jit(solution)/shard_map/while/body/eval_jaxpr/ppermute | solution.py:22
  142.7 1.1 fusion.65
  144.6 1.9 collective-permute-start
  149.1 12.1 %collective-permute-done = f32[384,2,2,128]{3,2,0,1:T(2,128)S(1)} collective-permute-done((f32[384,2,2,128]{3,2,0,1:T(2,128)S(1)}, f32[384,2,2,128]{3,2,0,1:T(2,128)S(1)}, u32[]{:S(2)}, u32[]{:S(2)}) %collective-permute-start) | collective-permute-done | bytes 786464 | tf_op jit(solution)/shard_map/while/body/eval_jaxpr/ppermute | solution.py:22
  161.9 1.1 fusion.65
  163.8 1.9 collective-permute-start
  168.3 12.1 %collective-permute-done = f32[384,2,2,128]{3,2,0,1:T(2,128)S(1)} collective-permute-done((f32[384,2,2,128]{3,2,0,1:T(2,128)S(1)}, f32[384,2,2,128]{3,2,0,1:T(2,128)S(1)}, u32[]{:S(2)}, u32[]{:S(2)}) %collective-permute-start) | collective-permute-done | bytes 786464 | tf_op jit(solution)/shard_map/while/body/eval_jaxpr/ppermute | solution.py:22
  181.1 1.1 fusion.65
  182.2 0.7 fusion.67
  183.0 1.9 collective-permute-start
  187.5 12.1 %collective-permute-done = f32[384,2,2,128]{3,2,0,1:T(2,128)S(1)} collective-permute-done((f32[384,2,2,128]{3,2,0,1:T(2,128)S(1)}, f32[384,2,2,128]{3,2,0,1:T(2,128)S(1)}, u32[]{:S(2)}, u32[]{:S(2)}) %collective-permute-start) | collective-permute-done | bytes 786464 | tf_op jit(solution)/shard_map/while/body/eval_jaxpr/ppermute | solution.py:22
  200.2 1.1 fusion.65
  202.2 1.9 collective-permute-start
  206.7 12.1 %collective-permute-done = f32[384,2,2,128]{3,2,0,1:T(2,128)S(1)} collective-permute-done((f32[384,2,2,128]{3,2,0,1:T(2,128)S(1)}, f32[384,2,2,128]{3,2,0,1:T(2,128)S(1)}, u32[]{:S(2)}, u32[]{:S(2)}) %collective-permute-start) | collective-permute-done | bytes 786464 | tf_op jit(solution)/shard_map/while/body/eval_jaxpr/ppermute | solution.py:22
  219.4 1.1 fusion.65
  220.5 0.7 fusion.67
  221.3 1.9 collective-permute-start
  225.8 12.1 %collective-permute-done = f32[384,2,2,128]{3,2,0,1:T(2,128)S(1)} collective-permute-done((f32[384,2,2,128]{3,2,0,1:T(2,128)S(1)}, f32[384,2,2,128]{3,2,0,1:T(2,128)S(1)}, u32[]{:S(2)}, u32[]{:S(2)}) %collective-permute-start) | collective-permute-done | bytes 786464 | tf_op jit(solution)/shard_map/while/body/eval_jaxpr/ppermute | solution.py:22
  238.6 1.1 fusion.65
  240.5 1.9 collective-permute-start
  245.0 12.1 %collective-permute-done = f32[384,2,2,128]{3,2,0,1:T(2,128)S(1)} collective-permute-done((f32[384,2,2,128]{3,2,0,1:T(2,128)S(1)}, f32[384,2,2,128]{3,2,0,1:T(2,128)S(1)}, u32[]{:S(2)}, u32[]{:S(2)}) %collective-permute-start) | collective-permute-done | bytes 786464 | tf_op jit(solution)/shard_map/while/body/eval_jaxpr/ppermute | solution.py:22
  257.8 1.1 fusion.65
  259.7 1.9 collective-permute-start
  264.2 12.1 %collective-permute-done = f32[384,2,2,128]{3,2,0,1:T(2,128)S(1)} collective-permute-done((f32[384,2,2,128]{3,2,0,1:T(2,128)S(1)}, f32[384,2,2,128]{3,2,0,1:T(2,128)S(1)}, u32[]{:S(2)}, u32[]{:S(2)}) %collective-permute-start) | collective-permute-done | bytes 786464 | tf_op jit(solution)/shard_map/while/body/eval_jaxpr/ppermute | solution.py:22
  276.9 1.1 fusion.65
  278.0 0.7 fusion.67
  278.8 1.9 collective-permute-start
  283.3 12.1 %collective-permute-done = f32[384,2,2,128]{3,2,0,1:T(2,128)S(1)} collective-permute-done((f32[384,2,2,128]{3,2,0,1:T(2,128)S(1)}, f32[384,2,2,128]{3,2,0,1:T(2,128)S(1)}, u32[]{:S(2)}, u32[]{:S(2)}) %collective-permute-start) | collective-permute-done | bytes 786464 | tf_op jit(solution)/shard_map/while/body/eval_jaxpr/ppermute | solution.py:22
  296.1 1.1 fusion.65
  298.0 1.9 collective-permute-start
  302.5 12.1 %collective-permute-done = f32[384,2,2,128]{3,2,0,1:T(2,128)S(1)} collective-permute-done((f32[384,2,2,128]{3,2,0,1:T(2,128)S(1)}, f32[384,2,2,128]{3,2,0,1:T(2,128)S(1)}, u32[]{:S(2)}, u32[]{:S(2)}) %collective-permute-start) | collective-permute-done | bytes 786464 | tf_op jit(solution)/shard_map/while/body/eval_jaxpr/ppermute | solution.py:22
  315.3 1.1 fusion.65
  317.2 1.9 collective-permute-start
  321.7 12.1 %collective-permute-done = f32[384,2,2,128]{3,2,0,1:T(2,128)S(1)} collective-permute-done((f32[384,2,2,128]{3,2,0,1:T(2,128)S(1)}, f32[384,2,2,128]{3,2,0,1:T(2,128)S(1)}, u32[]{:S(2)}, u32[]{:S(2)}) %collective-permute-start) | collective-permute-done | bytes 786464 | tf_op jit(solution)/shard_map/while/body/eval_jaxpr/ppermute | solution.py:22
  334.4 1.1 fusion.65
  336.3 1.9 collective-permute-start
  340.8 12.1 %collective-permute-done = f32[384,2,2,128]{3,2,0,1:T(2,128)S(1)} collective-permute-done((f32[384,2,2,128]{3,2,0,1:T(2,128)S(1)}, f32[384,2,2,128]{3,2,0,1:T(2,128)S(1)}, u32[]{:S(2)}, u32[]{:S(2)}) %collective-permute-start) | collective-permute-done | bytes 786464 | tf_op jit(solution)/shard_map/while/body/eval_jaxpr/ppermute | solution.py:22
  353.6 1.1 fusion.65
  355.5 1.9 collective-permute-start
  360.0 12.1 %collective-permute-done = f32[384,2,2,128]{3,2,0,1:T(2,128)S(1)} collective-permute-done((f32[384,2,2,128]{3,2,0,1:T(2,128)S(1)}, f32[384,2,2,128]{3,2,0,1:T(2,128)S(1)}, u32[]{:S(2)}, u32[]{:S(2)}) %collective-permute-start) | collective-permute-done | bytes 786464 | tf_op jit(solution)/shard_map/while/body/eval_jaxpr/ppermute | solution.py:22
  372.8 1.1 fusion.65
  374.7 4.9 %copy.31 = f32[17,2,2,128,128]{4,3,2,1,0:T(8,128)} copy(f32[17,2,2,128,128]{4,3,1,2,0:T(8,128)} %get-tuple-element.114) | data formatting | bytes 8912896 | tf_op jit(solution)/shard_map/while | solution.py:93
  (98 shorter events, 36.0 us)
Async XLA Ops:
  0.0 7.5 %copy-start.1 = (f32[384,2,2,128]{3,2,1,0:T(2,128)S(1)}, f32[384,2,2,128]{3,2,1,0:T(2,128)}, u32[]{:S(2)}) copy-start(f32[384,2,2,128]{3,2,1,0:T(2,128)} %param.5) | copy-start | bytes 2359300
  1.0 5.2 %collective-permute-start.1 = (f32[48,2,2,128]{3,0,2,1:T(8,128)S(1)}, f32[48,2,2,128]{3,0,2,1:T(8,128)S(1)}, u32[]{:S(2)}, u32[]{:S(2)}) collective-permute-start(f32[48,2,2,128]{3,0,2,1:T(8,128)S(1)} %copy.55), channel_id=1, source_target_pairs={{0,32},{32,64},{64,96},{96,128},{128,160},{160,192},{192,224},{224... | collective-permute-start | bytes 294920 | tf_op jit(solution)/shard_map/ppermute | solution.py:16
  7.8 19.9 %copy-start.2 = (s32[1,17]{1,0:T(1,128)S(1)}, s32[1,17]{1,0:T(1,128)}, u32[]{:S(2)}) copy-start(s32[1,17]{1,0:T(1,128)} %param.7) | copy-start | bytes 208
  11.3 51.0 %all-to-all-start = ((f32[24,32,2,128]{3,0,2,1:T(8,128)}), f32[24,32,2,128]{3,0,2,1:T(8,128)S(1)}, u32[]{:S(2)}, u32[]{:S(2)}) async-start(f32[24,32,2,128]{3,0,2,1:T(8,128)} %pad_maximum_fusion), calls=%async_computation | async-start | bytes 1572864 | tf_op jit(solution)/shard_map/all_to_all | solution.py:71
  65.9 2.0 copy-start
  68.0 16.6 %collective-permute-start = (f32[384,2,2,128]{3,2,0,1:T(2,128)S(1)}, f32[384,2,2,128]{3,2,0,1:T(2,128)S(1)}, u32[]{:S(2)}, u32[]{:S(2)}) collective-permute-start(f32[384,2,2,128]{3,2,0,1:T(2,128)S(1)} %get-tuple-element.209), channel_id=1, source_target_pairs={{1,0},{2,1},{3,2},{4,3},{5,4},{6,5},{7,6},{8,7},{9,8},{10,9},{11,1... | collective-permute-start | bytes 2359304 | tf_op jit(solution)/shard_map/while/body/eval_jaxpr/ppermute | solution.py:22
  87.1 16.6 %collective-permute-start = (f32[384,2,2,128]{3,2,0,1:T(2,128)S(1)}, f32[384,2,2,128]{3,2,0,1:T(2,128)S(1)}, u32[]{:S(2)}, u32[]{:S(2)}) collective-permute-start(f32[384,2,2,128]{3,2,0,1:T(2,128)S(1)} %get-tuple-element.209), channel_id=1, source_target_pairs={{1,0},{2,1},{3,2},{4,3},{5,4},{6,5},{7,6},{8,7},{9,8},{10,9},{11,1... | collective-permute-start | bytes 2359304 | tf_op jit(solution)/shard_map/while/body/eval_jaxpr/ppermute | solution.py:22
  106.3 16.6 %collective-permute-start = (f32[384,2,2,128]{3,2,0,1:T(2,128)S(1)}, f32[384,2,2,128]{3,2,0,1:T(2,128)S(1)}, u32[]{:S(2)}, u32[]{:S(2)}) collective-permute-start(f32[384,2,2,128]{3,2,0,1:T(2,128)S(1)} %get-tuple-element.209), channel_id=1, source_target_pairs={{1,0},{2,1},{3,2},{4,3},{5,4},{6,5},{7,6},{8,7},{9,8},{10,9},{11,1... | collective-permute-start | bytes 2359304 | tf_op jit(solution)/shard_map/while/body/eval_jaxpr/ppermute | solution.py:22
  125.5 16.6 %collective-permute-start = (f32[384,2,2,128]{3,2,0,1:T(2,128)S(1)}, f32[384,2,2,128]{3,2,0,1:T(2,128)S(1)}, u32[]{:S(2)}, u32[]{:S(2)}) collective-permute-start(f32[384,2,2,128]{3,2,0,1:T(2,128)S(1)} %get-tuple-element.209), channel_id=1, source_target_pairs={{1,0},{2,1},{3,2},{4,3},{5,4},{6,5},{7,6},{8,7},{9,8},{10,9},{11,1... | collective-permute-start | bytes 2359304 | tf_op jit(solution)/shard_map/while/body/eval_jaxpr/ppermute | solution.py:22
  144.6 16.6 %collective-permute-start = (f32[384,2,2,128]{3,2,0,1:T(2,128)S(1)}, f32[384,2,2,128]{3,2,0,1:T(2,128)S(1)}, u32[]{:S(2)}, u32[]{:S(2)}) collective-permute-start(f32[384,2,2,128]{3,2,0,1:T(2,128)S(1)} %get-tuple-element.209), channel_id=1, source_target_pairs={{1,0},{2,1},{3,2},{4,3},{5,4},{6,5},{7,6},{8,7},{9,8},{10,9},{11,1... | collective-permute-start | bytes 2359304 | tf_op jit(solution)/shard_map/while/body/eval_jaxpr/ppermute | solution.py:22
  163.8 16.6 %collective-permute-start = (f32[384,2,2,128]{3,2,0,1:T(2,128)S(1)}, f32[384,2,2,128]{3,2,0,1:T(2,128)S(1)}, u32[]{:S(2)}, u32[]{:S(2)}) collective-permute-start(f32[384,2,2,128]{3,2,0,1:T(2,128)S(1)} %get-tuple-element.209), channel_id=1, source_target_pairs={{1,0},{2,1},{3,2},{4,3},{5,4},{6,5},{7,6},{8,7},{9,8},{10,9},{11,1... | collective-permute-start | bytes 2359304 | tf_op jit(solution)/shard_map/while/body/eval_jaxpr/ppermute | solution.py:22
  183.0 16.6 %collective-permute-start = (f32[384,2,2,128]{3,2,0,1:T(2,128)S(1)}, f32[384,2,2,128]{3,2,0,1:T(2,128)S(1)}, u32[]{:S(2)}, u32[]{:S(2)}) collective-permute-start(f32[384,2,2,128]{3,2,0,1:T(2,128)S(1)} %get-tuple-element.209), channel_id=1, source_target_pairs={{1,0},{2,1},{3,2},{4,3},{5,4},{6,5},{7,6},{8,7},{9,8},{10,9},{11,1... | collective-permute-start | bytes 2359304 | tf_op jit(solution)/shard_map/while/body/eval_jaxpr/ppermute | solution.py:22
  202.2 16.6 %collective-permute-start = (f32[384,2,2,128]{3,2,0,1:T(2,128)S(1)}, f32[384,2,2,128]{3,2,0,1:T(2,128)S(1)}, u32[]{:S(2)}, u32[]{:S(2)}) collective-permute-start(f32[384,2,2,128]{3,2,0,1:T(2,128)S(1)} %get-tuple-element.209), channel_id=1, source_target_pairs={{1,0},{2,1},{3,2},{4,3},{5,4},{6,5},{7,6},{8,7},{9,8},{10,9},{11,1... | collective-permute-start | bytes 2359304 | tf_op jit(solution)/shard_map/while/body/eval_jaxpr/ppermute | solution.py:22
  221.3 16.6 %collective-permute-start = (f32[384,2,2,128]{3,2,0,1:T(2,128)S(1)}, f32[384,2,2,128]{3,2,0,1:T(2,128)S(1)}, u32[]{:S(2)}, u32[]{:S(2)}) collective-permute-start(f32[384,2,2,128]{3,2,0,1:T(2,128)S(1)} %get-tuple-element.209), channel_id=1, source_target_pairs={{1,0},{2,1},{3,2},{4,3},{5,4},{6,5},{7,6},{8,7},{9,8},{10,9},{11,1... | collective-permute-start | bytes 2359304 | tf_op jit(solution)/shard_map/while/body/eval_jaxpr/ppermute | solution.py:22
  240.5 16.6 %collective-permute-start = (f32[384,2,2,128]{3,2,0,1:T(2,128)S(1)}, f32[384,2,2,128]{3,2,0,1:T(2,128)S(1)}, u32[]{:S(2)}, u32[]{:S(2)}) collective-permute-start(f32[384,2,2,128]{3,2,0,1:T(2,128)S(1)} %get-tuple-element.209), channel_id=1, source_target_pairs={{1,0},{2,1},{3,2},{4,3},{5,4},{6,5},{7,6},{8,7},{9,8},{10,9},{11,1... | collective-permute-start | bytes 2359304 | tf_op jit(solution)/shard_map/while/body/eval_jaxpr/ppermute | solution.py:22
  259.7 16.6 %collective-permute-start = (f32[384,2,2,128]{3,2,0,1:T(2,128)S(1)}, f32[384,2,2,128]{3,2,0,1:T(2,128)S(1)}, u32[]{:S(2)}, u32[]{:S(2)}) collective-permute-start(f32[384,2,2,128]{3,2,0,1:T(2,128)S(1)} %get-tuple-element.209), channel_id=1, source_target_pairs={{1,0},{2,1},{3,2},{4,3},{5,4},{6,5},{7,6},{8,7},{9,8},{10,9},{11,1... | collective-permute-start | bytes 2359304 | tf_op jit(solution)/shard_map/while/body/eval_jaxpr/ppermute | solution.py:22
  278.8 16.6 %collective-permute-start = (f32[384,2,2,128]{3,2,0,1:T(2,128)S(1)}, f32[384,2,2,128]{3,2,0,1:T(2,128)S(1)}, u32[]{:S(2)}, u32[]{:S(2)}) collective-permute-start(f32[384,2,2,128]{3,2,0,1:T(2,128)S(1)} %get-tuple-element.209), channel_id=1, source_target_pairs={{1,0},{2,1},{3,2},{4,3},{5,4},{6,5},{7,6},{8,7},{9,8},{10,9},{11,1... | collective-permute-start | bytes 2359304 | tf_op jit(solution)/shard_map/while/body/eval_jaxpr/ppermute | solution.py:22
  298.0 16.6 %collective-permute-start = (f32[384,2,2,128]{3,2,0,1:T(2,128)S(1)}, f32[384,2,2,128]{3,2,0,1:T(2,128)S(1)}, u32[]{:S(2)}, u32[]{:S(2)}) collective-permute-start(f32[384,2,2,128]{3,2,0,1:T(2,128)S(1)} %get-tuple-element.209), channel_id=1, source_target_pairs={{1,0},{2,1},{3,2},{4,3},{5,4},{6,5},{7,6},{8,7},{9,8},{10,9},{11,1... | collective-permute-start | bytes 2359304 | tf_op jit(solution)/shard_map/while/body/eval_jaxpr/ppermute | solution.py:22
  317.2 16.6 %collective-permute-start = (f32[384,2,2,128]{3,2,0,1:T(2,128)S(1)}, f32[384,2,2,128]{3,2,0,1:T(2,128)S(1)}, u32[]{:S(2)}, u32[]{:S(2)}) collective-permute-start(f32[384,2,2,128]{3,2,0,1:T(2,128)S(1)} %get-tuple-element.209), channel_id=1, source_target_pairs={{1,0},{2,1},{3,2},{4,3},{5,4},{6,5},{7,6},{8,7},{9,8},{10,9},{11,1... | collective-permute-start | bytes 2359304 | tf_op jit(solution)/shard_map/while/body/eval_jaxpr/ppermute | solution.py:22
  336.3 16.6 %collective-permute-start = (f32[384,2,2,128]{3,2,0,1:T(2,128)S(1)}, f32[384,2,2,128]{3,2,0,1:T(2,128)S(1)}, u32[]{:S(2)}, u32[]{:S(2)}) collective-permute-start(f32[384,2,2,128]{3,2,0,1:T(2,128)S(1)} %get-tuple-element.209), channel_id=1, source_target_pairs={{1,0},{2,1},{3,2},{4,3},{5,4},{6,5},{7,6},{8,7},{9,8},{10,9},{11,1... | collective-permute-start | bytes 2359304 | tf_op jit(solution)/shard_map/while/body/eval_jaxpr/ppermute | solution.py:22
  355.5 16.6 %collective-permute-start = (f32[384,2,2,128]{3,2,0,1:T(2,128)S(1)}, f32[384,2,2,128]{3,2,0,1:T(2,128)S(1)}, u32[]{:S(2)}, u32[]{:S(2)}) collective-permute-start(f32[384,2,2,128]{3,2,0,1:T(2,128)S(1)} %get-tuple-element.209), channel_id=1, source_target_pairs={{1,0},{2,1},{3,2},{4,3},{5,4},{6,5},{7,6},{8,7},{9,8},{10,9},{11,1... | collective-permute-start | bytes 2359304 | tf_op jit(solution)/shard_map/while/body/eval_jaxpr/ppermute | solution.py:22
where the time goes:
time: 381 us; the launch traced here: 380 us
  waiting for transfers between devices  222 us (58%)
  starting transfers between devices  55.4 us (15%)
  loops' own time  31.8 us (8%)
  other arithmetic  24.3 us (6%)
  local copies, waits for them, and re-layouts  23.4 us (6%)
  matrix products  20.6 us (5%)
    ppermute x16, waiting for transfers between devices, from_behind(): return lax.ppermute(block, axis, route)  189 us
    ppermute x16, starting transfers between devices, from_behind(): return lax.ppermute(block, axis, route)  35.5 us
    all_to_all x1, waiting for transfers between devices, local(): lax.all_to_all(spectra, 'ta', split_axis=1, concat_axis=0, tiled=True)  31.9 us
    another operation x1, loops' own time, local(): lax.fori_loop(1, slot_count, advance_step, (local_block, block_holder))  31.8 us
    dot_general x17, matrix products, correlate(): jnp.einsum('tcx,tcy->cxy', left_flat, right_flat, precision=lax.Precision...  18.5 us
    all_to_all x1, starting transfers between devices, local(): lax.all_to_all(spectra, 'ta', split_axis=1, concat_axis=0, tiled=True)  16.3 us
    dynamic_update_slice x17, other arithmetic, place_tile(): return lax.dynamic_update_index_in_dim(block_holder, tile, target, 0)  11.7 us
    reduce_sum x17, other arithmetic, place_tile(): target = jnp.sum(jnp.where(slot_row == distance, slot_positions, 0))  10.8 us
  transfers between devices with their start and end apart: 18, of which 18 were waited for; matrix products, arithmetic and copies ran while one was open for 3% of the time, Pallas kernels for 0%

commit v1 on v0

v1 whole, which is shorter than its diff:
```python
import functools
import math

import jax
import jax.numpy as jnp
import numpy as np
from jax import lax
from jax.experimental import pallas as pl
from jax.experimental.pallas import tpu as pltpu
from jax.sharding import PartitionSpec as P

TAPS = 4
FINE = 16
COARSE = 2
NX = 4
CHIPS = 16
PAIRS = CHIPS // 2 + 1


def dft_rows(frames):
    groups = COARSE * FINE // 2
    w = np.zeros((2, 2, groups, frames, frames, FINE, COARSE, 2), np.float64)
    j = np.arange(FINE)
    for k in range(2):
        for g in range(groups):
            c, f = g // (FINE // 2), 2 * (g % (FINE // 2)) + k
            theta = 2.0 * math.pi * ((j * f) % FINE) / FINE
            cosine, sine = np.cos(theta) / math.sqrt(FINE), np.sin(theta) / math.sqrt(FINE)
            for m in range(frames):
                w[k, 0, g, m, m, :, c, 0] = cosine
                w[k, 0, g, m, m, :, c, 1] = sine
                w[k, 1, g, m, m, :, c, 0] = -sine
                w[k, 1, g, m, m, :, c, 1] = cosine
    return w.reshape(2, 2, groups * frames, frames * FINE * COARSE * 2).astype(np.float32)


def spectra_kernel(k_ref, own_ref, other_ref, own_lead_ref, other_lead_ref, taps_ref, w_ref, out_ref, pad):
    first = k_ref[0] == 0
    lead = own_lead_ref.shape[0]
    lanes = own_ref.shape[1]
    for source, mate, rows in (
        (own_lead_ref, other_lead_ref, pl.ds(0, lead)),
        (own_ref, other_ref, pl.ds(lead, own_ref.shape[0])),
    ):
        a, b = source[...], mate[...]
        pad[rows, 0:lanes] = jnp.where(first, a, b)
        pad[rows, lanes : 2 * lanes] = jnp.where(first, b, a)
    frame = taps_ref.shape[1]
    chunk = w_ref.shape[3]
    per = chunk // frame
    groups = out_ref.shape[0]
    tap_rows = [jnp.concatenate([taps_ref[p], taps_ref[p]], axis=1)[None] for p in range(TAPS)]
    for part in range(own_ref.shape[0] // chunk):
        total = None
        for p in range(TAPS):
            rows = pad[pl.ds(part * chunk + (TAPS - 1 - p) * frame, chunk), :]
            term = tap_rows[p] * rows.reshape(per, frame, 2 * lanes)
            total = term if total is None else total + term
        total = total.reshape(chunk, 2 * lanes)
        for ri in range(2):
            result = jnp.dot(
                w_ref[0, ri], total, precision=lax.Precision.HIGHEST, preferred_element_type=jnp.float32
            )
            out_ref[:, pl.ds(part * per, per), pl.ds(ri * 2 * lanes, 2 * lanes)] = result.reshape(
                groups, per, 2 * lanes
            )


def spectra_of(k, own, other, own_lead, other_lead, taps):
    frames = 8
    rows, lanes = own.shape
    w = jnp.asarray(dft_rows(frames))
    tap_rows = jnp.broadcast_to(jnp.repeat(taps, COARSE * 2, axis=1)[:, :, None], (TAPS, FINE * COARSE * 2, lanes))
    groups = COARSE * FINE // 2
    whole = lambda shape: pl.BlockSpec(shape, lambda i, k: (0,) * len(shape))
    return pl.pallas_call(
        spectra_kernel,
        out_shape=jax.ShapeDtypeStruct((groups, rows // (FINE * COARSE * 2), 4 * lanes), jnp.float32),
        grid_spec=pltpu.PrefetchScalarGridSpec(
            num_scalar_prefetch=1,
            grid=(1,),
            in_specs=[
                whole(own.shape),
                whole(other.shape),
                whole(own_lead.shape),
                whole(other_lead.shape),
                whole(tap_rows.shape),
                pl.BlockSpec((1,) + w.shape[1:], lambda i, k: (k[0], 0, 0, 0)),
            ],
            out_specs=whole((groups, rows // (FINE * COARSE * 2), 4 * lanes)),
            scratch_shapes=[pltpu.VMEM((rows + own_lead.shape[0], 2 * lanes), jnp.float32)],
        ),
        compiler_params=pltpu.CompilerParams(vmem_limit_bytes=32 * 2**20),
    )(k, own, other, own_lead, other_lead, tap_rows, w)


def split(x):
    high = x.astype(jnp.bfloat16)
    return high, (x - high.astype(jnp.float32)).astype(jnp.bfloat16)


def correlate_kernel(scale, at_ref, left_ref, right_ref, own_ref, send_ref, left_high, left_low):
    width = left_ref.shape[1] // 2
    half = width // 2
    total = left_ref.shape[0]

    @pl.when(pl.program_id(0) == 0)
    def _():
        turned = left_ref[...].T
        real_high, real_low = split(turned[:width] * scale)
        imag_high, imag_low = split(turned[width:] * scale)
        for store, real, imag in ((left_high, real_high, imag_high), (left_low, real_low, imag_low)):
            store[0:width, 0:total] = real
            store[0:width, total : 2 * total] = imag
            store[width : 2 * width, 0:total] = imag
            store[width : 2 * width, total : 2 * total] = -real

    right = right_ref[0]
    high, low = split(jnp.concatenate([right[:, :width], right[:, width:]], axis=0))
    dot = functools.partial(jnp.dot, preferred_element_type=jnp.float32)
    product = dot(left_high[...], high) + dot(left_high[...], low) + dot(left_low[...], high)
    first = at_ref[0] == 0

    for mine, goal in ((True, own_ref), (False, send_ref)):
        for r in range(2):
            for ri in range(2):
                rows0 = product[ri * width : ri * width + half, r * half : (r + 1) * half]
                rows1 = product[ri * width + half : (ri + 1) * width, r * half : (r + 1) * half]
                goal[r, ri] = jnp.where(first, rows0, rows1) if mine else jnp.where(first, rows1, rows0)


def correlated(at, left, rights, spectra_count):
    rows, lanes = left.shape
    half = lanes // 4
    tiles = jax.ShapeDtypeStruct((2 * PAIRS, 2, half, half), jnp.float32)
    return pl.pallas_call(
        functools.partial(correlate_kernel, 1.0 / spectra_count),
        out_shape=(tiles, tiles),
        grid_spec=pltpu.PrefetchScalarGridSpec(
            num_scalar_prefetch=1,
            grid=(PAIRS,),
            in_specs=[
                pl.BlockSpec((rows, lanes), lambda e, at: (0, 0)),
                pl.BlockSpec((1, rows, lanes), lambda e, at: (lax.rem(at[1] + e, CHIPS), 0, 0)),
            ],
            out_specs=[pl.BlockSpec((2, 2, half, half), lambda e, at: (e, 0, 0, 0))] * 2,
            scratch_shapes=[pltpu.VMEM((lanes, 2 * rows), jnp.bfloat16)] * 2,
        ),
        compiler_params=pltpu.CompilerParams(vmem_limit_bytes=40 * 2**20),
    )(at, left, rights)


def place_kernel(at_ref, map_ref, own_ref, got_ref, out_ref, sems):
    k = at_ref[0]
    slots = out_ref.shape[0]
    copies = []
    for s in range(slots):
        tile = map_ref[s] + k
        copies.append(pltpu.make_async_copy(own_ref.at[tile], out_ref.at[s, k], sems.at[2 * s]))
        copies.append(pltpu.make_async_copy(got_ref.at[tile], out_ref.at[s, 1 - k], sems.at[2 * s + 1]))
    for copy in copies:
        copy.start()
    for copy in copies:
        copy.wait()


def placed(at, slot_row, own, got):
    slots = slot_row.shape[0]
    half = own.shape[-1]
    return pl.pallas_call(
        place_kernel,
        out_shape=jax.ShapeDtypeStruct((slots, 2, 2, half, half), jnp.float32),
        grid_spec=pltpu.PrefetchScalarGridSpec(
            num_scalar_prefetch=2,
            grid=(1,),
            in_specs=[pl.BlockSpec(memory_space=pl.ANY)] * 2,
            out_specs=pl.BlockSpec(memory_space=pl.ANY),
            scratch_shapes=[pltpu.SemaphoreType.DMA((2 * slots,))],
        ),
    )(at, slot_row, own, got)


def local(voltages, taps, tile_map):
    n_ta, n_aa = lax.axis_size("ta"), lax.axis_size("aa")
    me = lax.axis_index("aa").astype(jnp.int32)
    k = lax.rem(me, 2)
    at = jnp.stack([k, me // 2])
    samples, coarse, parts, lanes = voltages.shape
    own = voltages.reshape(samples * coarse * parts, lanes)
    lead = own[own.shape[0] - (TAPS - 1) * FINE * coarse * parts :]
    mate = [(i, i ^ 1) for i in range(n_aa)]
    other = lax.ppermute(own, "aa", mate)
    own_lead = lax.ppermute(lead, "ta", [(t, t + 1) for t in range(n_ta - 1)])
    other_lead = lax.ppermute(own_lead, "aa", mate)
    spectra = spectra_of(at, own, other, own_lead, other_lead, taps)
    block = lax.all_to_all(spectra, "ta", split_axis=0, concat_axis=0, tiled=True)
    block = block.reshape(-1, 4 * lanes)
    same_core = [[2 * c + core for c in range(n_aa // 2)] for core in range(2)]
    gathered = lax.all_gather(block, "aa", axis_index_groups=same_core)
    own_tiles, send_tiles = correlated(at, block, gathered, block.shape[0])
    got_tiles = lax.ppermute(send_tiles, "aa", mate)
    return placed(at, tile_map[0], own_tiles, got_tiles)


def solution(mesh):
    in_specs = (P("ta", None, None, "aa"), P(), P("aa", None))
    out_specs = P("aa", "ta", None, None, None)
    return jax.shard_map(local, mesh=mesh, in_specs=in_specs, out_specs=out_specs, check_vma=False)
```

time: 381 us -> 349 us (0.916)
  the two profiles are of different devices: /device:TPU:31 before, /device:TPU:1 now
where the time goes in v1:
time: 349 us
  Pallas kernels  150 us (43%)
  waiting for transfers between devices  112 us (32%)
  blocking collectives  49.2 us (14%)
  starting transfers between devices  15.1 us (4%)
  between operations  13.5 us (4%)
  local copies, waits for them, and re-layouts  8.15 us (2%)
    pallas_call x1, Pallas kernels, placed(): pl.pallas_call(place_kernel, out_shape=jax.ShapeDtypeStruct((slots, 2, 2,...  137 us
    all_gather x1, waiting for transfers between devices, local(): gathered = lax.all_gather(block, 'aa', axis_index_groups=same_core)  106 us
    all_to_all x1, blocking collectives, local(): lax.all_to_all(spectra, 'ta', split_axis=0, concat_axis=0, tiled=True)  49.2 us
    pallas_call x1, Pallas kernels, correlated(): pl.pallas_call(functools.partial(correlate_kernel, 1.0 / spectra_count),...  10.6 us
    ppermute x1, starting transfers between devices, local(): other = lax.ppermute(own, 'aa', mate)  8.78 us
  transfers between devices with their start and end apart: 5, of which 4 were waited for; matrix products, arithmetic and copies ran while one was open for 1% of the time, Pallas kernels for 0%

profile of v1, /device:TPU:1, one launch (start us, length us, event | category | flops | bytes accessed | tf_op | source)
XLA Modules:
  0.0 348.9 jit_solution(8410785568387072767)
XLA Ops:
  6.5 0.0 all-gather.2.cloned.1.call-start
  6.5 8.8 %collective-permute-start = (f32[1536,128]{1,0:T(8,128)}, f32[1536,128]{1,0:T(8,128)S(1)}, u32[]{:S(2)}, u32[]{:S(2)}) collective-permute-start(f32[1536,128]{1,0:T(8,128)} %bitcast.9), channel_id=1, source_target_pairs={{0,1},{1,0},{2,3},{3,2},{4,5},{5,4},{6,7},{7,6},{8,9},{9,8},{10,11... | collective-permute-start | bytes 2359304 | tf_op jit(solution)/shard_map/ppermute | solution.py:192
  15.3 0.9 slice.6
  16.2 1.3 collective-permute-start.1
  17.5 0.8 broadcast_in_dim.10
  18.3 0.1 broadcast_in_dim.11
  18.4 1.5 collective-permute-done.1.own_lead_ref
  19.9 2.5 collective-permute-start.2
  22.4 0.1 pad_add_fusion.k_ref.at_ref
  22.5 0.0 copy-start.4
  22.5 0.8 collective-permute-done.2.other_lead_ref
  23.3 0.0 collective-permute-done.other_ref
  23.3 0.1 broadcast_in_dim.12.taps_ref
  23.4 0.0 copy-start.2
  23.4 1.2 copy-done.2
  24.7 0.0 copy-start.3
  24.7 1.1 copy-done.3
  25.8 2.7 shard_map.46
  28.5 49.2 %all_to_all.5 = f32[16,24,512]{2,1,0:T(8,128)} all-to-all(f32[16,24,512]{2,1,0:T(8,128)S(1)} %shard_map.46), channel_id=1, replica_groups=mesh['ta'=16,'aa'=32] {'ta'}, dimensions={0} | all-to-all | bytes 1572864 | tf_op jit(solution)/shard_map/all_to_all | solution.py:196
  77.7 0.0 all-gather.2.cloned.1.call-update
  77.8 105.9 %all-gather.2.cloned.1.call-done.right_ref = f32[16,384,512]{2,1,0:T(8,128)} async-done(((f32[1,384,512]{2,1,0:T(8,128)}), f32[16,384,512]{2,1,0:T(8,128)}) %all-gather.2.cloned.1.call-update) | async-done | bytes 12582928 | tf_op jit(solution)/shard_map/all_gather | solution.py:199
  183.6 0.0 copy-done.4
  183.6 0.0 copy-start
  183.6 1.1 copy-done
  184.8 10.6 %shard_map.47 = (f32[18,2,128,128]{3,2,1,0:T(8,128)S(1)}, f32[18,2,128,128]{3,2,1,0:T(8,128)S(1)}) custom-call(s32[2]{0:T(128)S(1)} %pad_add_fusion.k_ref.at_ref, f32[384,512]{1,0:T(8,128)S(1)} %bitcast.8, f32[16,384,512]{2,1,0:T(8,128)} %all-gather.2.cloned.1.call-done.right_ref), custom_call_target="tpu_custom_call" | custom-call | tf_op jit(solution)/shard_map/pallas_call | solution.py:136
  195.4 0.0 copy-start.1
  195.4 1.4 copy-done.1
  196.8 2.6 collective-permute-start.3
  199.4 4.1 %collective-permute-done.3.got_ref = f32[18,2,128,128]{3,2,1,0:T(8,128)S(1)} collective-permute-done((f32[18,2,128,128]{3,2,1,0:T(8,128)S(1)}, f32[18,2,128,128]{3,2,1,0:T(8,128)S(1)}, u32[]{:S(2)}, u32[]{:S(2)}) %collective-permute-start.3) | collective-permute-done | bytes 2359328 | tf_op jit(solution)/shard_map/ppermute | solution.py:201
  203.5 0.0 copy-start.5
  203.5 1.4 copy-done.5
  204.9 137.1 %shard_map.48 = f32[17,2,2,128,128]{4,3,2,1,0:T(8,128)} custom-call(s32[2]{0:T(128)} %copy-done.4, s32[17]{0:T(128)} %bitcast.12, f32[18,2,128,128]{3,2,1,0:T(8,128)} %copy-done.1, f32[18,2,128,128]{3,2,1,0:T(8,128)} %copy-done.5), custom_call_target="tpu_custom_call" | custom-call | tf_op jit(solution)/shard_map/pallas_call | solution.py:170
Async XLA Ops:
  6.5 177.1 %all-gather.2.cloned.1.call-start = ((), (), s32[]{:S(2)}) async-start(), calls=%async_computation.1 | async-start | bytes 13369344 | tf_op jit(solution)/shard_map/all_gather | solution.py:199
  6.5 16.8 %collective-permute-start = (f32[1536,128]{1,0:T(8,128)}, f32[1536,128]{1,0:T(8,128)S(1)}, u32[]{:S(2)}, u32[]{:S(2)}) collective-permute-start(f32[1536,128]{1,0:T(8,128)} %bitcast.9), channel_id=1, source_target_pairs={{0,1},{1,0},{2,3},{3,2},{4,5},{5,4},{6,7},{7,6},{8,9},{9,8},{10,11... | collective-permute-start | bytes 2359304 | tf_op jit(solution)/shard_map/ppermute | solution.py:192
  16.2 3.7 %collective-permute-start.1 = (f32[192,128]{1,0:T(8,128)S(1)}, f32[192,128]{1,0:T(8,128)S(1)}, u32[]{:S(2)}, u32[]{:S(2)}) collective-permute-start(f32[192,128]{1,0:T(8,128)S(1)} %bitcast.11), channel_id=1, source_target_pairs={{0,32},{32,64},{64,96},{96,128},{128,160},{160,192},{192,224},{224... | collective-permute-start | bytes 294920 | tf_op jit(solution)/shard_map/ppermute | solution.py:193
  19.9 3.4 collective-permute-start.2
  22.5 161.2 %copy-start.4 = (s32[2]{0:T(128)}, s32[2]{0:T(128)S(1)}, u32[]{:S(2)}) copy-start(s32[2]{0:T(128)S(1)} %pad_add_fusion.k_ref.at_ref) | copy-start | bytes 28
  23.4 1.2 copy-start.2
  24.7 1.1 copy-start.3
  183.6 1.1 copy-start
  195.4 1.4 copy-start.1
  196.8 6.7 %collective-permute-start.3 = (f32[18,2,128,128]{3,2,1,0:T(8,128)S(1)}, f32[18,2,128,128]{3,2,1,0:T(8,128)S(1)}, u32[]{:S(2)}, u32[]{:S(2)}) collective-permute-start(f32[18,2,128,128]{3,2,1,0:T(8,128)S(1)} %get-tuple-element.8), channel_id=1, source_target_pairs={{0,1},{1,0},{2,3},{3,2},{4,5},{5,4},{6,7},{7,6},{8,9},{9,8},{10,11... | collective-permute-start | bytes 7077896 | tf_op jit(solution)/shard_map/ppermute | solution.py:201
  203.5 1.4 copy-start.5
Sparse Core Ops, SparseCore 0:
  77.9 105.7 all-gather.1

commit v2 on v1

v2 whole, which is shorter than its diff:
```python
import functools
import math

import jax
import jax.numpy as jnp
import numpy as np
from jax import lax
from jax.experimental import pallas as pl
from jax.experimental.pallas import tpu as pltpu
from jax.sharding import PartitionSpec as P

TAPS = 4
FINE = 16
COARSE = 2
NY = 4
NX = 4


def dft_rows(frames):
    groups = COARSE * FINE // 2
    w = np.zeros((2, 2, groups, frames, frames, FINE, COARSE, 2), np.float64)
    j = np.arange(FINE)
    for k in range(2):
        for g in range(groups):
            c, f = g // (FINE // 2), 2 * (g % (FINE // 2)) + k
            theta = 2.0 * math.pi * ((j * f) % FINE) / FINE
            cosine, sine = np.cos(theta) / math.sqrt(FINE), np.sin(theta) / math.sqrt(FINE)
            for m in range(frames):
                w[k, 0, g, m, m, :, c, 0] = cosine
                w[k, 0, g, m, m, :, c, 1] = sine
                w[k, 1, g, m, m, :, c, 0] = -sine
                w[k, 1, g, m, m, :, c, 1] = cosine
    return w.reshape(2, 2, groups * frames, frames * FINE * COARSE * 2).astype(np.float32)


def spectra_kernel(k_ref, own_ref, other_ref, own_lead_ref, other_lead_ref, taps_ref, w_ref, real_ref, imag_ref, pad):
    first = k_ref[0] == 0
    lead = own_lead_ref.shape[0]
    lanes = own_ref.shape[1]
    for source, mate, rows in (
        (own_lead_ref, other_lead_ref, pl.ds(0, lead)),
        (own_ref, other_ref, pl.ds(lead, own_ref.shape[0])),
    ):
        a, b = source[...], mate[...]
        pad[rows, 0:lanes] = jnp.where(first, a, b)
        pad[rows, lanes : 2 * lanes] = jnp.where(first, b, a)
    frame = taps_ref.shape[1]
    chunk = w_ref.shape[3]
    per = chunk // frame
    groups = real_ref.shape[0]
    tap_rows = [jnp.concatenate([taps_ref[p], taps_ref[p]], axis=1)[None] for p in range(TAPS)]
    for part in range(own_ref.shape[0] // chunk):
        total = None
        for p in range(TAPS):
            rows = pad[pl.ds(part * chunk + (TAPS - 1 - p) * frame, chunk), :]
            term = tap_rows[p] * rows.reshape(per, frame, 2 * lanes)
            total = term if total is None else total + term
        total = total.reshape(chunk, 2 * lanes)
        for ri, goal in enumerate((real_ref, imag_ref)):
            result = jnp.dot(
                w_ref[0, ri], total, precision=lax.Precision.HIGHEST, preferred_element_type=jnp.float32
            )
            goal[:, pl.ds(part * per, per), :] = result.reshape(groups, per, 2 * lanes)


def spectra_of(k, own, other, own_lead, other_lead, taps):
    frames = 8
    rows, lanes = own.shape
    w = jnp.asarray(dft_rows(frames))
    tap_rows = jnp.broadcast_to(jnp.repeat(taps, COARSE * 2, axis=1)[:, :, None], (TAPS, FINE * COARSE * 2, lanes))
    groups = COARSE * FINE // 2
    whole = lambda shape: pl.BlockSpec(shape, lambda i, k: (0,) * len(shape))
    goal = (groups, rows // (FINE * COARSE * 2), 2 * lanes)
    return pl.pallas_call(
        spectra_kernel,
        out_shape=(jax.ShapeDtypeStruct(goal, jnp.float32),) * 2,
        grid_spec=pltpu.PrefetchScalarGridSpec(
            num_scalar_prefetch=1,
            grid=(1,),
            in_specs=[
                whole(own.shape),
                whole(other.shape),
                whole(own_lead.shape),
                whole(other_lead.shape),
                whole(tap_rows.shape),
                pl.BlockSpec((1,) + w.shape[1:], lambda i, k: (k[0], 0, 0, 0)),
            ],
            out_specs=[whole(goal)] * 2,
            scratch_shapes=[pltpu.VMEM((rows + own_lead.shape[0], 2 * lanes), jnp.float32)],
        ),
        compiler_params=pltpu.CompilerParams(vmem_limit_bytes=32 * 2**20),
    )(k, own, other, own_lead, other_lead, tap_rows, w)


E = (
    (0, 0, 0, 0),
    (4, 4, 4, 4),
    (8, 8, 8, 8),
    (5, 5, 5, 1),
    (7, 3, 3, 3),
    (1, 1, 1, 5),
    (3, 7, 7, 7),
    (6, 6, 2, 2),
    (2, 2, 6, 6),
)


def moved(block, routes):
    pairs = []
    for columns, dy, dx in routes:
        for y in range(NY):
            for x in columns:
                for core in range(2):
                    source = ((y + dy) % NY * NX + (x + dx) % NX) * 2 + core
                    pairs.append((source, (y * NX + x) * 2 + core))
    return lax.ppermute(block, "aa", pairs)


def gather(a, x, part):
    every = (0, 1, 2, 3)
    b = moved(a, [(every, 1, 0)])
    a_right = moved(a, [((0, 1, 2), 0, 1)])
    a_left = moved(a, [((0,), 0, -1)])
    d = moved(b, [(every, 2 - 1, 0)])
    b_right = moved(b, [(every, 0, 1)])
    b_left = moved(b, [(every, 0, -1)])
    if part == 0:
        from_right = moved(b_right, [((1, 2, 3), 0, 1)])
        from_left = moved(jnp.where(x == 3, b_left, d), [(every, 0, -1)])
        from_down = moved(b_right, [((3,), 1, 0)])
        far = (
            moved(jnp.where(x == 0, from_left, from_right), [((0, 1), -1, 0)]),
            moved(from_left, [((2, 3), 0, -1)]),
        )
        five, six, seven = (a_right, from_down), (from_left, a_left), (from_right, from_left)
    else:
        from_right = moved(jnp.where(x == 0, d, b_right), [((0, 3), 0, 1)])
        from_left = moved(b_left, [((1, 2, 3), 0, -1)])
        from_down = moved(b_left, [((1, 2, 3), 1, 0)])
        leaving = jnp.where(x == 1, from_left, jnp.where(x == 2, from_down, from_right))
        far = (moved(leaving, [((0, 1), -1, 0), ((2,), 0, 1), ((3,), 0, -1)]),)
        five, six, seven = (a_right, from_right), (from_down, a_left), (from_left, from_right)
    return [(a,), (b,), (d,), (b_right,), (b_left,), five, six, seven, far]


LAST = ((), (), (), (), (), (3,), (0,), (0,), (2, 3))


def split(x):
    high = x.astype(jnp.bfloat16)
    return high, (x - high.astype(jnp.float32)).astype(jnp.bfloat16)


def left_kernel(scale, real_ref, imag_ref, out_ref):
    total, width = real_ref.shape
    real, imag = split(real_ref[...].T * scale), split(imag_ref[...].T * scale)
    for part in range(2):
        out_ref[part, 0:width, 0:total] = real[part]
        out_ref[part, 0:width, total : 2 * total] = imag[part]
        out_ref[part, width : 2 * width, 0:total] = imag[part]
        out_ref[part, width : 2 * width, total : 2 * total] = -real[part]


def left_of(real, imag):
    total, width = real.shape
    return pl.pallas_call(
        functools.partial(left_kernel, 1.0 / total),
        out_shape=jax.ShapeDtypeStruct((2, 2 * width, 2 * total), jnp.bfloat16),
        compiler_params=pltpu.CompilerParams(vmem_limit_bytes=24 * 2**20),
        cost_estimate=pl.CostEstimate(flops=2 * total * width, bytes_accessed=16 * total * width, transcendentals=0),
    )(real, imag)


def correlate_kernel(columns, counts, at_ref, left_ref, *refs):
    n = len(columns)
    rights, (own_ref, send_ref), (store,) = refs[: -3], refs[-3:-1], refs[-1:]
    total, width = rights[0].shape
    half = width // 2
    first, x = at_ref[0] == 0, at_ref[1]
    place = 0
    for p in range(n):
        for part in range(2):
            count = counts[p][part]
            value = rights[place][...]
            if count == 2:
                last = functools.reduce(jnp.logical_or, [x == c for c in columns[p]])
                value = jnp.where(last, rights[place + 1][...], value)
            place += count
            high, low = split(value)
            store[p, 0, part * total : (part + 1) * total, :] = high
            store[p, 1, part * total : (part + 1) * total, :] = low

    def one(p, carry):
        dot = functools.partial(jnp.dot, preferred_element_type=jnp.float32)
        high, low = store[p, 0], store[p, 1]
        product = dot(left_ref[0], high) + dot(left_ref[0], low) + dot(left_ref[1], high)
        for r in range(2):
            for ri in range(2):
                rows0 = product[ri * width : ri * width + half, r * half : (r + 1) * half]
                rows1 = product[ri * width + half : (ri + 1) * width, r * half : (r + 1) * half]
                own_ref[2 * p + r, ri] = jnp.where(first, rows0, rows1)
                send_ref[2 * p + r, ri] = jnp.where(first, rows1, rows0)
        return carry

    lax.fori_loop(0, n, one, 0)


def correlated(at, left, positions, columns):
    n = len(positions)
    counts = tuple(tuple(len(part) for part in position) for position in positions)
    rights = [array for position in positions for part in position for array in part]
    total, width = rights[0].shape
    tiles = jax.ShapeDtypeStruct((2 * n, 2, width // 2, width // 2), jnp.float32)
    vmem = pl.BlockSpec(memory_space=pltpu.VMEM)
    return pl.pallas_call(
        functools.partial(correlate_kernel, columns, counts),
        out_shape=(tiles, tiles),
        in_specs=[pl.BlockSpec(memory_space=pltpu.SMEM)] + [vmem] * (1 + len(rights)),
        out_specs=[vmem] * 2,
        scratch_shapes=[pltpu.VMEM((n, 2, 2 * total, width), jnp.bfloat16)],
        compiler_params=pltpu.CompilerParams(vmem_limit_bytes=40 * 2**20),
        cost_estimate=pl.CostEstimate(
            flops=n * 24 * total * width * width, bytes_accessed=n * 12 * total * width, transcendentals=0
        ),
    )(at, left, *rights)


def place_kernel(sizes, at_ref, e_ref, slot_ref, *refs):
    n = len(sizes)
    owns, gots, out_ref, sems = refs[:n], refs[n : 2 * n], refs[2 * n], refs[2 * n + 1]
    k = at_ref[0]
    copies = []
    position = 0
    for own, got, size in zip(owns, gots, sizes, strict=True):
        for p in range(size):
            for r in range(2):
                distance = 2 * e_ref[position] + r - k
                unless = 1 if position == 0 and r == 0 else 0 if position == 2 and r == 1 else None
                slot = slot_ref[jnp.clip(distance, 0, slot_ref.shape[0] - 1)]
                index = 2 * (2 * position + r)
                copies.append((
                    unless,
                    pltpu.make_async_copy(own.at[2 * p + r], out_ref.at[slot, k], sems.at[index]),
                    pltpu.make_async_copy(got.at[2 * p + r], out_ref.at[slot, 1 - k], sems.at[index + 1]),
                ))
            position += 1

    def each(act):
        for unless, *pair in copies:
            if unless is None:
                for copy in pair:
                    act(copy)
            else:

                @pl.when(k != unless)
                def _(pair=pair):
                    for copy in pair:
                        act(copy)

    each(lambda copy: copy.start())
    each(lambda copy: copy.wait())


def placed(at, e, slot, owns, gots):
    half = owns[0].shape[-1]
    sizes = tuple(own.shape[0] // 2 for own in owns)
    smem, vmem = pl.BlockSpec(memory_space=pltpu.SMEM), pl.BlockSpec(memory_space=pltpu.VMEM)
    return pl.pallas_call(
        functools.partial(place_kernel, sizes),
        out_shape=jax.ShapeDtypeStruct((slot.shape[0], 2, 2, half, half), jnp.float32),
        in_specs=[smem] * 3 + [vmem] * (2 * len(owns)),
        out_specs=pl.BlockSpec(memory_space=pl.ANY),
        scratch_shapes=[pltpu.SemaphoreType.DMA((4 * sum(sizes),))],
        compiler_params=pltpu.CompilerParams(vmem_limit_bytes=24 * 2**20),
    )(at, e, slot, *owns, *gots)


GROUPS = ((0, 1), (2, 3, 4), (5, 6, 7), (8,))


def local(voltages, taps, tile_map):
    n_ta, n_aa = lax.axis_size("ta"), lax.axis_size("aa")
    me = lax.axis_index("aa").astype(jnp.int32)
    x = lax.rem(me // 2, NX)
    at = jnp.stack([lax.rem(me, 2), x])
    samples, coarse, parts, lanes = voltages.shape
    own = voltages.reshape(samples * coarse * parts, lanes)
    lead = own[own.shape[0] - (TAPS - 1) * FINE * coarse * parts :]
    mate = [(i, i ^ 1) for i in range(n_aa)]
    later = [(t * n_aa + i, (t + 1) * n_aa + i) for t in range(n_ta - 1) for i in range(n_aa)]
    own_lead = lax.ppermute(lead, ("ta", "aa"), later)
    other_lead = lax.ppermute(lead, ("ta", "aa"), [(s, d ^ 1) for s, d in later])
    other = lax.ppermute(own, "aa", mate)
    spectra = spectra_of(at, own, other, own_lead, other_lead, taps)
    blocks = [
        lax.all_to_all(part, "ta", split_axis=0, concat_axis=0, tiled=True).reshape(-1, 2 * lanes) for part in spectra
    ]
    left = left_of(*blocks)
    taken = [gather(block, x, part) for part, block in enumerate(blocks)]
    owns, gots = [], []
    for group in GROUPS:
        mine, leaving = correlated(
            at, left, [tuple(part[p] for part in taken) for p in group], tuple(LAST[p] for p in group)
        )
        owns.append(mine)
        gots.append(lax.ppermute(leaving, "aa", mate))
    slots = jnp.arange(tile_map.shape[1], dtype=jnp.int32)
    slot = jnp.sum(jnp.where(tile_map[0][None, :] == slots[:, None], slots[None, :], 0), axis=1)
    e = jnp.asarray(np.array(E, np.int32).T)[x]
    return placed(at, e, slot, owns, gots)


def solution(mesh):
    in_specs = (P("ta", None, None, "aa"), P(), P("aa", None))
    out_specs = P("aa", "ta", None, None, None)
    return jax.shard_map(local, mesh=mesh, in_specs=in_specs, out_specs=out_specs, check_vma=False)
```

time: 349 us -> 201 us (0.58)
  the two profiles are of different devices: /device:TPU:1 before, /device:TPU:39 now
where the time goes in v2:
time: 201 us; the launch traced here: 200 us
  starting transfers between devices  98.9 us (49%)
  blocking collectives  36.4 us (18%)
  waiting for transfers between devices  32.6 us (16%)
  Pallas kernels  22.2 us (11%)
  local copies, waits for them, and re-layouts  8.27 us (4%)
    ppermute x21, starting transfers between devices, moved(): return lax.ppermute(block, 'aa', pairs)  59.4 us
    all_to_all x1, blocking collectives, local(): lax.all_to_all(part, 'ta', split_axis=0, concat_axis=0, tiled=True)  36.4 us
    ppermute x4, starting transfers between devices, local(): gots.append(lax.ppermute(leaving, 'aa', mate))  21.4 us
    all_to_all x1, waiting for transfers between devices, local(): lax.all_to_all(part, 'ta', split_axis=0, concat_axis=0, tiled=True)  16.8 us
    pallas_call x4, Pallas kernels, correlated(): pl.pallas_call(functools.partial(correlate_kernel, columns, counts), out_...  14.9 us
    ppermute x21, waiting for transfers between devices, moved(): return lax.ppermute(block, 'aa', pairs)  13.4 us
    all_to_all x1, starting transfers between devices, local(): lax.all_to_all(part, 'ta', split_axis=0, concat_axis=0, tiled=True)  8.31 us
    unnamed x26, local copies, waits for them, and re-layouts  5.74 us
  transfers between devices with their start and end apart: 29, of which 7 were waited for; matrix products, arithmetic and copies ran while one was open for 2% of the time, Pallas kernels for 8%

profile of v2, /device:TPU:39, one launch (start us, length us, event | category | flops | bytes accessed | tf_op | source)
XLA Modules:
  0.0 200.0 jit_solution(9270585475268741596)
XLA Ops:
  0.0 2.6 %collective-permute-start = (f32[1536,128]{1,0:T(8,128)}, f32[1536,128]{1,0:T(8,128)S(1)}, u32[]{:S(2)}, u32[]{:S(2)}) collective-permute-start(f32[1536,128]{1,0:T(8,128)} %bitcast.19), channel_id=1, source_target_pairs={{0,1},{1,0},{2,3},{3,2},{4,5},{5,4},{6,7},{7,6},{8,9},{9,8},{10,11... | collective-permute-start | bytes 2359304 | tf_op jit(solution)/shard_map/ppermute | solution.py:293
  2.6 0.9 slice.6
  3.5 3.5 %collective-permute-start.1 = (f32[192,128]{1,0:T(8,128)S(1)}, f32[192,128]{1,0:T(8,128)S(1)}, u32[]{:S(2)}, u32[]{:S(2)}) collective-permute-start(f32[192,128]{1,0:T(8,128)S(1)} %bitcast.21), channel_id=1, source_target_pairs={{0,32},{1,33},{2,34},{3,35},{4,36},{5,37},{6,38},{7,39},{8,40},{9,... | collective-permute-start | bytes 294920 | tf_op jit(solution)/shard_map/ppermute | solution.py:291
  7.0 3.7 %collective-permute-start.2 = (f32[192,128]{1,0:T(8,128)S(1)}, f32[192,128]{1,0:T(8,128)S(1)}, u32[]{:S(2)}, u32[]{:S(2)}) collective-permute-start(f32[192,128]{1,0:T(8,128)S(1)} %bitcast.22), channel_id=1, source_target_pairs={{0,33},{1,32},{2,35},{3,34},{4,37},{5,36},{6,39},{7,38},{8,41},{9,... | collective-permute-start | bytes 294920 | tf_op jit(solution)/shard_map/ppermute | solution.py:292
  10.8 0.8 broadcast_in_dim.26
  11.5 0.1 broadcast_in_dim.27
  11.6 0.1 pad_add_fusion.k_ref.at_ref
  11.7 1.9 collective-permute-done.2.other_lead_ref
  13.6 0.1 broadcast_in_dim.28.taps_ref
  13.7 0.0 copy-start
  13.7 1.2 copy-done
  15.0 1.1 copy-done.1
  16.1 3.4 %shard_map.55 = (f32[16,24,256]{2,1,0:T(8,128)S(1)}, f32[16,24,256]{2,1,0:T(8,128)}) custom-call(s32[2]{0:T(128)S(1)} %pad_add_fusion.k_ref.at_ref, f32[1536,128]{1,0:T(8,128)S(1)} %bitcast.20, f32[1536,128]{1,0:T(8,128)S(1)} %collective-permute-done.other_ref, f32[192,128]{1,0:T(8,128)S(1)} %collective-permute-done.1.own_lead_ref, ...), custom_call_target="tpu_custom_call" | custom-call | tf_op jit(solution)/shard_map/pallas_call | solution.py:74
  19.5 36.4 %all_to_all.10 = f32[16,24,256]{2,1,0:T(8,128)S(1)} all-to-all(f32[16,24,256]{2,1,0:T(8,128)S(1)} %get-tuple-element.15), channel_id=1, replica_groups=mesh['ta'=16,'aa'=32] {'ta'}, dimensions={0} | all-to-all | bytes 786432 | tf_op jit(solution)/shard_map/all_to_all | solution.py:296
  55.9 8.3 %all-to-all-start.1 = ((f32[16,24,256]{2,1,0:T(8,128)}), f32[16,24,256]{2,1,0:T(8,128)S(1)}, u32[]{:S(2)}, u32[]{:S(2)}) async-start(f32[16,24,256]{2,1,0:T(8,128)} %get-tuple-element.16), calls=%async_computation.1 | async-start | bytes 786432 | tf_op jit(solution)/shard_map/all_to_all | solution.py:296
  64.2 4.6 %collective-permute-start.3 = (f32[384,256]{1,0:T(8,128)S(1)}, f32[384,256]{1,0:T(8,128)S(1)}, u32[]{:S(2)}, u32[]{:S(2)}) collective-permute-start(f32[384,256]{1,0:T(8,128)S(1)} %bitcast.9), channel_id=1, source_target_pairs={{8,0},{9,1},{10,2},{11,3},{12,4},{13,5},{14,6},{15,7},{16,8},{17,9... | collective-permute-start | bytes 1179656 | tf_op jit(solution)/shard_map/ppermute | solution.py:116
  68.8 16.8 %all-to-all-done.1 = f32[16,24,256]{2,1,0:T(8,128)S(1)} async-done(((f32[16,24,256]{2,1,0:T(8,128)}), f32[16,24,256]{2,1,0:T(8,128)S(1)}, u32[]{:S(2)}, u32[]{:S(2)}) %all-to-all-start.1) | async-done | bytes 393248 | tf_op jit(solution)/shard_map/all_to_all | solution.py:296
  85.6 4.6 %collective-permute-start.4 = (f32[384,256]{1,0:T(8,128)S(1)}, f32[384,256]{1,0:T(8,128)S(1)}, u32[]{:S(2)}, u32[]{:S(2)}) collective-permute-start(f32[384,256]{1,0:T(8,128)S(1)} %bitcast.14), channel_id=1, source_target_pairs={{8,0},{9,1},{10,2},{11,3},{12,4},{13,5},{14,6},{15,7},{16,8},{17,9... | collective-permute-start | bytes 1179656 | tf_op jit(solution)/shard_map/ppermute | solution.py:116
  90.3 0.0 collective-permute-done.3.refs_2_
  90.3 2.4 %collective-permute-start.5 = (f32[384,256]{1,0:T(8,128)S(1)}, f32[384,256]{1,0:T(8,128)S(1)}, u32[]{:S(2)}, u32[]{:S(2)}) collective-permute-start(f32[384,256]{1,0:T(8,128)S(1)} %collective-permute-done.3.refs_2_), channel_id=1, source_target_pairs={{8,0},{9,1},{10,2},{11,3},{12,4},{13,5},{14,6},{15,7},{16,8},{17,9... | collective-permute-start | bytes 1179656 | tf_op jit(solution)/shard_map/ppermute | solution.py:116
  92.7 2.1 %collective-permute-start.9 = (f32[384,256]{1,0:T(8,128)S(1)}, f32[384,256]{1,0:T(8,128)S(1)}, u32[]{:S(2)}, u32[]{:S(2)}) collective-permute-start(f32[384,256]{1,0:T(8,128)S(1)} %collective-permute-done.3.refs_2_), channel_id=1, source_target_pairs={{6,0},{7,1},{0,2},{1,3},{2,4},{3,5},{4,6},{5,7},{14,8},{15,9},{8,1... | collective-permute-start | bytes 1179656 | tf_op jit(solution)/shard_map/ppermute | solution.py:116
  94.8 3.2 %collective-permute-start.11 = (f32[384,256]{1,0:T(8,128)S(1)}, f32[384,256]{1,0:T(8,128)S(1)}, u32[]{:S(2)}, u32[]{:S(2)}) collective-permute-start(f32[384,256]{1,0:T(8,128)S(1)} %bitcast.10), channel_id=1, source_target_pairs={{2,0},{3,1},{4,2},{5,3},{6,4},{7,5},{10,8},{11,9},{12,10},{13,11},... | collective-permute-start | bytes 1179656 | tf_op jit(solution)/shard_map/ppermute | solution.py:116
  98.0 0.0 collective-permute-done.4.refs_3_
  98.0 4.1 %collective-permute-start.6 = (f32[384,256]{1,0:T(8,128)S(1)}, f32[384,256]{1,0:T(8,128)S(1)}, u32[]{:S(2)}, u32[]{:S(2)}) collective-permute-start(f32[384,256]{1,0:T(8,128)S(1)} %collective-permute-done.4.refs_3_), channel_id=1, source_target_pairs={{8,0},{9,1},{10,2},{11,3},{12,4},{13,5},{14,6},{15,7},{16,8},{17,9... | collective-permute-start | bytes 1179656 | tf_op jit(solution)/shard_map/ppermute | solution.py:116
  102.1 2.5 %collective-permute-start.7 = (f32[384,256]{1,0:T(8,128)S(1)}, f32[384,256]{1,0:T(8,128)}, u32[]{:S(2)}, u32[]{:S(2)}) collective-permute-start(f32[384,256]{1,0:T(8,128)S(1)} %collective-permute-done.3.refs_2_), channel_id=1, source_target_pairs={{2,0},{3,1},{4,2},{5,3},{6,4},{7,5},{0,6},{1,7},{10,8},{11,9},{12,... | collective-permute-start | bytes 1179656 | tf_op jit(solution)/shard_map/ppermute | solution.py:116
  104.6 0.6 collective-permute-done.5.refs_0_
  105.2 2.4 %collective-permute-start.8 = (f32[384,256]{1,0:T(8,128)S(1)}, f32[384,256]{1,0:T(8,128)S(1)}, u32[]{:S(2)}, u32[]{:S(2)}) collective-permute-start(f32[384,256]{1,0:T(8,128)S(1)} %collective-permute-done.4.refs_3_), channel_id=1, source_target_pairs={{2,0},{3,1},{4,2},{5,3},{6,4},{7,5},{0,6},{1,7},{10,8},{11,9},{12,... | collective-permute-start | bytes 1179656 | tf_op jit(solution)/shard_map/ppermute | solution.py:116
  107.7 2.9 %collective-permute-start.13 = (f32[384,256]{1,0:T(8,128)S(1)}, f32[384,256]{1,0:T(8,128)}, u32[]{:S(2)}, u32[]{:S(2)}) collective-permute-start(f32[384,256]{1,0:T(8,128)S(1)} %bitcast.15), channel_id=1, source_target_pairs={{2,0},{3,1},{4,2},{5,3},{6,4},{7,5},{10,8},{11,9},{12,10},{13,11},... | collective-permute-start | bytes 1179656 | tf_op jit(solution)/shard_map/ppermute | solution.py:116
  110.6 0.8 broadcast_select_fusion
  111.4 0.8 copy-done.10
  112.2 3.2 %collective-permute-start.16 = (f32[384,256]{1,0:T(8,128)S(1)}, f32[384,256]{1,0:T(8,128)}, u32[]{:S(2)}, u32[]{:S(2)}) collective-permute-start(f32[384,256]{1,0:T(8,128)S(1)} %bitcast.11), channel_id=1, source_target_pairs={{6,0},{7,1},{14,8},{15,9},{22,16},{23,17},{30,24},{31,25},{38,32},... | collective-permute-start | bytes 1179656 | tf_op jit(solution)/shard_map/ppermute | solution.py:116
  115.3 1.9 collective-permute-start.10
  117.3 2.7 %collective-permute-start.15 = (f32[384,256]{1,0:T(8,128)}, f32[384,256]{1,0:T(8,128)S(1)}, u32[]{:S(2)}, u32[]{:S(2)}) collective-permute-start(f32[384,256]{1,0:T(8,128)} %broadcast_select_fusion), channel_id=1, source_target_pairs={{6,0},{7,1},{0,2},{1,3},{2,4},{3,5},{4,6},{5,7},{14,8},{15,9},{8,1... | collective-permute-start | bytes 1179656 | tf_op jit(solution)/shard_map/ppermute | solution.py:116
  120.0 3.6 %collective-permute-start.19 = (f32[384,256]{1,0:T(8,128)}, f32[384,256]{1,0:T(8,128)S(1)}, u32[]{:S(2)}, u32[]{:S(2)}) collective-permute-start(f32[384,256]{1,0:T(8,128)} %collective-permute-done.7.refs_2_), channel_id=1, source_target_pairs={{4,2},{5,3},{6,4},{7,5},{0,6},{1,7},{12,10},{13,11},{14,12},{15,13... | collective-permute-start | bytes 1179656 | tf_op jit(solution)/shard_map/ppermute | solution.py:116
  123.7 0.3 shard_map.56.left_ref
  124.0 0.1 broadcast_select_fusion.2
  124.0 3.9 %collective-permute-done.13.refs_2_ = f32[384,256]{1,0:T(8,128)} collective-permute-done((f32[384,256]{1,0:T(8,128)S(1)}, f32[384,256]{1,0:T(8,128)}, u32[]{:S(2)}, u32[]{:S(2)}) %collective-permute-start.13) | collective-permute-done | bytes 393248 | tf_op jit(solution)/shard_map/ppermute | solution.py:116
  128.0 4.5 %collective-permute-start.18 = (f32[384,256]{1,0:T(8,128)S(1)}, f32[384,256]{1,0:T(8,128)S(1)}, u32[]{:S(2)}, u32[]{:S(2)}) collective-permute-start(f32[384,256]{1,0:T(8,128)S(1)} %bitcast.17), channel_id=1, source_target_pairs={{6,0},{7,1},{14,8},{15,9},{22,16},{23,17},{30,24},{31,25},{38,32},... | collective-permute-start | bytes 1179656 | tf_op jit(solution)/shard_map/ppermute | solution.py:116
  132.5 1.3 collective-permute-start.14
  133.8 2.5 %collective-permute-start.12 = (f32[384,256]{1,0:T(8,128)}, f32[384,256]{1,0:T(8,128)S(1)}, u32[]{:S(2)}, u32[]{:S(2)}) collective-permute-start(f32[384,256]{1,0:T(8,128)} %collective-permute-done.7.refs_2_), channel_id=1, source_target_pairs={{14,6},{15,7},{22,14},{23,15},{30,22},{31,23},{6,30},{7,31},{46,38... | collective-permute-start | bytes 1179656 | tf_op jit(solution)/shard_map/ppermute | solution.py:116
  136.3 3.5 %collective-permute-start.17 = (f32[384,256]{1,0:T(8,128)}, f32[384,256]{1,0:T(8,128)S(1)}, u32[]{:S(2)}, u32[]{:S(2)}) collective-permute-start(f32[384,256]{1,0:T(8,128)} %collective-permute-done.10.refs_5_), channel_id=1, source_target_pairs={{10,2},{11,3},{12,4},{13,5},{14,6},{15,7},{18,10},{19,11},{20,12},... | collective-permute-start | bytes 1179656 | tf_op jit(solution)/shard_map/ppermute | solution.py:116
  139.8 0.7 copy-done.4
  140.6 1.3 collective-permute-start.20
  141.9 4.8 %shard_map.58 = (f32[6,2,128,128]{3,2,1,0:T(8,128)S(1)}, f32[6,2,128,128]{3,2,1,0:T(8,128)}) custom-call(s32[2]{0:T(128)S(1)} %pad_add_fusion.k_ref.at_ref, bf16[2,512,768]{2,1,0:T(8,128)(2,1)S(1)} %shard_map.56.left_ref, f32[384,256]{1,0:T(8,128)S(1)} %collective-permute-done.5.refs_0_, f32[384,256]{1,0:T(8,128)S(1)} %collective-permute-done.6.refs_1_, ...), custom_call_target="tpu_custom_call" | custom-call | flops 1811939328 | bytes 3538944 | tf_op jit(solution)/shard_map/pallas_call | solution.py:215
  146.7 0.1 broadcast_select_fusion.1
  146.8 12.9 %collective-permute-start.25 = (f32[6,2,128,128]{3,2,1,0:T(8,128)}, f32[6,2,128,128]{3,2,1,0:T(8,128)S(1)}, u32[]{:S(2)}, u32[]{:S(2)}) collective-permute-start(f32[6,2,128,128]{3,2,1,0:T(8,128)} %get-tuple-element.22), channel_id=1, source_target_pairs={{0,1},{1,0},{2,3},{3,2},{4,5},{5,4},{6,7},{7,6},{8,9},{9,8},{10,11... | collective-permute-start | bytes 2359304 | tf_op jit(solution)/shard_map/ppermute | solution.py:306
  159.7 0.7 collective-permute-start.21
  160.4 4.9 %shard_map.59 = (f32[6,2,128,128]{3,2,1,0:T(8,128)S(1)}, f32[6,2,128,128]{3,2,1,0:T(8,128)}) custom-call(s32[2]{0:T(128)S(1)} %pad_add_fusion.k_ref.at_ref, bf16[2,512,768]{2,1,0:T(8,128)(2,1)S(1)} %shard_map.56.left_ref, f32[384,256]{1,0:T(8,128)S(1)} %copy-done.11, f32[384,256]{1,0:T(8,128)S(1)} %collective-permute-done.12.refs_1_, ...), custom_call_target="tpu_custom_call" | custom-call | flops 1811939328 | bytes 3538944 | tf_op jit(solution)/shard_map/pallas_call | solution.py:215
  165.3 2.9 %collective-permute-start.26 = (f32[6,2,128,128]{3,2,1,0:T(8,128)}, f32[6,2,128,128]{3,2,1,0:T(8,128)}, u32[]{:S(2)}, u32[]{:S(2)}) collective-permute-start(f32[6,2,128,128]{3,2,1,0:T(8,128)} %get-tuple-element.23), channel_id=1, source_target_pairs={{0,1},{1,0},{2,3},{3,2},{4,5},{5,4},{6,7},{7,6},{8,9},{9,8},{10,11... | collective-permute-start | bytes 2359304 | tf_op jit(solution)/shard_map/ppermute | solution.py:306
  168.2 1.3 collective-permute-start.22
  169.5 0.1 select_select_fusion
  169.6 4.0 %collective-permute-start.23 = (f32[384,256]{1,0:T(8,128)S(1)}, f32[384,256]{1,0:T(8,128)S(1)}, u32[]{:S(2)}, u32[]{:S(2)}) collective-permute-start(f32[384,256]{1,0:T(8,128)S(1)} %select_select_fusion), channel_id=1, source_target_pairs={{24,0},{25,1},{26,2},{27,3},{0,8},{1,9},{2,10},{3,11},{8,16},{9,17... | collective-permute-start | bytes 1179656 | tf_op jit(solution)/shard_map/ppermute | solution.py:116
  173.7 3.2 %shard_map.57 = (f32[4,2,128,128]{3,2,1,0:T(8,128)S(1)}, f32[4,2,128,128]{3,2,1,0:T(8,128)}) custom-call(s32[2]{0:T(128)S(1)} %pad_add_fusion.k_ref.at_ref, bf16[2,512,768]{2,1,0:T(8,128)(2,1)S(1)} %shard_map.56.left_ref, f32[384,256]{1,0:T(8,128)S(1)} %bitcast.13, f32[384,256]{1,0:T(8,128)S(1)} %bitcast.18, f32[384,256]{1,0:T(8,128)S(1)} %copy-done.7, ...), custom_call_target="tpu_custom_call" | custom-call | flops 1207959552 | bytes 2359296 | tf_op jit(solution)/shard_map/pallas_call | solution.py:215
  176.8 0.8 copy-done.2
  177.6 2.7 %collective-permute-start.24 = (f32[4,2,128,128]{3,2,1,0:T(8,128)}, f32[4,2,128,128]{3,2,1,0:T(8,128)S(1)}, u32[]{:S(2)}, u32[]{:S(2)}) collective-permute-start(f32[4,2,128,128]{3,2,1,0:T(8,128)} %get-tuple-element.21), channel_id=1, source_target_pairs={{0,1},{1,0},{2,3},{3,2},{4,5},{5,4},{6,7},{7,6},{8,9},{9,8},{10,11... | collective-permute-start | bytes 1572872 | tf_op jit(solution)/shard_map/ppermute | solution.py:306
  180.3 0.3 collective-permute-done.22.refs_1_
  180.7 8.4 %collective-permute-done.23.refs_2_ = f32[384,256]{1,0:T(8,128)S(1)} collective-permute-done((f32[384,256]{1,0:T(8,128)S(1)}, f32[384,256]{1,0:T(8,128)S(1)}, u32[]{:S(2)}, u32[]{:S(2)}) %collective-permute-start.23) | collective-permute-done | bytes 393248 | tf_op jit(solution)/shard_map/ppermute | solution.py:116
  189.1 2.1 %shard_map.60 = (f32[2,2,128,128]{3,2,1,0:T(8,128)S(1)}, f32[2,2,128,128]{3,2,1,0:T(8,128)}) custom-call(s32[2]{0:T(128)S(1)} %pad_add_fusion.k_ref.at_ref, bf16[2,512,768]{2,1,0:T(8,128)(2,1)S(1)} %shard_map.56.left_ref, f32[384,256]{1,0:T(8,128)S(1)} %collective-permute-done.21.refs_0_, f32[384,256]{1,0:T(8,128)S(1)} %collective-permute-done.22.refs_1_, ...), custom_call_target="tpu_custom_call" | custom-call | flops 603979776 | bytes 1179648 | tf_op jit(solution)/shard_map/pallas_call | solution.py:215
  191.1 2.9 %collective-permute-start.27 = (f32[2,2,128,128]{3,2,1,0:T(8,128)}, f32[2,2,128,128]{3,2,1,0:T(8,128)S(1)}, u32[]{:S(2)}, u32[]{:S(2)}) collective-permute-start(f32[2,2,128,128]{3,2,1,0:T(8,128)} %get-tuple-element.24), channel_id=1, source_target_pairs={{0,1},{1,0},{2,3},{3,2},{4,5},{5,4},{6,7},{7,6},{8,9},{9,8},{10,11... | collective-permute-start | bytes 786440 | tf_op jit(solution)/shard_map/ppermute | solution.py:306
  194.1 0.7 dynamic-slice_bitcast_fusion.e_ref
  194.8 0.1 select_reduce_fusion.slot_ref
  194.9 0.5 collective-permute-done.27.refs_7_
  195.4 1.0 copy-done.3
  196.5 3.5 %shard_map.61 = f32[17,2,2,128,128]{4,3,2,1,0:T(8,128)} custom-call(s32[2]{0:T(128)S(1)} %pad_add_fusion.k_ref.at_ref, s32[9]{0:T(128)S(1)} %dynamic-slice_bitcast_fusion.e_ref, s32[17]{0:T(128)S(1)} %select_reduce_fusion.slot_ref, f32[4,2,128,128]{3,2,1,0:T(8,128)S(1)} %copy-done.3, f32[6,2,128,128]{3,2,1,0:T(8,128)S(1)} %get-tuple-element.18.refs_1_, ...), custom_call_target="tpu_custom_call" | custom-call | tf_op jit(solution)/shard_map/pallas_call | solution.py:268
  (39 shorter events, 0.1 us)
Async XLA Ops:
  0.0 13.6 %collective-permute-start = (f32[1536,128]{1,0:T(8,128)}, f32[1536,128]{1,0:T(8,128)S(1)}, u32[]{:S(2)}, u32[]{:S(2)}) collective-permute-start(f32[1536,128]{1,0:T(8,128)} %bitcast.19), channel_id=1, source_target_pairs={{0,1},{1,0},{2,3},{3,2},{4,5},{5,4},{6,7},{7,6},{8,9},{9,8},{10,11... | collective-permute-start | bytes 2359304 | tf_op jit(solution)/shard_map/ppermute | solution.py:293
  3.5 8.2 %collective-permute-start.1 = (f32[192,128]{1,0:T(8,128)S(1)}, f32[192,128]{1,0:T(8,128)S(1)}, u32[]{:S(2)}, u32[]{:S(2)}) collective-permute-start(f32[192,128]{1,0:T(8,128)S(1)} %bitcast.21), channel_id=1, source_target_pairs={{0,32},{1,33},{2,34},{3,35},{4,36},{5,37},{6,38},{7,39},{8,40},{9,... | collective-permute-start | bytes 294920 | tf_op jit(solution)/shard_map/ppermute | solution.py:291
  7.0 6.6 %collective-permute-start.2 = (f32[192,128]{1,0:T(8,128)S(1)}, f32[192,128]{1,0:T(8,128)S(1)}, u32[]{:S(2)}, u32[]{:S(2)}) collective-permute-start(f32[192,128]{1,0:T(8,128)S(1)} %bitcast.22), channel_id=1, source_target_pairs={{0,33},{1,32},{2,35},{3,34},{4,37},{5,36},{6,39},{7,38},{8,41},{9,... | collective-permute-start | bytes 294920 | tf_op jit(solution)/shard_map/ppermute | solution.py:292
  13.7 1.2 copy-start
  15.0 1.1 copy-start.1
  55.9 29.7 %all-to-all-start.1 = ((f32[16,24,256]{2,1,0:T(8,128)}), f32[16,24,256]{2,1,0:T(8,128)S(1)}, u32[]{:S(2)}, u32[]{:S(2)}) async-start(f32[16,24,256]{2,1,0:T(8,128)} %get-tuple-element.16), calls=%async_computation.1 | async-start | bytes 786432 | tf_op jit(solution)/shard_map/all_to_all | solution.py:296
  64.2 26.0 %collective-permute-start.3 = (f32[384,256]{1,0:T(8,128)S(1)}, f32[384,256]{1,0:T(8,128)S(1)}, u32[]{:S(2)}, u32[]{:S(2)}) collective-permute-start(f32[384,256]{1,0:T(8,128)S(1)} %bitcast.9), channel_id=1, source_target_pairs={{8,0},{9,1},{10,2},{11,3},{12,4},{13,5},{14,6},{15,7},{16,8},{17,9... | collective-permute-start | bytes 1179656 | tf_op jit(solution)/shard_map/ppermute | solution.py:116
  85.6 12.4 %collective-permute-start.4 = (f32[384,256]{1,0:T(8,128)S(1)}, f32[384,256]{1,0:T(8,128)S(1)}, u32[]{:S(2)}, u32[]{:S(2)}) collective-permute-start(f32[384,256]{1,0:T(8,128)S(1)} %bitcast.14), channel_id=1, source_target_pairs={{8,0},{9,1},{10,2},{11,3},{12,4},{13,5},{14,6},{15,7},{16,8},{17,9... | collective-permute-start | bytes 1179656 | tf_op jit(solution)/shard_map/ppermute | solution.py:116
  90.3 27.0 %copy-start.6 = (f32[384,256]{1,0:T(8,128)}, f32[384,256]{1,0:T(8,128)S(1)}, u32[]{:S(2)}) copy-start(f32[384,256]{1,0:T(8,128)S(1)} %collective-permute-done.3.refs_2_) | copy-start | bytes 1179652
  90.3 14.9 %collective-permute-start.5 = (f32[384,256]{1,0:T(8,128)S(1)}, f32[384,256]{1,0:T(8,128)S(1)}, u32[]{:S(2)}, u32[]{:S(2)}) collective-permute-start(f32[384,256]{1,0:T(8,128)S(1)} %collective-permute-done.3.refs_2_), channel_id=1, source_target_pairs={{8,0},{9,1},{10,2},{11,3},{12,4},{13,5},{14,6},{15,7},{16,8},{17,9... | collective-permute-start | bytes 1179656 | tf_op jit(solution)/shard_map/ppermute | solution.py:116
  92.7 15.0 %collective-permute-start.9 = (f32[384,256]{1,0:T(8,128)S(1)}, f32[384,256]{1,0:T(8,128)S(1)}, u32[]{:S(2)}, u32[]{:S(2)}) collective-permute-start(f32[384,256]{1,0:T(8,128)S(1)} %collective-permute-done.3.refs_2_), channel_id=1, source_target_pairs={{6,0},{7,1},{0,2},{1,3},{2,4},{3,5},{4,6},{5,7},{14,8},{15,9},{8,1... | collective-permute-start | bytes 1179656 | tf_op jit(solution)/shard_map/ppermute | solution.py:116
  94.8 16.6 %collective-permute-start.11 = (f32[384,256]{1,0:T(8,128)S(1)}, f32[384,256]{1,0:T(8,128)S(1)}, u32[]{:S(2)}, u32[]{:S(2)}) collective-permute-start(f32[384,256]{1,0:T(8,128)S(1)} %bitcast.10), channel_id=1, source_target_pairs={{2,0},{3,1},{4,2},{5,3},{6,4},{7,5},{10,8},{11,9},{12,10},{13,11},... | collective-permute-start | bytes 1179656 | tf_op jit(solution)/shard_map/ppermute | solution.py:116
  98.0 41.8 %copy-start.8 = (f32[384,256]{1,0:T(8,128)}, f32[384,256]{1,0:T(8,128)S(1)}, u32[]{:S(2)}) copy-start(f32[384,256]{1,0:T(8,128)S(1)} %collective-permute-done.4.refs_3_) | copy-start | bytes 1179652
  98.0 17.4 %collective-permute-start.6 = (f32[384,256]{1,0:T(8,128)S(1)}, f32[384,256]{1,0:T(8,128)S(1)}, u32[]{:S(2)}, u32[]{:S(2)}) collective-permute-start(f32[384,256]{1,0:T(8,128)S(1)} %collective-permute-done.4.refs_3_), channel_id=1, source_target_pairs={{8,0},{9,1},{10,2},{11,3},{12,4},{13,5},{14,6},{15,7},{16,8},{17,9... | collective-permute-start | bytes 1179656 | tf_op jit(solution)/shard_map/ppermute | solution.py:116
  102.1 15.2 %collective-permute-start.7 = (f32[384,256]{1,0:T(8,128)S(1)}, f32[384,256]{1,0:T(8,128)}, u32[]{:S(2)}, u32[]{:S(2)}) collective-permute-start(f32[384,256]{1,0:T(8,128)S(1)} %collective-permute-done.3.refs_2_), channel_id=1, source_target_pairs={{2,0},{3,1},{4,2},{5,3},{6,4},{7,5},{0,6},{1,7},{10,8},{11,9},{12,... | collective-permute-start | bytes 1179656 | tf_op jit(solution)/shard_map/ppermute | solution.py:116
  105.2 14.8 %collective-permute-start.8 = (f32[384,256]{1,0:T(8,128)S(1)}, f32[384,256]{1,0:T(8,128)S(1)}, u32[]{:S(2)}, u32[]{:S(2)}) collective-permute-start(f32[384,256]{1,0:T(8,128)S(1)} %collective-permute-done.4.refs_3_), channel_id=1, source_target_pairs={{2,0},{3,1},{4,2},{5,3},{6,4},{7,5},{0,6},{1,7},{10,8},{11,9},{12,... | collective-permute-start | bytes 1179656 | tf_op jit(solution)/shard_map/ppermute | solution.py:116
  107.7 20.3 %collective-permute-start.13 = (f32[384,256]{1,0:T(8,128)S(1)}, f32[384,256]{1,0:T(8,128)}, u32[]{:S(2)}, u32[]{:S(2)}) collective-permute-start(f32[384,256]{1,0:T(8,128)S(1)} %bitcast.15), channel_id=1, source_target_pairs={{2,0},{3,1},{4,2},{5,3},{6,4},{7,5},{10,8},{11,9},{12,10},{13,11},... | collective-permute-start | bytes 1179656 | tf_op jit(solution)/shard_map/ppermute | solution.py:116
  111.4 0.8 copy-start.10
  112.2 20.3 %collective-permute-start.16 = (f32[384,256]{1,0:T(8,128)S(1)}, f32[384,256]{1,0:T(8,128)}, u32[]{:S(2)}, u32[]{:S(2)}) collective-permute-start(f32[384,256]{1,0:T(8,128)S(1)} %bitcast.11), channel_id=1, source_target_pairs={{6,0},{7,1},{14,8},{15,9},{22,16},{23,17},{30,24},{31,25},{38,32},... | collective-permute-start | bytes 1179656 | tf_op jit(solution)/shard_map/ppermute | solution.py:116
  115.3 18.4 %collective-permute-start.10 = (f32[384,256]{1,0:T(8,128)S(1)}, f32[384,256]{1,0:T(8,128)}, u32[]{:S(2)}, u32[]{:S(2)}) collective-permute-start(f32[384,256]{1,0:T(8,128)S(1)} %collective-permute-done.4.refs_3_), channel_id=1, source_target_pairs={{6,0},{7,1},{0,2},{1,3},{2,4},{3,5},{4,6},{5,7},{14,8},{15,9},{8,1... | collective-permute-start | bytes 1179656 | tf_op jit(solution)/shard_map/ppermute | solution.py:116
  117.3 19.0 %collective-permute-start.15 = (f32[384,256]{1,0:T(8,128)}, f32[384,256]{1,0:T(8,128)S(1)}, u32[]{:S(2)}, u32[]{:S(2)}) collective-permute-start(f32[384,256]{1,0:T(8,128)} %broadcast_select_fusion), channel_id=1, source_target_pairs={{6,0},{7,1},{0,2},{1,3},{2,4},{3,5},{4,6},{5,7},{14,8},{15,9},{8,1... | collective-permute-start | bytes 1179656 | tf_op jit(solution)/shard_map/ppermute | solution.py:116
  120.0 19.8 %collective-permute-start.19 = (f32[384,256]{1,0:T(8,128)}, f32[384,256]{1,0:T(8,128)S(1)}, u32[]{:S(2)}, u32[]{:S(2)}) collective-permute-start(f32[384,256]{1,0:T(8,128)} %collective-permute-done.7.refs_2_), channel_id=1, source_target_pairs={{4,2},{5,3},{6,4},{7,5},{0,6},{1,7},{12,10},{13,11},{14,12},{15,13... | collective-permute-start | bytes 1179656 | tf_op jit(solution)/shard_map/ppermute | solution.py:116
  124.0 36.4 %copy-start.11 = (f32[384,256]{1,0:T(8,128)S(1)}, f32[384,256]{1,0:T(8,128)}, u32[]{:S(2)}) copy-start(f32[384,256]{1,0:T(8,128)} %copy-done.10) | copy-start | bytes 1179652
  128.0 18.8 %collective-permute-start.18 = (f32[384,256]{1,0:T(8,128)S(1)}, f32[384,256]{1,0:T(8,128)S(1)}, u32[]{:S(2)}, u32[]{:S(2)}) collective-permute-start(f32[384,256]{1,0:T(8,128)S(1)} %bitcast.17), channel_id=1, source_target_pairs={{6,0},{7,1},{14,8},{15,9},{22,16},{23,17},{30,24},{31,25},{38,32},... | collective-permute-start | bytes 1179656 | tf_op jit(solution)/shard_map/ppermute | solution.py:116
  132.5 27.9 %collective-permute-start.14 = (f32[384,256]{1,0:T(8,128)S(1)}, f32[384,256]{1,0:T(8,128)S(1)}, u32[]{:S(2)}, u32[]{:S(2)}) collective-permute-start(f32[384,256]{1,0:T(8,128)S(1)} %broadcast_select_fusion.2), channel_id=1, source_target_pairs={{2,0},{3,1},{0,6},{1,7},{10,8},{11,9},{8,14},{9,15},{18,16},{19,17... | collective-permute-start | bytes 1179656 | tf_op jit(solution)/shard_map/ppermute | solution.py:116
  133.8 25.9 %collective-permute-start.12 = (f32[384,256]{1,0:T(8,128)}, f32[384,256]{1,0:T(8,128)S(1)}, u32[]{:S(2)}, u32[]{:S(2)}) collective-permute-start(f32[384,256]{1,0:T(8,128)} %collective-permute-done.7.refs_2_), channel_id=1, source_target_pairs={{14,6},{15,7},{22,14},{23,15},{30,22},{31,23},{6,30},{7,31},{46,38... | collective-permute-start | bytes 1179656 | tf_op jit(solution)/shard_map/ppermute | solution.py:116
  136.3 24.1 %collective-permute-start.17 = (f32[384,256]{1,0:T(8,128)}, f32[384,256]{1,0:T(8,128)S(1)}, u32[]{:S(2)}, u32[]{:S(2)}) collective-permute-start(f32[384,256]{1,0:T(8,128)} %collective-permute-done.10.refs_5_), channel_id=1, source_target_pairs={{10,2},{11,3},{12,4},{13,5},{14,6},{15,7},{18,10},{19,11},{20,12},... | collective-permute-start | bytes 1179656 | tf_op jit(solution)/shard_map/ppermute | solution.py:116
  139.8 0.8 copy-start.4
  140.6 19.8 %collective-permute-start.20 = (f32[384,256]{1,0:T(8,128)}, f32[384,256]{1,0:T(8,128)S(1)}, u32[]{:S(2)}, u32[]{:S(2)}) collective-permute-start(f32[384,256]{1,0:T(8,128)} %collective-permute-done.10.refs_5_), channel_id=1, source_target_pairs={{0,2},{1,3},{2,4},{3,5},{4,6},{5,7},{8,10},{9,11},{10,12},{11,13},... | collective-permute-start | bytes 1179656 | tf_op jit(solution)/shard_map/ppermute | solution.py:116
  141.9 4.8 %copy-start.5 = (f32[384,256]{1,0:T(8,128)S(1)}, f32[384,256]{1,0:T(8,128)}, u32[]{:S(2)}) copy-start(f32[384,256]{1,0:T(8,128)} %copy-done.4) | copy-start | bytes 1179652
  146.7 26.9 %copy-start.7 = (f32[384,256]{1,0:T(8,128)S(1)}, f32[384,256]{1,0:T(8,128)}, u32[]{:S(2)}) copy-start(f32[384,256]{1,0:T(8,128)} %copy-done.6) | copy-start | bytes 1179652
  146.7 26.9 %copy-start.9 = (f32[384,256]{1,0:T(8,128)S(1)}, f32[384,256]{1,0:T(8,128)}, u32[]{:S(2)}) copy-start(f32[384,256]{1,0:T(8,128)} %copy-done.8) | copy-start | bytes 1179652
  146.8 48.1 %collective-permute-start.25 = (f32[6,2,128,128]{3,2,1,0:T(8,128)}, f32[6,2,128,128]{3,2,1,0:T(8,128)S(1)}, u32[]{:S(2)}, u32[]{:S(2)}) collective-permute-start(f32[6,2,128,128]{3,2,1,0:T(8,128)} %get-tuple-element.22), channel_id=1, source_target_pairs={{0,1},{1,0},{2,3},{3,2},{4,5},{5,4},{6,7},{7,6},{8,9},{9,8},{10,11... | collective-permute-start | bytes 2359304 | tf_op jit(solution)/shard_map/ppermute | solution.py:306
  159.7 18.0 %collective-permute-start.21 = (f32[384,256]{1,0:T(8,128)S(1)}, f32[384,256]{1,0:T(8,128)S(1)}, u32[]{:S(2)}, u32[]{:S(2)}) collective-permute-start(f32[384,256]{1,0:T(8,128)S(1)} %broadcast_select_fusion.1), channel_id=1, source_target_pairs={{24,0},{25,1},{26,2},{27,3},{0,8},{1,9},{2,10},{3,11},{8,16},{9,17... | collective-permute-start | bytes 1179656 | tf_op jit(solution)/shard_map/ppermute | solution.py:116
  165.3 29.5 %copy-start.12 = (s32[1,17]{1,0:T(1,128)S(1)}, s32[1,17]{1,0:T(1,128)}, u32[]{:S(2)}) copy-start(s32[1,17]{1,0:T(1,128)} %param.7) | copy-start | bytes 208
  165.3 30.1 %collective-permute-start.26 = (f32[6,2,128,128]{3,2,1,0:T(8,128)}, f32[6,2,128,128]{3,2,1,0:T(8,128)}, u32[]{:S(2)}, u32[]{:S(2)}) collective-permute-start(f32[6,2,128,128]{3,2,1,0:T(8,128)} %get-tuple-element.23), channel_id=1, source_target_pairs={{0,1},{1,0},{2,3},{3,2},{4,5},{5,4},{6,7},{7,6},{8,9},{9,8},{10,11... | collective-permute-start | bytes 2359304 | tf_op jit(solution)/shard_map/ppermute | solution.py:306
  168.2 12.4 %collective-permute-start.22 = (f32[384,256]{1,0:T(8,128)S(1)}, f32[384,256]{1,0:T(8,128)S(1)}, u32[]{:S(2)}, u32[]{:S(2)}) collective-permute-start(f32[384,256]{1,0:T(8,128)S(1)} %collective-permute-done.15.refs_4_.refs_9_), channel_id=1, source_target_pairs={{2,4},{3,5},{4,6},{5,7},{10,12},{11,13},{12,14},{13,15},{18,20},{1... | collective-permute-start | bytes 1179656 | tf_op jit(solution)/shard_map/ppermute | solution.py:116
  169.6 19.5 %collective-permute-start.23 = (f32[384,256]{1,0:T(8,128)S(1)}, f32[384,256]{1,0:T(8,128)S(1)}, u32[]{:S(2)}, u32[]{:S(2)}) collective-permute-start(f32[384,256]{1,0:T(8,128)S(1)} %select_select_fusion), channel_id=1, source_target_pairs={{24,0},{25,1},{26,2},{27,3},{0,8},{1,9},{2,10},{3,11},{8,16},{9,17... | collective-permute-start | bytes 1179656 | tf_op jit(solution)/shard_map/ppermute | solution.py:116
  176.8 0.8 copy-start.2
  177.6 17.2 %collective-permute-start.24 = (f32[4,2,128,128]{3,2,1,0:T(8,128)}, f32[4,2,128,128]{3,2,1,0:T(8,128)S(1)}, u32[]{:S(2)}, u32[]{:S(2)}) collective-permute-start(f32[4,2,128,128]{3,2,1,0:T(8,128)} %get-tuple-element.21), channel_id=1, source_target_pairs={{0,1},{1,0},{2,3},{3,2},{4,5},{5,4},{6,7},{7,6},{8,9},{9,8},{10,11... | collective-permute-start | bytes 1572872 | tf_op jit(solution)/shard_map/ppermute | solution.py:306
  191.1 4.3 %collective-permute-start.27 = (f32[2,2,128,128]{3,2,1,0:T(8,128)}, f32[2,2,128,128]{3,2,1,0:T(8,128)S(1)}, u32[]{:S(2)}, u32[]{:S(2)}) collective-permute-start(f32[2,2,128,128]{3,2,1,0:T(8,128)} %get-tuple-element.24), channel_id=1, source_target_pairs={{0,1},{1,0},{2,3},{3,2},{4,5},{5,4},{6,7},{7,6},{8,9},{9,8},{10,11... | collective-permute-start | bytes 786440 | tf_op jit(solution)/shard_map/ppermute | solution.py:306
  195.4 1.0 copy-start.3

commit v3 on v2

v3 whole, which is shorter than its diff:
```python
import functools
import math

import jax
import jax.numpy as jnp
import numpy as np
from jax import lax
from jax.experimental import pallas as pl
from jax.experimental.pallas import tpu as pltpu
from jax.sharding import PartitionSpec as P

TAPS = 4
FINE = 16
COARSE = 2
NY = 4
NX = 4


def dft_rows(frames):
    groups = COARSE * FINE // 2
    w = np.zeros((2, 2, groups, frames, frames, FINE, COARSE, 2), np.float64)
    j = np.arange(FINE)
    for k in range(2):
        for g in range(groups):
            c, f = g // (FINE // 2), 2 * (g % (FINE // 2)) + k
            theta = 2.0 * math.pi * ((j * f) % FINE) / FINE
            cosine, sine = np.cos(theta) / math.sqrt(FINE), np.sin(theta) / math.sqrt(FINE)
            for m in range(frames):
                w[k, 0, g, m, m, :, c, 0] = cosine
                w[k, 0, g, m, m, :, c, 1] = sine
                w[k, 1, g, m, m, :, c, 0] = -sine
                w[k, 1, g, m, m, :, c, 1] = cosine
    return w.reshape(2, 2, groups * frames, frames * FINE * COARSE * 2).astype(np.float32)


def spectra_kernel(k_ref, own_ref, other_ref, own_lead_ref, other_lead_ref, taps_ref, w_ref, out_ref, pad):
    first = k_ref[0] == 0
    lead = own_lead_ref.shape[0]
    lanes = own_ref.shape[1]
    for source, mate, rows in (
        (own_lead_ref, other_lead_ref, pl.ds(0, lead)),
        (own_ref, other_ref, pl.ds(lead, own_ref.shape[0])),
    ):
        a, b = source[...], mate[...]
        pad[rows, 0:lanes] = jnp.where(first, a, b)
        pad[rows, lanes : 2 * lanes] = jnp.where(first, b, a)
    frame = taps_ref.shape[1]
    chunk = w_ref.shape[3]
    per = chunk // frame
    groups = out_ref.shape[0]
    tap_rows = [jnp.concatenate([taps_ref[p], taps_ref[p]], axis=1)[None] for p in range(TAPS)]
    for part in range(own_ref.shape[0] // chunk):
        total = None
        for p in range(TAPS):
            rows = pad[pl.ds(part * chunk + (TAPS - 1 - p) * frame, chunk), :]
            term = tap_rows[p] * rows.reshape(per, frame, 2 * lanes)
            total = term if total is None else total + term
        total = total.reshape(chunk, 2 * lanes)
        for ri in range(2):
            result = jnp.dot(
                w_ref[0, ri], total, precision=lax.Precision.HIGHEST, preferred_element_type=jnp.float32
            )
            out_ref[:, pl.ds(part * per, per), pl.ds(ri * 2 * lanes, 2 * lanes)] = result.reshape(
                groups, per, 2 * lanes
            )


def spectra_of(k, own, other, own_lead, other_lead, taps):
    frames = 8
    rows, lanes = own.shape
    w = jnp.asarray(dft_rows(frames))
    tap_rows = jnp.broadcast_to(jnp.repeat(taps, COARSE * 2, axis=1)[:, :, None], (TAPS, FINE * COARSE * 2, lanes))
    groups = COARSE * FINE // 2
    whole = lambda shape: pl.BlockSpec(shape, lambda i, k: (0,) * len(shape))
    goal = (groups, rows // (FINE * COARSE * 2), 4 * lanes)
    return pl.pallas_call(
        spectra_kernel,
        out_shape=jax.ShapeDtypeStruct(goal, jnp.float32),
        grid_spec=pltpu.PrefetchScalarGridSpec(
            num_scalar_prefetch=1,
            grid=(1,),
            in_specs=[
                whole(own.shape),
                whole(other.shape),
                whole(own_lead.shape),
                whole(other_lead.shape),
                whole(tap_rows.shape),
                pl.BlockSpec((1,) + w.shape[1:], lambda i, k: (k[0], 0, 0, 0)),
            ],
            out_specs=whole(goal),
            scratch_shapes=[pltpu.VMEM((rows + own_lead.shape[0], 2 * lanes), jnp.float32)],
        ),
        compiler_params=pltpu.CompilerParams(vmem_limit_bytes=32 * 2**20),
    )(k, own, other, own_lead, other_lead, tap_rows, w)


E = (
    (0, 0, 0, 0),
    (4, 4, 4, 4),
    (8, 8, 8, 8),
    (5, 5, 5, 1),
    (7, 3, 3, 3),
    (2, 2, 2, 2),
    (1, 1, 1, 5),
    (3, 7, 7, 7),
    (6, 6, 6, 6),
)


def moved(block, routes):
    pairs = []
    for columns, dy, dx in routes:
        for y in range(NY):
            for x in columns:
                for core in range(2):
                    source = ((y + dy) % NY * NX + (x + dx) % NX) * 2 + core
                    pairs.append((source, (y * NX + x) * 2 + core))
    return lax.ppermute(block, "aa", pairs)


def gather(a, x):
    every = (0, 1, 2, 3)
    b = moved(a, [(every, 1, 0)])
    a_right = moved(a, [((0, 1, 2), 0, 1)])
    a_left = moved(a, [((0,), 0, -1)])
    b_right = moved(b, [(every, 0, 1)])
    b_left = moved(b, [(every, 0, -1)])
    d = moved(b, [(every, 1, 0)])
    from_right = moved(jnp.where((x == 1) | (x == 2), a_right, b_right), [(every, 0, 1)])
    from_left = moved(jnp.where(x == 2, d, b_left), [((0, 1, 3), 0, -1)])
    from_down = moved(jnp.where(x == 3, b_right, b_left), [((1, 2, 3), 1, 0)])
    rows = a.shape[0] // 2
    halves = pl.ds(0, rows), pl.ds(rows, rows)
    far = moved(from_down[:rows], [((2, 3), 0, -1)]), moved(from_right[rows:], [((2, 3), 1, 0)])
    both = lambda *choices: tuple(tuple((columns, array, half) for columns, array in choices) for half in halves)
    return [
        both((every, a)),
        both((every, b)),
        both((every, d)),
        both((every, b_right)),
        both((every, b_left)),
        both((every, from_right)),
        both(((0, 1, 2), a_right), ((3,), from_down)),
        both(((0,), a_left), ((1, 2), from_down), ((3,), from_left)),
        tuple((((0, 1), from_left, half), ((2, 3), last, halves[0])) for half, last in zip(halves, far, strict=True)),
    ]


def split(x):
    high = x.astype(jnp.bfloat16)
    return high, (x - high.astype(jnp.float32)).astype(jnp.bfloat16)


def left_kernel(scale, block_ref, out_ref):
    total, lanes = block_ref.shape
    width = lanes // 2
    turned = block_ref[...].T * scale
    real, imag = split(turned[:width]), split(turned[width:])
    for part in range(2):
        out_ref[part, 0:width, 0:total] = real[part]
        out_ref[part, 0:width, total : 2 * total] = imag[part]
        out_ref[part, width : 2 * width, 0:total] = imag[part]
        out_ref[part, width : 2 * width, total : 2 * total] = -real[part]


def left_of(block):
    total, lanes = block.shape
    return pl.pallas_call(
        functools.partial(left_kernel, 1.0 / total),
        out_shape=jax.ShapeDtypeStruct((2, lanes, 2 * total), jnp.bfloat16),
        compiler_params=pltpu.CompilerParams(vmem_limit_bytes=24 * 2**20),
        cost_estimate=pl.CostEstimate(flops=total * lanes, bytes_accessed=8 * total * lanes, transcendentals=0),
    )(block)


def correlate_kernel(plan, at_ref, left_ref, *refs):
    n = len(plan)
    rights, (own_ref, send_ref, store, sems) = refs[:-4], refs[-4:]
    half = own_ref.shape[-1]
    width = 2 * half
    rows = store.shape[1] // 2
    first, x = at_ref[0] == 0, at_ref[1]

    def each(p, act):
        for h, choices in enumerate(plan[p]):
            for columns, place, taken in choices:

                def one():
                    goal = store.at[p, pl.ds(h * rows, rows)]
                    act(pltpu.make_async_copy(rights[place].at[taken], goal, sems.at[2 * p + h]))

                if len(choices) == 1:
                    one()
                else:
                    pl.when(functools.reduce(jnp.logical_or, [x == c for c in columns]))(one)

    dot = functools.partial(jnp.dot, preferred_element_type=jnp.float32)
    for p in range(n):
        each(p, lambda copy: copy.start())
    for p in range(n):
        each(p, lambda copy: copy.wait())
        high, low = split(jnp.concatenate([store[p, :, :width], store[p, :, width:]], axis=0))
        product = dot(left_ref[0], high) + dot(left_ref[0], low) + dot(left_ref[1], high)
        for r in range(2):
            for ri in range(2):
                rows0 = product[ri * width : ri * width + half, r * half : (r + 1) * half]
                rows1 = product[ri * width + half : (ri + 1) * width, r * half : (r + 1) * half]
                own_ref[2 * p + r, ri] = jnp.where(first, rows0, rows1)
                send_ref[2 * p + r, ri] = jnp.where(first, rows1, rows0)


def correlated(at, left, positions):
    n = len(positions)
    arrays = []

    def place_of(array):
        for place, known in enumerate(arrays):
            if known is array:
                return place
        arrays.append(array)
        return len(arrays) - 1

    plan = [
        [[(columns, place_of(array), taken) for columns, array, taken in choices] for choices in position]
        for position in positions
    ]
    width, total = left.shape[1] // 2, left.shape[2] // 2
    tiles = jax.ShapeDtypeStruct((2 * n, 2, width // 2, width // 2), jnp.float32)
    vmem = pl.BlockSpec(memory_space=pltpu.VMEM)
    return pl.pallas_call(
        functools.partial(correlate_kernel, plan),
        out_shape=(tiles, tiles),
        in_specs=[pl.BlockSpec(memory_space=pltpu.SMEM), vmem] + [pl.BlockSpec(memory_space=pl.ANY)] * len(arrays),
        out_specs=[vmem] * 2,
        scratch_shapes=[pltpu.VMEM((n, total, 2 * width), jnp.float32), pltpu.SemaphoreType.DMA((2 * n,))],
        compiler_params=pltpu.CompilerParams(vmem_limit_bytes=40 * 2**20),
        cost_estimate=pl.CostEstimate(
            flops=n * 24 * total * width * width, bytes_accessed=n * 12 * total * width, transcendentals=0
        ),
    )(at, left, *arrays)


def place_kernel(groups, at_ref, slot_ref, *refs):
    n = len(groups)
    owns, gots, (out_ref, sems) = refs[-2 * n - 2 : -n - 2], refs[-n - 2 : -2], refs[-2:]
    k, x = at_ref[0], at_ref[1]
    copies = []
    for group, own, got in zip(groups, owns, gots, strict=True):
        for i, position in enumerate(group):
            first, *others = E[position]
            e = jnp.int32(first)
            for column, value in enumerate(others):
                if value != first:
                    e = jnp.where(x == column + 1, value, e)
            copies += tile_copies(k, position, i, e, slot_ref, own, got, out_ref, sems, len(copies))

    def each(act):
        for unless, *pair in copies:
            if unless is None:
                for copy in pair:
                    act(copy)
            else:

                @pl.when(k != unless)
                def _(pair=pair):
                    for copy in pair:
                        act(copy)

    each(lambda copy: copy.start())
    each(lambda copy: copy.wait())


def tile_copies(k, position, i, e, slot_ref, own, got, out_ref, sems, count):
    copies = []
    for r in range(2):
        distance = 2 * e + r - k
        unless = 1 if position == 0 and r == 0 else 0 if position == 2 and r == 1 else None
        slot = slot_ref[jnp.clip(distance, 0, slot_ref.shape[0] - 1)]
        tile, index = 2 * i + r, 2 * (count + r)
        copies.append((
            unless,
            pltpu.make_async_copy(own.at[tile], out_ref.at[slot, k], sems.at[index]),
            pltpu.make_async_copy(got.at[tile], out_ref.at[slot, 1 - k], sems.at[index + 1]),
        ))
    return copies


def placed(at, slot, groups, before, owns, gots):
    half = owns[0].shape[-1]
    smem, vmem = pl.BlockSpec(memory_space=pltpu.SMEM), pl.BlockSpec(memory_space=pltpu.VMEM)
    earlier = [] if before is None else [before]
    tiles = sum(own.shape[0] for own in owns)
    return pl.pallas_call(
        functools.partial(place_kernel, groups),
        out_shape=jax.ShapeDtypeStruct((slot.shape[0], 2, 2, half, half), jnp.float32),
        in_specs=[smem] * 2 + [pl.BlockSpec(memory_space=pl.ANY)] * len(earlier) + [vmem] * (2 * len(owns)),
        out_specs=pl.BlockSpec(memory_space=pl.ANY),
        input_output_aliases={2: 0} if earlier else {},
        scratch_shapes=[pltpu.SemaphoreType.DMA((2 * tiles,))],
        compiler_params=pltpu.CompilerParams(vmem_limit_bytes=24 * 2**20),
        cost_estimate=pl.CostEstimate(flops=0, bytes_accessed=16 * tiles * half * half, transcendentals=0),
    )(at, slot, *earlier, *owns, *gots)


GROUPS = ((0, 1, 2, 3, 4), (5, 6, 7), (8,))


def local(voltages, taps, tile_map):
    n_ta, n_aa = lax.axis_size("ta"), lax.axis_size("aa")
    me = lax.axis_index("aa").astype(jnp.int32)
    x = lax.rem(me // 2, NX)
    at = jnp.stack([lax.rem(me, 2), x])
    samples, coarse, parts, lanes = voltages.shape
    own = voltages.reshape(samples * coarse * parts, lanes)
    lead = own[own.shape[0] - (TAPS - 1) * FINE * coarse * parts :]
    mate = [(i, i ^ 1) for i in range(n_aa)]
    later = [(t * n_aa + i, (t + 1) * n_aa + i) for t in range(n_ta - 1) for i in range(n_aa)]
    own_lead = lax.ppermute(lead, ("ta", "aa"), later)
    other_lead = lax.ppermute(lead, ("ta", "aa"), [(s, d ^ 1) for s, d in later])
    other = lax.ppermute(own, "aa", mate)
    spectra = spectra_of(at, own, other, own_lead, other_lead, taps)
    block = lax.all_to_all(spectra, "ta", split_axis=0, concat_axis=0, tiled=True).reshape(-1, 4 * lanes)
    left = left_of(block)
    slots = jnp.arange(tile_map.shape[1], dtype=jnp.int32)
    slot = jnp.sum(jnp.where(tile_map[0][None, :] == slots[:, None], slots[None, :], 0), axis=1)
    taken = gather(block, x)
    owns, gots = [], []
    for group in GROUPS:
        mine, leaving = correlated(at, left, [taken[p] for p in group])
        owns.append(mine)
        gots.append(lax.ppermute(leaving, "aa", mate))
    return placed(at, slot, GROUPS, None, owns, gots)


def solution(mesh):
    in_specs = (P("ta", None, None, "aa"), P(), P("aa", None))
    out_specs = P("aa", "ta", None, None, None)
    return jax.shard_map(local, mesh=mesh, in_specs=in_specs, out_specs=out_specs, check_vma=False)
```

time: 201 us -> 180 us (0.90)
  the two profiles are of different devices: /device:TPU:39 before, /device:TPU:37 now
where the time goes in v3:
time: 180 us
  starting transfers between devices  60.4 us (34%)
  blocking collectives  54.6 us (30%)
  waiting for transfers between devices  37.5 us (21%)
  Pallas kernels  21 us (12%)
  local copies, waits for them, and re-layouts  4.25 us (2%)
    all_to_all x1, blocking collectives, local(): lax.all_to_all(spectra, 'ta', split_axis=0, concat_axis=0, tiled=True)  54.6 us
    ppermute x11, waiting for transfers between devices, moved(): return lax.ppermute(block, 'aa', pairs)  35.2 us
    ppermute x11, starting transfers between devices, moved(): return lax.ppermute(block, 'aa', pairs)  34.4 us
    ppermute x3, starting transfers between devices, local(): gots.append(lax.ppermute(leaving, 'aa', mate))  16.4 us
    pallas_call x3, Pallas kernels, correlated(): pl.pallas_call(functools.partial(correlate_kernel, plan), out_shape=(tile...  15.1 us
  transfers between devices with their start and end apart: 17, of which 8 were waited for; matrix products, arithmetic and copies ran while one was open for 2% of the time, Pallas kernels for 9%

profile of v3, /device:TPU:37, one launch (start us, length us, event | category | flops | bytes accessed | tf_op | source)
XLA Modules:
  0.0 179.7 jit_solution(12822069255299399978)
XLA Ops:
  0.0 2.6 %collective-permute-start = (f32[1536,128]{1,0:T(8,128)}, f32[1536,128]{1,0:T(8,128)S(1)}, u32[]{:S(2)}, u32[]{:S(2)}) collective-permute-start(f32[1536,128]{1,0:T(8,128)} %bitcast.11), channel_id=1, source_target_pairs={{0,1},{1,0},{2,3},{3,2},{4,5},{5,4},{6,7},{7,6},{8,9},{9,8},{10,11... | collective-permute-start | bytes 2359304 | tf_op jit(solution)/shard_map/ppermute | solution.py:320
  2.6 0.9 slice.12
  3.5 3.4 %collective-permute-start.2 = (f32[192,128]{1,0:T(8,128)S(1)}, f32[192,128]{1,0:T(8,128)S(1)}, u32[]{:S(2)}, u32[]{:S(2)}) collective-permute-start(f32[192,128]{1,0:T(8,128)S(1)} %bitcast.13), channel_id=1, source_target_pairs={{0,33},{1,32},{2,35},{3,34},{4,37},{5,36},{6,39},{7,38},{8,41},{9,... | collective-permute-start | bytes 294920 | tf_op jit(solution)/shard_map/ppermute | solution.py:319
  6.9 3.5 %collective-permute-start.1 = (f32[192,128]{1,0:T(8,128)S(1)}, f32[192,128]{1,0:T(8,128)S(1)}, u32[]{:S(2)}, u32[]{:S(2)}) collective-permute-start(f32[192,128]{1,0:T(8,128)S(1)} %bitcast.14), channel_id=1, source_target_pairs={{0,32},{1,33},{2,34},{3,35},{4,36},{5,37},{6,38},{7,39},{8,40},{9,... | collective-permute-start | bytes 294920 | tf_op jit(solution)/shard_map/ppermute | solution.py:318
  10.5 0.8 broadcast_in_dim.26
  11.3 0.1 broadcast_in_dim.27
  11.3 0.1 pad_add_fusion.k_ref.at_ref
  11.4 0.0 collective-permute-done.2.other_lead_ref
  11.4 1.3 collective-permute-done.1.own_lead_ref
  12.7 0.0 collective-permute-done.other_ref
  12.7 0.1 broadcast_in_dim.28.taps_ref
  12.8 0.0 copy-start
  12.8 1.2 copy-done
  14.0 0.0 copy-start.1
  14.0 1.1 copy-done.1
  15.2 2.7 %shard_map.46 = f32[16,24,512]{2,1,0:T(8,128)S(1)} custom-call(s32[2]{0:T(128)S(1)} %pad_add_fusion.k_ref.at_ref, f32[1536,128]{1,0:T(8,128)S(1)} %bitcast.12, f32[1536,128]{1,0:T(8,128)S(1)} %collective-permute-done.other_ref, f32[192,128]{1,0:T(8,128)S(1)} %collective-permute-done.1.own_lead_ref, f32[192,128]{1,0:T(8,128)S(1)} %collective-permute-done.2.other_lead_ref, ...), custom_call_target="tpu_custom_call" | custom-call | tf_op jit(solution)/shard_map/pallas_call | solution.py:76
  17.8 54.6 %all_to_all.5 = f32[16,24,512]{2,1,0:T(8,128)S(1)} all-to-all(f32[16,24,512]{2,1,0:T(8,128)S(1)} %shard_map.46), channel_id=1, replica_groups=mesh['ta'=16,'aa'=32] {'ta'}, dimensions={0} | all-to-all | bytes 1572864 | tf_op jit(solution)/shard_map/all_to_all | solution.py:322
  72.4 4.6 %collective-permute-start.3 = (f32[384,512]{1,0:T(8,128)S(1)}, f32[384,512]{1,0:T(8,128)}, u32[]{:S(2)}, u32[]{:S(2)}) collective-permute-start(f32[384,512]{1,0:T(8,128)S(1)} %bitcast.6), channel_id=1, source_target_pairs={{8,0},{9,1},{10,2},{11,3},{12,4},{13,5},{14,6},{15,7},{16,8},{17,9... | collective-permute-start | bytes 2359304 | tf_op jit(solution)/shard_map/ppermute | solution.py:118
  77.1 2.2 %collective-permute-start.7 = (f32[384,512]{1,0:T(8,128)S(1)}, f32[384,512]{1,0:T(8,128)S(1)}, u32[]{:S(2)}, u32[]{:S(2)}) collective-permute-start(f32[384,512]{1,0:T(8,128)S(1)} %bitcast.7), channel_id=1, source_target_pairs={{2,0},{3,1},{4,2},{5,3},{6,4},{7,5},{10,8},{11,9},{12,10},{13,11},... | collective-permute-start | bytes 2359304 | tf_op jit(solution)/shard_map/ppermute | solution.py:118
  79.2 12.7 %collective-permute-done.3.refs_1_ = f32[384,512]{1,0:T(8,128)} collective-permute-done((f32[384,512]{1,0:T(8,128)S(1)}, f32[384,512]{1,0:T(8,128)}, u32[]{:S(2)}, u32[]{:S(2)}) %collective-permute-start.3) | collective-permute-done | bytes 786464 | tf_op jit(solution)/shard_map/ppermute | solution.py:118
  91.9 2.8 %collective-permute-start.6 = (f32[384,512]{1,0:T(8,128)}, f32[384,512]{1,0:T(8,128)S(1)}, u32[]{:S(2)}, u32[]{:S(2)}) collective-permute-start(f32[384,512]{1,0:T(8,128)} %collective-permute-done.3.refs_1_), channel_id=1, source_target_pairs={{6,0},{7,1},{0,2},{1,3},{2,4},{3,5},{4,6},{5,7},{14,8},{15,9},{8,1... | collective-permute-start | bytes 2359304 | tf_op jit(solution)/shard_map/ppermute | solution.py:118
  94.7 2.5 %collective-permute-start.5 = (f32[384,512]{1,0:T(8,128)}, f32[384,512]{1,0:T(8,128)S(1)}, u32[]{:S(2)}, u32[]{:S(2)}) collective-permute-start(f32[384,512]{1,0:T(8,128)} %collective-permute-done.3.refs_1_), channel_id=1, source_target_pairs={{2,0},{3,1},{4,2},{5,3},{6,4},{7,5},{0,6},{1,7},{10,8},{11,9},{12,... | collective-permute-start | bytes 2359304 | tf_op jit(solution)/shard_map/ppermute | solution.py:118
  97.2 5.4 %collective-permute-start.4 = (f32[384,512]{1,0:T(8,128)}, f32[384,512]{1,0:T(8,128)}, u32[]{:S(2)}, u32[]{:S(2)}) collective-permute-start(f32[384,512]{1,0:T(8,128)} %collective-permute-done.3.refs_1_), channel_id=1, source_target_pairs={{8,0},{9,1},{10,2},{11,3},{12,4},{13,5},{14,6},{15,7},{16,8},{17,9... | collective-permute-start | bytes 2359304 | tf_op jit(solution)/shard_map/ppermute | solution.py:118
  102.6 0.7 collective-permute-start.10
  103.3 0.0 collective-permute-done.7.refs_1_
  103.3 6.9 %collective-permute-done.6.refs_4_ = f32[384,512]{1,0:T(8,128)S(1)} collective-permute-done((f32[384,512]{1,0:T(8,128)}, f32[384,512]{1,0:T(8,128)S(1)}, u32[]{:S(2)}, u32[]{:S(2)}) %collective-permute-start.6) | collective-permute-done | bytes 786464 | tf_op jit(solution)/shard_map/ppermute | solution.py:118
  110.2 2.5 %collective-permute-done.5.refs_3_ = f32[384,512]{1,0:T(8,128)S(1)} collective-permute-done((f32[384,512]{1,0:T(8,128)}, f32[384,512]{1,0:T(8,128)S(1)}, u32[]{:S(2)}, u32[]{:S(2)}) %collective-permute-start.5) | collective-permute-done | bytes 786464 | tf_op jit(solution)/shard_map/ppermute | solution.py:118
  112.8 3.5 %collective-permute-done.4.refs_2_ = f32[384,512]{1,0:T(8,128)} collective-permute-done((f32[384,512]{1,0:T(8,128)}, f32[384,512]{1,0:T(8,128)}, u32[]{:S(2)}, u32[]{:S(2)}) %collective-permute-start.4) | collective-permute-done | bytes 786464 | tf_op jit(solution)/shard_map/ppermute | solution.py:118
  116.3 1.5 broadcast_select_fusion
  117.8 1.7 collective-permute-start.11
  119.5 5.3 %collective-permute-start.9 = (f32[384,512]{1,0:T(8,128)S(1)}, f32[384,512]{1,0:T(8,128)S(1)}, u32[]{:S(2)}, u32[]{:S(2)}) collective-permute-start(f32[384,512]{1,0:T(8,128)S(1)} %get-tuple-element.18), channel_id=1, source_target_pairs={{10,2},{11,3},{12,4},{13,5},{14,6},{15,7},{18,10},{19,11},{20,12},... | collective-permute-start | bytes 2359304 | tf_op jit(solution)/shard_map/ppermute | solution.py:118
  124.8 1.9 %collective-permute-start.8 = (f32[384,512]{1,0:T(8,128)S(1)}, f32[384,512]{1,0:T(8,128)S(1)}, u32[]{:S(2)}, u32[]{:S(2)}) collective-permute-start(f32[384,512]{1,0:T(8,128)S(1)} %get-tuple-element.19), channel_id=1, source_target_pairs={{2,0},{3,1},{4,2},{5,3},{6,4},{7,5},{0,6},{1,7},{10,8},{11,9},{12,... | collective-permute-start | bytes 2359304 | tf_op jit(solution)/shard_map/ppermute | solution.py:118
  126.8 0.3 shard_map.47.left_ref
  127.1 8.0 %shard_map.48 = (f32[10,2,128,128]{3,2,1,0:T(8,128)S(1)}, f32[10,2,128,128]{3,2,1,0:T(8,128)S(1)}) custom-call(s32[2]{0:T(128)S(1)} %pad_add_fusion.k_ref.at_ref, bf16[2,512,768]{2,1,0:T(8,128)(2,1)S(1)} %shard_map.47.left_ref, f32[384,512]{1,0:T(8,128)S(1)} %bitcast.10, f32[384,512]{1,0:T(8,128)} %collective-permute-done.3.refs_1_, ...), custom_call_target="tpu_custom_call" | custom-call | flops 3019898880 | bytes 5898240 | tf_op jit(solution)/shard_map/pallas_call | solution.py:230
  135.1 6.9 %collective-permute-start.14 = (f32[10,2,128,128]{3,2,1,0:T(8,128)S(1)}, f32[10,2,128,128]{3,2,1,0:T(8,128)S(1)}, u32[]{:S(2)}, u32[]{:S(2)}) collective-permute-start(f32[10,2,128,128]{3,2,1,0:T(8,128)S(1)} %get-tuple-element.14), channel_id=1, source_target_pairs={{0,1},{1,0},{2,3},{3,2},{4,5},{5,4},{6,7},{7,6},{8,9},{9,8},{10,11... | collective-permute-start | bytes 3932168 | tf_op jit(solution)/shard_map/ppermute | solution.py:331
  142.0 0.0 collective-permute-done.10.refs_3_
  142.0 0.0 collective-permute-done.11.refs_4_.refs_0_
  142.0 0.0 collective-permute-done.9.refs_2_
  142.0 0.0 collective-permute-done.8.refs_0_
  142.0 5.3 %shard_map.49 = (f32[6,2,128,128]{3,2,1,0:T(8,128)S(1)}, f32[6,2,128,128]{3,2,1,0:T(8,128)S(1)}) custom-call(s32[2]{0:T(128)S(1)} %pad_add_fusion.k_ref.at_ref, bf16[2,512,768]{2,1,0:T(8,128)(2,1)S(1)} %shard_map.47.left_ref, f32[384,512]{1,0:T(8,128)S(1)} %collective-permute-done.8.refs_0_, f32[384,512]{1,0:T(8,128)S(1)} %collective-permute-done.7.refs_1_, ...), custom_call_target="tpu_custom_call" | custom-call | flops 1811939328 | bytes 3538944 | tf_op jit(solution)/shard_map/pallas_call | solution.py:230
  147.3 6.6 %collective-permute-start.15 = (f32[6,2,128,128]{3,2,1,0:T(8,128)S(1)}, f32[6,2,128,128]{3,2,1,0:T(8,128)S(1)}, u32[]{:S(2)}, u32[]{:S(2)}) collective-permute-start(f32[6,2,128,128]{3,2,1,0:T(8,128)S(1)} %get-tuple-element.15), channel_id=1, source_target_pairs={{0,1},{1,0},{2,3},{3,2},{4,5},{5,4},{6,7},{7,6},{8,9},{9,8},{10,11... | collective-permute-start | bytes 2359304 | tf_op jit(solution)/shard_map/ppermute | solution.py:331
  153.9 4.5 %collective-permute-start.12 = (f32[192,512]{1,0:T(8,128)S(1)}, f32[192,512]{1,0:T(8,128)S(1)}, u32[]{:S(2)}, u32[]{:S(2)}) collective-permute-start(f32[192,512]{1,0:T(8,128)S(1)} %slice.16), channel_id=1, source_target_pairs={{2,4},{3,5},{4,6},{5,7},{10,12},{11,13},{12,14},{13,15},{18,20},{1... | collective-permute-start | bytes 1179656 | tf_op jit(solution)/shard_map/ppermute | solution.py:118
  158.5 0.0 copy-start.2
  158.5 2.7 %collective-permute-start.13 = (f32[192,512]{1,0:T(8,128)S(1)}, f32[192,512]{1,0:T(8,128)S(1)}, u32[]{:S(2)}, u32[]{:S(2)}) collective-permute-start(f32[192,512]{1,0:T(8,128)S(1)} %slice.17), channel_id=1, source_target_pairs={{12,4},{13,5},{14,6},{15,7},{20,12},{21,13},{22,14},{23,15},{28,20... | collective-permute-start | bytes 1179656 | tf_op jit(solution)/shard_map/ppermute | solution.py:118
  161.2 5.7 %collective-permute-done.12.refs_1_ = f32[192,512]{1,0:T(8,128)S(1)} collective-permute-done((f32[192,512]{1,0:T(8,128)S(1)}, f32[192,512]{1,0:T(8,128)S(1)}, u32[]{:S(2)}, u32[]{:S(2)}) %collective-permute-start.12) | collective-permute-done | bytes 393248 | tf_op jit(solution)/shard_map/ppermute | solution.py:118
  167.0 3.8 %collective-permute-done.13.refs_2_ = f32[192,512]{1,0:T(8,128)S(1)} collective-permute-done((f32[192,512]{1,0:T(8,128)S(1)}, f32[192,512]{1,0:T(8,128)S(1)}, u32[]{:S(2)}, u32[]{:S(2)}) %collective-permute-start.13) | collective-permute-done | bytes 393248 | tf_op jit(solution)/shard_map/ppermute | solution.py:118
  170.8 1.7 shard_map.50
  172.6 3.0 %collective-permute-start.16 = (f32[2,2,128,128]{3,2,1,0:T(8,128)S(1)}, f32[2,2,128,128]{3,2,1,0:T(8,128)S(1)}, u32[]{:S(2)}, u32[]{:S(2)}) collective-permute-start(f32[2,2,128,128]{3,2,1,0:T(8,128)S(1)} %get-tuple-element.16), channel_id=1, source_target_pairs={{0,1},{1,0},{2,3},{3,2},{4,5},{5,4},{6,7},{7,6},{8,9},{9,8},{10,11... | collective-permute-start | bytes 786440 | tf_op jit(solution)/shard_map/ppermute | solution.py:331
  175.6 0.0 copy-done.2
  175.6 0.1 select_reduce_fusion.slot_ref
  175.7 0.0 collective-permute-done.14.refs_3_
  175.7 1.0 collective-permute-done.16.refs_5_
  176.7 0.0 collective-permute-done.15.refs_4_
  176.7 2.9 %shard_map.51 = f32[17,2,2,128,128]{4,3,2,1,0:T(8,128)} custom-call(s32[2]{0:T(128)S(1)} %pad_add_fusion.k_ref.at_ref, s32[17]{0:T(128)S(1)} %select_reduce_fusion.slot_ref, f32[10,2,128,128]{3,2,1,0:T(8,128)S(1)} %get-tuple-element.11.refs_0_, f32[6,2,128,128]{3,2,1,0:T(8,128)S(1)} %get-tuple-element.12.refs_1_, ...), custom_call_target="tpu_custom_call" | custom-call | bytes 4718592 | tf_op jit(solution)/shard_map/pallas_call | solution.py:293
  (2 shorter events, 0.1 us)
Async XLA Ops:
  0.0 12.7 %collective-permute-start = (f32[1536,128]{1,0:T(8,128)}, f32[1536,128]{1,0:T(8,128)S(1)}, u32[]{:S(2)}, u32[]{:S(2)}) collective-permute-start(f32[1536,128]{1,0:T(8,128)} %bitcast.11), channel_id=1, source_target_pairs={{0,1},{1,0},{2,3},{3,2},{4,5},{5,4},{6,7},{7,6},{8,9},{9,8},{10,11... | collective-permute-start | bytes 2359304 | tf_op jit(solution)/shard_map/ppermute | solution.py:320
  3.5 7.9 %collective-permute-start.2 = (f32[192,128]{1,0:T(8,128)S(1)}, f32[192,128]{1,0:T(8,128)S(1)}, u32[]{:S(2)}, u32[]{:S(2)}) collective-permute-start(f32[192,128]{1,0:T(8,128)S(1)} %bitcast.13), channel_id=1, source_target_pairs={{0,33},{1,32},{2,35},{3,34},{4,37},{5,36},{6,39},{7,38},{8,41},{9,... | collective-permute-start | bytes 294920 | tf_op jit(solution)/shard_map/ppermute | solution.py:319
  6.9 5.8 %collective-permute-start.1 = (f32[192,128]{1,0:T(8,128)S(1)}, f32[192,128]{1,0:T(8,128)S(1)}, u32[]{:S(2)}, u32[]{:S(2)}) collective-permute-start(f32[192,128]{1,0:T(8,128)S(1)} %bitcast.14), channel_id=1, source_target_pairs={{0,32},{1,33},{2,34},{3,35},{4,36},{5,37},{6,38},{7,39},{8,40},{9,... | collective-permute-start | bytes 294920 | tf_op jit(solution)/shard_map/ppermute | solution.py:318
  12.8 1.2 copy-start
  14.0 1.1 copy-start.1
  72.4 19.5 %collective-permute-start.3 = (f32[384,512]{1,0:T(8,128)S(1)}, f32[384,512]{1,0:T(8,128)}, u32[]{:S(2)}, u32[]{:S(2)}) collective-permute-start(f32[384,512]{1,0:T(8,128)S(1)} %bitcast.6), channel_id=1, source_target_pairs={{8,0},{9,1},{10,2},{11,3},{12,4},{13,5},{14,6},{15,7},{16,8},{17,9... | collective-permute-start | bytes 2359304 | tf_op jit(solution)/shard_map/ppermute | solution.py:118
  77.1 26.3 %collective-permute-start.7 = (f32[384,512]{1,0:T(8,128)S(1)}, f32[384,512]{1,0:T(8,128)S(1)}, u32[]{:S(2)}, u32[]{:S(2)}) collective-permute-start(f32[384,512]{1,0:T(8,128)S(1)} %bitcast.7), channel_id=1, source_target_pairs={{2,0},{3,1},{4,2},{5,3},{6,4},{7,5},{10,8},{11,9},{12,10},{13,11},... | collective-permute-start | bytes 2359304 | tf_op jit(solution)/shard_map/ppermute | solution.py:118
  91.9 18.3 %collective-permute-start.6 = (f32[384,512]{1,0:T(8,128)}, f32[384,512]{1,0:T(8,128)S(1)}, u32[]{:S(2)}, u32[]{:S(2)}) collective-permute-start(f32[384,512]{1,0:T(8,128)} %collective-permute-done.3.refs_1_), channel_id=1, source_target_pairs={{6,0},{7,1},{0,2},{1,3},{2,4},{3,5},{4,6},{5,7},{14,8},{15,9},{8,1... | collective-permute-start | bytes 2359304 | tf_op jit(solution)/shard_map/ppermute | solution.py:118
  94.7 18.1 %collective-permute-start.5 = (f32[384,512]{1,0:T(8,128)}, f32[384,512]{1,0:T(8,128)S(1)}, u32[]{:S(2)}, u32[]{:S(2)}) collective-permute-start(f32[384,512]{1,0:T(8,128)} %collective-permute-done.3.refs_1_), channel_id=1, source_target_pairs={{2,0},{3,1},{4,2},{5,3},{6,4},{7,5},{0,6},{1,7},{10,8},{11,9},{12,... | collective-permute-start | bytes 2359304 | tf_op jit(solution)/shard_map/ppermute | solution.py:118
  97.2 19.1 %collective-permute-start.4 = (f32[384,512]{1,0:T(8,128)}, f32[384,512]{1,0:T(8,128)}, u32[]{:S(2)}, u32[]{:S(2)}) collective-permute-start(f32[384,512]{1,0:T(8,128)} %collective-permute-done.3.refs_1_), channel_id=1, source_target_pairs={{8,0},{9,1},{10,2},{11,3},{12,4},{13,5},{14,6},{15,7},{16,8},{17,9... | collective-permute-start | bytes 2359304 | tf_op jit(solution)/shard_map/ppermute | solution.py:118
  102.6 39.4 %collective-permute-start.10 = (f32[384,512]{1,0:T(8,128)S(1)}, f32[384,512]{1,0:T(8,128)S(1)}, u32[]{:S(2)}, u32[]{:S(2)}) collective-permute-start(f32[384,512]{1,0:T(8,128)S(1)} %bitcast.8), channel_id=1, source_target_pairs={{6,0},{7,1},{14,8},{15,9},{22,16},{23,17},{30,24},{31,25},{38,32},... | collective-permute-start | bytes 2359304 | tf_op jit(solution)/shard_map/ppermute | solution.py:118
  117.8 24.2 %collective-permute-start.11 = (f32[384,512]{1,0:T(8,128)S(1)}, f32[384,512]{1,0:T(8,128)S(1)}, u32[]{:S(2)}, u32[]{:S(2)}) collective-permute-start(f32[384,512]{1,0:T(8,128)S(1)} %get-tuple-element.17), channel_id=1, source_target_pairs={{6,0},{7,1},{0,2},{1,3},{4,6},{5,7},{14,8},{15,9},{8,10},{9,11},{1... | collective-permute-start | bytes 2359304 | tf_op jit(solution)/shard_map/ppermute | solution.py:118
  119.5 22.5 %collective-permute-start.9 = (f32[384,512]{1,0:T(8,128)S(1)}, f32[384,512]{1,0:T(8,128)S(1)}, u32[]{:S(2)}, u32[]{:S(2)}) collective-permute-start(f32[384,512]{1,0:T(8,128)S(1)} %get-tuple-element.18), channel_id=1, source_target_pairs={{10,2},{11,3},{12,4},{13,5},{14,6},{15,7},{18,10},{19,11},{20,12},... | collective-permute-start | bytes 2359304 | tf_op jit(solution)/shard_map/ppermute | solution.py:118
  124.8 17.2 %collective-permute-start.8 = (f32[384,512]{1,0:T(8,128)S(1)}, f32[384,512]{1,0:T(8,128)S(1)}, u32[]{:S(2)}, u32[]{:S(2)}) collective-permute-start(f32[384,512]{1,0:T(8,128)S(1)} %get-tuple-element.19), channel_id=1, source_target_pairs={{2,0},{3,1},{4,2},{5,3},{6,4},{7,5},{0,6},{1,7},{10,8},{11,9},{12,... | collective-permute-start | bytes 2359304 | tf_op jit(solution)/shard_map/ppermute | solution.py:118
  135.1 40.6 %collective-permute-start.14 = (f32[10,2,128,128]{3,2,1,0:T(8,128)S(1)}, f32[10,2,128,128]{3,2,1,0:T(8,128)S(1)}, u32[]{:S(2)}, u32[]{:S(2)}) collective-permute-start(f32[10,2,128,128]{3,2,1,0:T(8,128)S(1)} %get-tuple-element.14), channel_id=1, source_target_pairs={{0,1},{1,0},{2,3},{3,2},{4,5},{5,4},{6,7},{7,6},{8,9},{9,8},{10,11... | collective-permute-start | bytes 3932168 | tf_op jit(solution)/shard_map/ppermute | solution.py:331
  147.3 29.4 %collective-permute-start.15 = (f32[6,2,128,128]{3,2,1,0:T(8,128)S(1)}, f32[6,2,128,128]{3,2,1,0:T(8,128)S(1)}, u32[]{:S(2)}, u32[]{:S(2)}) collective-permute-start(f32[6,2,128,128]{3,2,1,0:T(8,128)S(1)} %get-tuple-element.15), channel_id=1, source_target_pairs={{0,1},{1,0},{2,3},{3,2},{4,5},{5,4},{6,7},{7,6},{8,9},{9,8},{10,11... | collective-permute-start | bytes 2359304 | tf_op jit(solution)/shard_map/ppermute | solution.py:331
  153.9 13.0 %collective-permute-start.12 = (f32[192,512]{1,0:T(8,128)S(1)}, f32[192,512]{1,0:T(8,128)S(1)}, u32[]{:S(2)}, u32[]{:S(2)}) collective-permute-start(f32[192,512]{1,0:T(8,128)S(1)} %slice.16), channel_id=1, source_target_pairs={{2,4},{3,5},{4,6},{5,7},{10,12},{11,13},{12,14},{13,15},{18,20},{1... | collective-permute-start | bytes 1179656 | tf_op jit(solution)/shard_map/ppermute | solution.py:118
  158.5 17.1 %copy-start.2 = (s32[1,17]{1,0:T(1,128)S(1)}, s32[1,17]{1,0:T(1,128)}, u32[]{:S(2)}) copy-start(s32[1,17]{1,0:T(1,128)} %param.6) | copy-start | bytes 208
  158.5 12.3 %collective-permute-start.13 = (f32[192,512]{1,0:T(8,128)S(1)}, f32[192,512]{1,0:T(8,128)S(1)}, u32[]{:S(2)}, u32[]{:S(2)}) collective-permute-start(f32[192,512]{1,0:T(8,128)S(1)} %slice.17), channel_id=1, source_target_pairs={{12,4},{13,5},{14,6},{15,7},{20,12},{21,13},{22,14},{23,15},{28,20... | collective-permute-start | bytes 1179656 | tf_op jit(solution)/shard_map/ppermute | solution.py:118
  172.6 4.2 %collective-permute-start.16 = (f32[2,2,128,128]{3,2,1,0:T(8,128)S(1)}, f32[2,2,128,128]{3,2,1,0:T(8,128)S(1)}, u32[]{:S(2)}, u32[]{:S(2)}) collective-permute-start(f32[2,2,128,128]{3,2,1,0:T(8,128)S(1)} %get-tuple-element.16), channel_id=1, source_target_pairs={{0,1},{1,0},{2,3},{3,2},{4,5},{5,4},{6,7},{7,6},{8,9},{9,8},{10,11... | collective-permute-start | bytes 786440 | tf_op jit(solution)/shard_map/ppermute | solution.py:331

commit v4 on v3

--- a/solution.py
+++ b/solution.py
@@ -122,16 +122,16 @@
     every = (0, 1, 2, 3)
     b = moved(a, [(every, 1, 0)])
     a_right = moved(a, [((0, 1, 2), 0, 1)])
-    a_left = moved(a, [((0,), 0, -1)])
     b_right = moved(b, [(every, 0, 1)])
     b_left = moved(b, [(every, 0, -1)])
     d = moved(b, [(every, 1, 0)])
     from_right = moved(jnp.where((x == 1) | (x == 2), a_right, b_right), [(every, 0, 1)])
-    from_left = moved(jnp.where(x == 2, d, b_left), [((0, 1, 3), 0, -1)])
-    from_down = moved(jnp.where(x == 3, b_right, b_left), [((1, 2, 3), 1, 0)])
+    from_left = moved(jnp.where((x == 1) | (x == 2), d, b_left), [(every, 0, -1)])
+    from_down = moved(jnp.where(x == 3, b_right, b_left), [((1, 3), 1, 0)])
+    from_up = moved(b_left, [((0,), -1, 0)])
     rows = a.shape[0] // 2
     halves = pl.ds(0, rows), pl.ds(rows, rows)
-    far = moved(from_down[:rows], [((2, 3), 0, -1)]), moved(from_right[rows:], [((2, 3), 1, 0)])
+    far = moved(jnp.where(x == 2, from_left[:rows], from_down[:rows]), [((2, 3), 0, -1)]), moved(from_right[rows:], [((2, 3), 1, 0)])
     both = lambda *choices: tuple(tuple((columns, array, half) for columns, array in choices) for half in halves)
     return [
         both((every, a)),
@@ -141,7 +141,7 @@
         both((every, b_left)),
         both((every, from_right)),
         both(((0, 1, 2), a_right), ((3,), from_down)),
-        both(((0,), a_left), ((1, 2), from_down), ((3,), from_left)),
+        both(((0,), from_up), ((1,), from_down), ((2, 3), from_left)),
         tuple((((0, 1), from_left, half), ((2, 3), last, halves[0])) for half, last in zip(halves, far, strict=True)),
     ]
 
@@ -174,32 +174,22 @@
 
 
 def correlate_kernel(plan, at_ref, left_ref, *refs):
-    n = len(plan)
-    rights, (own_ref, send_ref, store, sems) = refs[:-4], refs[-4:]
+    rights, (own_ref, send_ref) = refs[:-2], refs[-2:]
     half = own_ref.shape[-1]
     width = 2 * half
-    rows = store.shape[1] // 2
     first, x = at_ref[0] == 0, at_ref[1]
-
-    def each(p, act):
-        for h, choices in enumerate(plan[p]):
-            for columns, place, taken in choices:
-
-                def one():
-                    goal = store.at[p, pl.ds(h * rows, rows)]
-                    act(pltpu.make_async_copy(rights[place].at[taken], goal, sems.at[2 * p + h]))
-
-                if len(choices) == 1:
-                    one()
-                else:
-                    pl.when(functools.reduce(jnp.logical_or, [x == c for c in columns]))(one)
-
     dot = functools.partial(jnp.dot, preferred_element_type=jnp.float32)
-    for p in range(n):
-        each(p, lambda copy: copy.start())
-    for p in range(n):
-        each(p, lambda copy: copy.wait())
-        high, low = split(jnp.concatenate([store[p, :, :width], store[p, :, width:]], axis=0))
+    for p, halves in enumerate(plan):
+        values = []
+        for choices in halves:
+            _, place, taken = choices[-1]
+            value = rights[place][taken, :]
+            for columns, place, taken in choices[:-1]:
+                here = functools.reduce(jnp.logical_or, [x == c for c in columns])
+                value = jnp.where(here, rights[place][taken, :], value)
+            values.append(value)
+        parts = [v[:, :width] for v in values] + [v[:, width:] for v in values]
+        high, low = split(jnp.concatenate(parts, axis=0))
         product = dot(left_ref[0], high) + dot(left_ref[0], low) + dot(left_ref[1], high)
         for r in range(2):
             for ri in range(2):
@@ -230,10 +220,9 @@
     return pl.pallas_call(
         functools.partial(correlate_kernel, plan),
         out_shape=(tiles, tiles),
-        in_specs=[pl.BlockSpec(memory_space=pltpu.SMEM), vmem] + [pl.BlockSpec(memory_space=pl.ANY)] * len(arrays),
+        in_specs=[pl.BlockSpec(memory_space=pltpu.SMEM)] + [vmem] * (1 + len(arrays)),
         out_specs=[vmem] * 2,
-        scratch_shapes=[pltpu.VMEM((n, total, 2 * width), jnp.float32), pltpu.SemaphoreType.DMA((2 * n,))],
-        compiler_params=pltpu.CompilerParams(vmem_limit_bytes=40 * 2**20),
+        compiler_params=pltpu.CompilerParams(vmem_limit_bytes=20 * 2**20),
         cost_estimate=pl.CostEstimate(
             flops=n * 24 * total * width * width, bytes_accessed=n * 12 * total * width, transcendentals=0
         ),
@@ -302,7 +291,7 @@
     )(at, slot, *earlier, *owns, *gots)
 
 
-GROUPS = ((0, 1, 2, 3, 4), (5, 6, 7), (8,))
+GROUPS = ((0, 1, 2, 3, 4), (5, 6, 7, 8))
 
 
 def local(voltages, taps, tile_map):
@@ -324,12 +313,11 @@
     slots = jnp.arange(tile_map.shape[1], dtype=jnp.int32)
     slot = jnp.sum(jnp.where(tile_map[0][None, :] == slots[:, None], slots[None, :], 0), axis=1)
     taken = gather(block, x)
-    owns, gots = [], []
+    out = None
     for group in GROUPS:
         mine, leaving = correlated(at, left, [taken[p] for p in group])
-        owns.append(mine)
-        gots.append(lax.ppermute(leaving, "aa", mate))
-    return placed(at, slot, GROUPS, None, owns, gots)
+        out = placed(at, slot, (group,), out, [mine], [lax.ppermute(leaving, "aa", mate)])
+    return out
 
 
 def solution(mesh):

time: 180 us -> 169 us (0.939)
  Pallas kernels: 21 us -> 15 us
  waiting for transfers between devices: 37.5 us -> 33.8 us
    pallas_call x3 -> x2, Pallas kernels: 15.1 us -> 7.9 us  [correlated(): pl.pallas_call(functools.partial(correlate_kernel, plan), out_shape=(tile...]
    ppermute x3 -> x2, starting transfers between devices: 16.4 us -> 9.96 us  [local(): lax.ppermute(leaving, 'aa', mate)]
    ppermute x11, starting transfers between devices: 34.4 us -> 39.4 us  [moved(): return lax.ppermute(block, 'aa', pairs)]
    ppermute x11, waiting for transfers between devices: 35.2 us -> 32.2 us  [moved(): return lax.ppermute(block, 'aa', pairs)]
    pallas_call x1 -> x2, Pallas kernels: 2.94 us -> 4.11 us  [placed(): pl.pallas_call(functools.partial(place_kernel, groups), out_shape=jax.Sha...]
  transfers between devices with their start and end apart: 17 -> 16, of which waited for: 8 -> 8; matrix products, arithmetic and copies ran while one was open for 2% -> 1% of each run, Pallas kernels for 9% -> 6%
where the time goes in v4:
time: 169 us
  starting transfers between devices  58.9 us (35%)
  blocking collectives  54.6 us (32%)
  waiting for transfers between devices  33.8 us (20%)
  Pallas kernels  15 us (9%)
  local copies, waits for them, and re-layouts  4.23 us (3%)
  other arithmetic  1.73 us (1%)
    all_to_all x1, blocking collectives, local(): lax.all_to_all(spectra, 'ta', split_axis=0, concat_axis=0, tiled=True)  54.6 us
    ppermute x11, starting transfers between devices, moved(): return lax.ppermute(block, 'aa', pairs)  39.4 us
    ppermute x11, waiting for transfers between devices, moved(): return lax.ppermute(block, 'aa', pairs)  32.2 us
    ppermute x2, starting transfers between devices, local(): lax.ppermute(leaving, 'aa', mate)  9.96 us
    pallas_call x2, Pallas kernels, correlated(): pl.pallas_call(functools.partial(correlate_kernel, plan), out_shape=(tile...  7.9 us
    pallas_call x2, Pallas kernels, placed(): pl.pallas_call(functools.partial(place_kernel, groups), out_shape=jax.Sha...  4.11 us
    ppermute x1, starting transfers between devices, local(): own_lead = lax.ppermute(lead, ('ta', 'aa'), later)  3.55 us
    ppermute x1, starting transfers between devices, local(): lax.ppermute(lead, ('ta', 'aa'), [(s, d ^ 1) for s, d in later])  3.43 us
  transfers between devices with their start and end apart: 16, of which 8 were waited for; matrix products, arithmetic and copies ran while one was open for 1% of the time, Pallas kernels for 6%

profile of v4, /device:TPU:37, one launch (start us, length us, event | category | flops | bytes accessed | tf_op | source)
XLA Modules:
  0.0 168.6 jit_solution(17415221881112168128)
XLA Ops:
  0.0 2.6 %collective-permute-start = (f32[1536,128]{1,0:T(8,128)}, f32[1536,128]{1,0:T(8,128)S(1)}, u32[]{:S(2)}, u32[]{:S(2)}) collective-permute-start(f32[1536,128]{1,0:T(8,128)} %bitcast.10), channel_id=1, source_target_pairs={{0,1},{1,0},{2,3},{3,2},{4,5},{5,4},{6,7},{7,6},{8,9},{9,8},{10,11... | collective-permute-start | bytes 2359304 | tf_op jit(solution)/shard_map/ppermute | solution.py:309
  2.6 0.9 slice.15
  3.5 3.4 %collective-permute-start.2 = (f32[192,128]{1,0:T(8,128)S(1)}, f32[192,128]{1,0:T(8,128)S(1)}, u32[]{:S(2)}, u32[]{:S(2)}) collective-permute-start(f32[192,128]{1,0:T(8,128)S(1)} %bitcast.12), channel_id=1, source_target_pairs={{0,33},{1,32},{2,35},{3,34},{4,37},{5,36},{6,39},{7,38},{8,41},{9,... | collective-permute-start | bytes 294920 | tf_op jit(solution)/shard_map/ppermute | solution.py:308
  6.9 3.5 %collective-permute-start.1 = (f32[192,128]{1,0:T(8,128)S(1)}, f32[192,128]{1,0:T(8,128)S(1)}, u32[]{:S(2)}, u32[]{:S(2)}) collective-permute-start(f32[192,128]{1,0:T(8,128)S(1)} %bitcast.13), channel_id=1, source_target_pairs={{0,32},{1,33},{2,34},{3,35},{4,36},{5,37},{6,38},{7,39},{8,40},{9,... | collective-permute-start | bytes 294920 | tf_op jit(solution)/shard_map/ppermute | solution.py:307
  10.5 0.8 broadcast_in_dim.26
  11.3 0.1 broadcast_in_dim.27
  11.3 0.1 pad_add_fusion.k_ref.at_ref
  11.4 0.0 collective-permute-done.2.other_lead_ref
  11.4 1.3 collective-permute-done.1.own_lead_ref
  12.7 0.0 collective-permute-done.other_ref
  12.7 0.1 broadcast_in_dim.28.taps_ref
  12.8 0.0 copy-start
  12.8 1.2 copy-done
  14.0 0.0 copy-start.1
  14.0 1.1 copy-done.1
  15.2 2.7 %shard_map.46 = f32[16,24,512]{2,1,0:T(8,128)S(1)} custom-call(s32[2]{0:T(128)S(1)} %pad_add_fusion.k_ref.at_ref, f32[1536,128]{1,0:T(8,128)S(1)} %bitcast.11, f32[1536,128]{1,0:T(8,128)S(1)} %collective-permute-done.other_ref, f32[192,128]{1,0:T(8,128)S(1)} %collective-permute-done.1.own_lead_ref, f32[192,128]{1,0:T(8,128)S(1)} %collective-permute-done.2.other_lead_ref, ...), custom_call_target="tpu_custom_call" | custom-call | tf_op jit(solution)/shard_map/pallas_call | solution.py:76
  17.8 54.6 %all_to_all.5 = f32[16,24,512]{2,1,0:T(8,128)S(1)} all-to-all(f32[16,24,512]{2,1,0:T(8,128)S(1)} %shard_map.46), channel_id=1, replica_groups=mesh['ta'=16,'aa'=32] {'ta'}, dimensions={0} | all-to-all | bytes 1572864 | tf_op jit(solution)/shard_map/all_to_all | solution.py:311
  72.4 4.6 %collective-permute-start.3 = (f32[384,512]{1,0:T(8,128)S(1)}, f32[384,512]{1,0:T(8,128)}, u32[]{:S(2)}, u32[]{:S(2)}) collective-permute-start(f32[384,512]{1,0:T(8,128)S(1)} %bitcast.6), channel_id=1, source_target_pairs={{8,0},{9,1},{10,2},{11,3},{12,4},{13,5},{14,6},{15,7},{16,8},{17,9... | collective-permute-start | bytes 2359304 | tf_op jit(solution)/shard_map/ppermute | solution.py:118
  77.1 2.2 %collective-permute-start.8 = (f32[384,512]{1,0:T(8,128)S(1)}, f32[384,512]{1,0:T(8,128)S(1)}, u32[]{:S(2)}, u32[]{:S(2)}) collective-permute-start(f32[384,512]{1,0:T(8,128)S(1)} %bitcast.7), channel_id=1, source_target_pairs={{2,0},{3,1},{4,2},{5,3},{6,4},{7,5},{10,8},{11,9},{12,10},{13,11},... | collective-permute-start | bytes 2359304 | tf_op jit(solution)/shard_map/ppermute | solution.py:118
  79.2 12.7 %collective-permute-done.3.refs_1_ = f32[384,512]{1,0:T(8,128)} collective-permute-done((f32[384,512]{1,0:T(8,128)S(1)}, f32[384,512]{1,0:T(8,128)}, u32[]{:S(2)}, u32[]{:S(2)}) %collective-permute-start.3) | collective-permute-done | bytes 786464 | tf_op jit(solution)/shard_map/ppermute | solution.py:118
  91.9 2.8 %collective-permute-start.6 = (f32[384,512]{1,0:T(8,128)}, f32[384,512]{1,0:T(8,128)S(1)}, u32[]{:S(2)}, u32[]{:S(2)}) collective-permute-start(f32[384,512]{1,0:T(8,128)} %collective-permute-done.3.refs_1_), channel_id=1, source_target_pairs={{6,0},{7,1},{0,2},{1,3},{2,4},{3,5},{4,6},{5,7},{14,8},{15,9},{8,1... | collective-permute-start | bytes 2359304 | tf_op jit(solution)/shard_map/ppermute | solution.py:118
  94.7 2.5 %collective-permute-start.5 = (f32[384,512]{1,0:T(8,128)}, f32[384,512]{1,0:T(8,128)S(1)}, u32[]{:S(2)}, u32[]{:S(2)}) collective-permute-start(f32[384,512]{1,0:T(8,128)} %collective-permute-done.3.refs_1_), channel_id=1, source_target_pairs={{2,0},{3,1},{4,2},{5,3},{6,4},{7,5},{0,6},{1,7},{10,8},{11,9},{12,... | collective-permute-start | bytes 2359304 | tf_op jit(solution)/shard_map/ppermute | solution.py:118
  97.2 5.4 %collective-permute-start.4 = (f32[384,512]{1,0:T(8,128)}, f32[384,512]{1,0:T(8,128)}, u32[]{:S(2)}, u32[]{:S(2)}) collective-permute-start(f32[384,512]{1,0:T(8,128)} %collective-permute-done.3.refs_1_), channel_id=1, source_target_pairs={{8,0},{9,1},{10,2},{11,3},{12,4},{13,5},{14,6},{15,7},{16,8},{17,9... | collective-permute-start | bytes 2359304 | tf_op jit(solution)/shard_map/ppermute | solution.py:118
  102.6 0.0 collective-permute-done.8.refs_1_
  102.6 7.6 %collective-permute-done.6.refs_4_ = f32[384,512]{1,0:T(8,128)S(1)} collective-permute-done((f32[384,512]{1,0:T(8,128)}, f32[384,512]{1,0:T(8,128)S(1)}, u32[]{:S(2)}, u32[]{:S(2)}) %collective-permute-start.6) | collective-permute-done | bytes 786464 | tf_op jit(solution)/shard_map/ppermute | solution.py:118
  110.2 2.5 %collective-permute-done.5.refs_3_ = f32[384,512]{1,0:T(8,128)S(1)} collective-permute-done((f32[384,512]{1,0:T(8,128)}, f32[384,512]{1,0:T(8,128)S(1)}, u32[]{:S(2)}, u32[]{:S(2)}) %collective-permute-start.5) | collective-permute-done | bytes 786464 | tf_op jit(solution)/shard_map/ppermute | solution.py:118
  112.8 3.5 %collective-permute-done.4.refs_2_ = f32[384,512]{1,0:T(8,128)} collective-permute-done((f32[384,512]{1,0:T(8,128)}, f32[384,512]{1,0:T(8,128)}, u32[]{:S(2)}, u32[]{:S(2)}) %collective-permute-start.4) | collective-permute-done | bytes 786464 | tf_op jit(solution)/shard_map/ppermute | solution.py:118
  116.3 1.5 broadcast_select_fusion.1
  117.8 1.9 %collective-permute-start.12 = (f32[384,512]{1,0:T(8,128)S(1)}, f32[384,512]{1,0:T(8,128)S(1)}, u32[]{:S(2)}, u32[]{:S(2)}) collective-permute-start(f32[384,512]{1,0:T(8,128)S(1)} %get-tuple-element.13), channel_id=1, source_target_pairs={{6,0},{7,1},{0,2},{1,3},{2,4},{3,5},{4,6},{5,7},{14,8},{15,9},{8,1... | collective-permute-start | bytes 2359304 | tf_op jit(solution)/shard_map/ppermute | solution.py:118
  119.7 0.7 collective-permute-start.10
  120.4 8.0 %collective-permute-start.9 = (f32[384,512]{1,0:T(8,128)S(1)}, f32[384,512]{1,0:T(8,128)S(1)}, u32[]{:S(2)}, u32[]{:S(2)}) collective-permute-start(f32[384,512]{1,0:T(8,128)S(1)} %get-tuple-element.15), channel_id=1, source_target_pairs={{2,0},{3,1},{4,2},{5,3},{6,4},{7,5},{0,6},{1,7},{10,8},{11,9},{12,... | collective-permute-start | bytes 2359304 | tf_op jit(solution)/shard_map/ppermute | solution.py:118
  128.4 0.7 collective-permute-start.11
  129.1 5.2 %collective-permute-done.12.refs_4_ = f32[384,512]{1,0:T(8,128)S(1)} collective-permute-done((f32[384,512]{1,0:T(8,128)S(1)}, f32[384,512]{1,0:T(8,128)S(1)}, u32[]{:S(2)}, u32[]{:S(2)}) %collective-permute-start.12) | collective-permute-done | bytes 786464 | tf_op jit(solution)/shard_map/ppermute | solution.py:118
  134.3 0.0 collective-permute-done.10.refs_2_
  134.3 0.1 slice_select_fusion
  134.4 6.0 %collective-permute-start.13 = (f32[192,512]{1,0:T(8,128)S(1)}, f32[192,512]{1,0:T(8,128)S(1)}, u32[]{:S(2)}, u32[]{:S(2)}) collective-permute-start(f32[192,512]{1,0:T(8,128)S(1)} %slice_select_fusion), channel_id=1, source_target_pairs={{2,4},{3,5},{4,6},{5,7},{10,12},{11,13},{12,14},{13,15},{18,20},{1... | collective-permute-start | bytes 1179656 | tf_op jit(solution)/shard_map/ppermute | solution.py:118
  140.4 0.7 collective-permute-done.9.refs_0_
  141.1 4.6 %collective-permute-start.14 = (f32[192,512]{1,0:T(8,128)S(1)}, f32[192,512]{1,0:T(8,128)S(1)}, u32[]{:S(2)}, u32[]{:S(2)}) collective-permute-start(f32[192,512]{1,0:T(8,128)S(1)} %slice.22), channel_id=1, source_target_pairs={{12,4},{13,5},{14,6},{15,7},{20,12},{21,13},{22,14},{23,15},{28,20... | collective-permute-start | bytes 1179656 | tf_op jit(solution)/shard_map/ppermute | solution.py:118
  145.7 0.3 shard_map.47.left_ref
  146.0 4.7 %shard_map.48 = (f32[10,2,128,128]{3,2,1,0:T(8,128)S(1)}, f32[10,2,128,128]{3,2,1,0:T(8,128)S(1)}) custom-call(s32[2]{0:T(128)S(1)} %pad_add_fusion.k_ref.at_ref, bf16[2,512,768]{2,1,0:T(8,128)(2,1)S(1)} %shard_map.47.left_ref, f32[384,512]{1,0:T(8,128)S(1)} %bitcast.9, f32[384,512]{1,0:T(8,128)} %collective-permute-done.3.refs_1_, ...), custom_call_target="tpu_custom_call" | custom-call | flops 3019898880 | bytes 5898240 | tf_op jit(solution)/shard_map/pallas_call | solution.py:220
  150.7 0.0 copy-start.2
  150.7 8.0 %collective-permute-start.7 = (f32[10,2,128,128]{3,2,1,0:T(8,128)S(1)}, f32[10,2,128,128]{3,2,1,0:T(8,128)S(1)}, u32[]{:S(2)}, u32[]{:S(2)}) collective-permute-start(f32[10,2,128,128]{3,2,1,0:T(8,128)S(1)} %get-tuple-element.10), channel_id=1, source_target_pairs={{0,1},{1,0},{2,3},{3,2},{4,5},{5,4},{6,7},{7,6},{8,9},{9,8},{10,11... | collective-permute-start | bytes 3932168 | tf_op jit(solution)/shard_map/ppermute | solution.py:319
  158.8 0.0 collective-permute-done.11.refs_3_
  158.8 0.0 collective-permute-done.13.refs_5_
  158.8 0.0 collective-permute-done.14.refs_6_
  158.8 3.2 %shard_map.50 = (f32[8,2,128,128]{3,2,1,0:T(8,128)S(1)}, f32[8,2,128,128]{3,2,1,0:T(8,128)S(1)}) custom-call(s32[2]{0:T(128)S(1)} %pad_add_fusion.k_ref.at_ref, bf16[2,512,768]{2,1,0:T(8,128)(2,1)S(1)} %shard_map.47.left_ref, f32[384,512]{1,0:T(8,128)S(1)} %collective-permute-done.9.refs_0_, f32[384,512]{1,0:T(8,128)S(1)} %collective-permute-done.8.refs_1_, ...), custom_call_target="tpu_custom_call" | custom-call | flops 2415919104 | bytes 4718592 | tf_op jit(solution)/shard_map/pallas_call | solution.py:220
  162.0 1.9 %collective-permute-start.15 = (f32[8,2,128,128]{3,2,1,0:T(8,128)S(1)}, f32[8,2,128,128]{3,2,1,0:T(8,128)S(1)}, u32[]{:S(2)}, u32[]{:S(2)}) collective-permute-start(f32[8,2,128,128]{3,2,1,0:T(8,128)S(1)} %get-tuple-element.12), channel_id=1, source_target_pairs={{0,1},{1,0},{2,3},{3,2},{4,5},{5,4},{6,7},{7,6},{8,9},{9,8},{10,11... | collective-permute-start | bytes 3145736 | tf_op jit(solution)/shard_map/ppermute | solution.py:319
  164.0 0.0 copy-done.2
  164.0 0.1 select_reduce_fusion.slot_ref
  164.1 0.0 collective-permute-done.7.refs_1_
  164.1 2.1 %shard_map.49.refs_0_ = f32[17,2,2,128,128]{4,3,2,1,0:T(8,128)} custom-call(s32[2]{0:T(128)S(1)} %pad_add_fusion.k_ref.at_ref, s32[17]{0:T(128)S(1)} %select_reduce_fusion.slot_ref, f32[10,2,128,128]{3,2,1,0:T(8,128)S(1)} %get-tuple-element.9.refs_0_, f32[10,2,128,128]{3,2,1,0:T(8,128)S(1)} %collective-permute-done.7.refs_1_), custom_call_target="tpu_custom_call" | custom-call | bytes 2621440 | tf_op jit(solution)/shard_map/pallas_call | solution.py:282
  166.2 0.4 collective-permute-done.15.refs_2_
  166.6 2.0 %shard_map.51 = f32[17,2,2,128,128]{4,3,2,1,0:T(8,128)} custom-call(s32[2]{0:T(128)S(1)} %pad_add_fusion.k_ref.at_ref, s32[17]{0:T(128)S(1)} %select_reduce_fusion.slot_ref, f32[17,2,2,128,128]{4,3,2,1,0:T(8,128)} %shard_map.49.refs_0_, f32[8,2,128,128]{3,2,1,0:T(8,128)S(1)} %get-tuple-element.11.refs_1_, ...), custom_call_target="tpu_custom_call", output_to_operand_aliasing={{}: (2, {})} | custom-call | bytes 2097152 | tf_op jit(solution)/shard_map/pallas_call | solution.py:282
  (1 shorter events, 0.0 us)
Async XLA Ops:
  0.0 12.7 %collective-permute-start = (f32[1536,128]{1,0:T(8,128)}, f32[1536,128]{1,0:T(8,128)S(1)}, u32[]{:S(2)}, u32[]{:S(2)}) collective-permute-start(f32[1536,128]{1,0:T(8,128)} %bitcast.10), channel_id=1, source_target_pairs={{0,1},{1,0},{2,3},{3,2},{4,5},{5,4},{6,7},{7,6},{8,9},{9,8},{10,11... | collective-permute-start | bytes 2359304 | tf_op jit(solution)/shard_map/ppermute | solution.py:309
  3.5 7.9 %collective-permute-start.2 = (f32[192,128]{1,0:T(8,128)S(1)}, f32[192,128]{1,0:T(8,128)S(1)}, u32[]{:S(2)}, u32[]{:S(2)}) collective-permute-start(f32[192,128]{1,0:T(8,128)S(1)} %bitcast.12), channel_id=1, source_target_pairs={{0,33},{1,32},{2,35},{3,34},{4,37},{5,36},{6,39},{7,38},{8,41},{9,... | collective-permute-start | bytes 294920 | tf_op jit(solution)/shard_map/ppermute | solution.py:308
  6.9 5.8 %collective-permute-start.1 = (f32[192,128]{1,0:T(8,128)S(1)}, f32[192,128]{1,0:T(8,128)S(1)}, u32[]{:S(2)}, u32[]{:S(2)}) collective-permute-start(f32[192,128]{1,0:T(8,128)S(1)} %bitcast.13), channel_id=1, source_target_pairs={{0,32},{1,33},{2,34},{3,35},{4,36},{5,37},{6,38},{7,39},{8,40},{9,... | collective-permute-start | bytes 294920 | tf_op jit(solution)/shard_map/ppermute | solution.py:307
  12.8 1.2 copy-start
  14.0 1.1 copy-start.1
  72.4 19.5 %collective-permute-start.3 = (f32[384,512]{1,0:T(8,128)S(1)}, f32[384,512]{1,0:T(8,128)}, u32[]{:S(2)}, u32[]{:S(2)}) collective-permute-start(f32[384,512]{1,0:T(8,128)S(1)} %bitcast.6), channel_id=1, source_target_pairs={{8,0},{9,1},{10,2},{11,3},{12,4},{13,5},{14,6},{15,7},{16,8},{17,9... | collective-permute-start | bytes 2359304 | tf_op jit(solution)/shard_map/ppermute | solution.py:118
  77.1 25.6 %collective-permute-start.8 = (f32[384,512]{1,0:T(8,128)S(1)}, f32[384,512]{1,0:T(8,128)S(1)}, u32[]{:S(2)}, u32[]{:S(2)}) collective-permute-start(f32[384,512]{1,0:T(8,128)S(1)} %bitcast.7), channel_id=1, source_target_pairs={{2,0},{3,1},{4,2},{5,3},{6,4},{7,5},{10,8},{11,9},{12,10},{13,11},... | collective-permute-start | bytes 2359304 | tf_op jit(solution)/shard_map/ppermute | solution.py:118
  91.9 18.3 %collective-permute-start.6 = (f32[384,512]{1,0:T(8,128)}, f32[384,512]{1,0:T(8,128)S(1)}, u32[]{:S(2)}, u32[]{:S(2)}) collective-permute-start(f32[384,512]{1,0:T(8,128)} %collective-permute-done.3.refs_1_), channel_id=1, source_target_pairs={{6,0},{7,1},{0,2},{1,3},{2,4},{3,5},{4,6},{5,7},{14,8},{15,9},{8,1... | collective-permute-start | bytes 2359304 | tf_op jit(solution)/shard_map/ppermute | solution.py:118
  94.7 18.1 %collective-permute-start.5 = (f32[384,512]{1,0:T(8,128)}, f32[384,512]{1,0:T(8,128)S(1)}, u32[]{:S(2)}, u32[]{:S(2)}) collective-permute-start(f32[384,512]{1,0:T(8,128)} %collective-permute-done.3.refs_1_), channel_id=1, source_target_pairs={{2,0},{3,1},{4,2},{5,3},{6,4},{7,5},{0,6},{1,7},{10,8},{11,9},{12,... | collective-permute-start | bytes 2359304 | tf_op jit(solution)/shard_map/ppermute | solution.py:118
  97.2 19.1 %collective-permute-start.4 = (f32[384,512]{1,0:T(8,128)}, f32[384,512]{1,0:T(8,128)}, u32[]{:S(2)}, u32[]{:S(2)}) collective-permute-start(f32[384,512]{1,0:T(8,128)} %collective-permute-done.3.refs_1_), channel_id=1, source_target_pairs={{8,0},{9,1},{10,2},{11,3},{12,4},{13,5},{14,6},{15,7},{16,8},{17,9... | collective-permute-start | bytes 2359304 | tf_op jit(solution)/shard_map/ppermute | solution.py:118
  117.8 16.5 %collective-permute-start.12 = (f32[384,512]{1,0:T(8,128)S(1)}, f32[384,512]{1,0:T(8,128)S(1)}, u32[]{:S(2)}, u32[]{:S(2)}) collective-permute-start(f32[384,512]{1,0:T(8,128)S(1)} %get-tuple-element.13), channel_id=1, source_target_pairs={{6,0},{7,1},{0,2},{1,3},{2,4},{3,5},{4,6},{5,7},{14,8},{15,9},{8,1... | collective-permute-start | bytes 2359304 | tf_op jit(solution)/shard_map/ppermute | solution.py:118
  119.7 14.6 %collective-permute-start.10 = (f32[384,512]{1,0:T(8,128)S(1)}, f32[384,512]{1,0:T(8,128)S(1)}, u32[]{:S(2)}, u32[]{:S(2)}) collective-permute-start(f32[384,512]{1,0:T(8,128)S(1)} %get-tuple-element.14), channel_id=1, source_target_pairs={{10,2},{11,3},{14,6},{15,7},{18,10},{19,11},{22,14},{23,15},{26,18... | collective-permute-start | bytes 2359304 | tf_op jit(solution)/shard_map/ppermute | solution.py:118
  120.4 20.6 %collective-permute-start.9 = (f32[384,512]{1,0:T(8,128)S(1)}, f32[384,512]{1,0:T(8,128)S(1)}, u32[]{:S(2)}, u32[]{:S(2)}) collective-permute-start(f32[384,512]{1,0:T(8,128)S(1)} %get-tuple-element.15), channel_id=1, source_target_pairs={{2,0},{3,1},{4,2},{5,3},{6,4},{7,5},{0,6},{1,7},{10,8},{11,9},{12,... | collective-permute-start | bytes 2359304 | tf_op jit(solution)/shard_map/ppermute | solution.py:118
  128.4 30.4 %collective-permute-start.11 = (f32[384,512]{1,0:T(8,128)S(1)}, f32[384,512]{1,0:T(8,128)S(1)}, u32[]{:S(2)}, u32[]{:S(2)}) collective-permute-start(f32[384,512]{1,0:T(8,128)S(1)} %collective-permute-done.6.refs_4_), channel_id=1, source_target_pairs={{24,0},{25,1},{0,8},{1,9},{8,16},{9,17},{16,24},{17,25},{56,32},{5... | collective-permute-start | bytes 2359304 | tf_op jit(solution)/shard_map/ppermute | solution.py:118
  134.4 24.4 %collective-permute-start.13 = (f32[192,512]{1,0:T(8,128)S(1)}, f32[192,512]{1,0:T(8,128)S(1)}, u32[]{:S(2)}, u32[]{:S(2)}) collective-permute-start(f32[192,512]{1,0:T(8,128)S(1)} %slice_select_fusion), channel_id=1, source_target_pairs={{2,4},{3,5},{4,6},{5,7},{10,12},{11,13},{12,14},{13,15},{18,20},{1... | collective-permute-start | bytes 1179656 | tf_op jit(solution)/shard_map/ppermute | solution.py:118
  141.1 17.7 %collective-permute-start.14 = (f32[192,512]{1,0:T(8,128)S(1)}, f32[192,512]{1,0:T(8,128)S(1)}, u32[]{:S(2)}, u32[]{:S(2)}) collective-permute-start(f32[192,512]{1,0:T(8,128)S(1)} %slice.22), channel_id=1, source_target_pairs={{12,4},{13,5},{14,6},{15,7},{20,12},{21,13},{22,14},{23,15},{28,20... | collective-permute-start | bytes 1179656 | tf_op jit(solution)/shard_map/ppermute | solution.py:118
  150.7 13.3 %copy-start.2 = (s32[1,17]{1,0:T(1,128)S(1)}, s32[1,17]{1,0:T(1,128)}, u32[]{:S(2)}) copy-start(s32[1,17]{1,0:T(1,128)} %param.6) | copy-start | bytes 208
  150.7 13.4 %collective-permute-start.7 = (f32[10,2,128,128]{3,2,1,0:T(8,128)S(1)}, f32[10,2,128,128]{3,2,1,0:T(8,128)S(1)}, u32[]{:S(2)}, u32[]{:S(2)}) collective-permute-start(f32[10,2,128,128]{3,2,1,0:T(8,128)S(1)} %get-tuple-element.10), channel_id=1, source_target_pairs={{0,1},{1,0},{2,3},{3,2},{4,5},{5,4},{6,7},{7,6},{8,9},{9,8},{10,11... | collective-permute-start | bytes 3932168 | tf_op jit(solution)/shard_map/ppermute | solution.py:319
  162.0 4.6 %collective-permute-start.15 = (f32[8,2,128,128]{3,2,1,0:T(8,128)S(1)}, f32[8,2,128,128]{3,2,1,0:T(8,128)S(1)}, u32[]{:S(2)}, u32[]{:S(2)}) collective-permute-start(f32[8,2,128,128]{3,2,1,0:T(8,128)S(1)} %get-tuple-element.12), channel_id=1, source_target_pairs={{0,1},{1,0},{2,3},{3,2},{4,5},{5,4},{6,7},{7,6},{8,9},{9,8},{10,11... | collective-permute-start | bytes 3145736 | tf_op jit(solution)/shard_map/ppermute | solution.py:319

commit v5 on v4

--- a/solution.py
+++ b/solution.py
@@ -118,7 +118,7 @@
     return lax.ppermute(block, "aa", pairs)
 
 
-def gather(a, x):
+def gather(a, x, work):
     every = (0, 1, 2, 3)
     b = moved(a, [(every, 1, 0)])
     a_right = moved(a, [((0, 1, 2), 0, 1)])
@@ -131,14 +131,11 @@
     from_up = moved(b_left, [((0,), -1, 0)])
     rows = a.shape[0] // 2
     halves = pl.ds(0, rows), pl.ds(rows, rows)
-    far = moved(jnp.where(x == 2, from_left[:rows], from_down[:rows]), [((2, 3), 0, -1)]), moved(from_right[rows:], [((2, 3), 1, 0)])
     both = lambda *choices: tuple(tuple((columns, array, half) for columns, array in choices) for half in halves)
-    return [
-        both((every, a)),
-        both((every, b)),
-        both((every, d)),
-        both((every, b_right)),
-        both((every, b_left)),
+    near = [both((every, array)) for array in (a, b, d, b_right, b_left)]
+    not_yet = jnp.minimum(jnp.abs(work(near)[0, 0, :1, :1]), 0.0) != 0.0
+    far = moved(jnp.where((x == 2) | not_yet, from_left[:rows], from_down[:rows]), [((2, 3), 0, -1)]), moved(from_right[rows:], [((2, 3), 1, 0)])
+    return near + [
         both((every, from_right)),
         both(((0, 1, 2), a_right), ((3,), from_down)),
         both(((0,), from_up), ((1,), from_down), ((2, 3), from_left)),
@@ -291,7 +288,7 @@
     )(at, slot, *earlier, *owns, *gots)
 
 
-GROUPS = ((0, 1, 2, 3, 4), (5, 6, 7, 8))
+GROUPS = ((0, 1, 2, 3, 4), (5, 6), (7, 8))
 
 
 def local(voltages, taps, tile_map):
@@ -312,12 +309,21 @@
     left = left_of(block)
     slots = jnp.arange(tile_map.shape[1], dtype=jnp.int32)
     slot = jnp.sum(jnp.where(tile_map[0][None, :] == slots[:, None], slots[None, :], 0), axis=1)
-    taken = gather(block, x)
-    out = None
-    for group in GROUPS:
-        mine, leaving = correlated(at, left, [taken[p] for p in group])
-        out = placed(at, slot, (group,), out, [mine], [lax.ppermute(leaving, "aa", mate)])
-    return out
+    slots = jnp.arange(tile_map.shape[1], dtype=jnp.int32)
+    slot = jnp.sum(jnp.where(tile_map[0][None, :] == slots[:, None], slots[None, :], 0), axis=1)
+    owns, gots = [], []
+
+    def work(positions):
+        mine, leaving = correlated(at, left, positions)
+        owns.append(mine)
+        gots.append(lax.ppermute(leaving, "aa", mate))
+        return mine
+
+    taken = gather(block, x, work)
+    for group in GROUPS[1:]:
+        work([taken[p] for p in group])
+    out = placed(at, slot, GROUPS[:-1], None, owns[:-1], gots[:-1])
+    return placed(at, slot, GROUPS[-1:], out, owns[-1:], gots[-1:])
 
 
 def solution(mesh):

time: 169 us -> 167 us (0.988)
  the two profiles are of different devices: /device:TPU:37 before, /device:TPU:39 now
where the time goes in v5:
time: 167 us; the launch traced here: 166 us
  starting transfers between devices  62.2 us (37%)
  blocking collectives  54.6 us (33%)
  waiting for transfers between devices  27.5 us (16%)
  Pallas kernels  15.7 us (9%)
  local copies, waits for them, and re-layouts  4.75 us (3%)
    all_to_all x1, blocking collectives, local(): lax.all_to_all(spectra, 'ta', split_axis=0, concat_axis=0, tiled=True)  54.6 us
    ppermute x11, starting transfers between devices, moved(): return lax.ppermute(block, 'aa', pairs)  32.6 us
    ppermute x11, waiting for transfers between devices, moved(): return lax.ppermute(block, 'aa', pairs)  26.2 us
    ppermute x3, starting transfers between devices, work(): gots.append(lax.ppermute(leaving, 'aa', mate))  20 us
    pallas_call x3, Pallas kernels, correlated(): pl.pallas_call(functools.partial(correlate_kernel, plan), out_shape=(tile...  8.63 us
    pallas_call x2, Pallas kernels, placed(): pl.pallas_call(functools.partial(place_kernel, groups), out_shape=jax.Sha...  4.12 us
    ppermute x1, starting transfers between devices, local(): own_lead = lax.ppermute(lead, ('ta', 'aa'), later)  3.55 us
    ppermute x1, starting transfers between devices, local(): lax.ppermute(lead, ('ta', 'aa'), [(s, d ^ 1) for s, d in later])  3.43 us
  transfers between devices with their start and end apart: 17, of which 6 were waited for; matrix products, arithmetic and copies ran while one was open for 2% of the time, Pallas kernels for 7%

profile of v5, /device:TPU:39, one launch (start us, length us, event | category | flops | bytes accessed | tf_op | source)
XLA Modules:
  0.0 166.3 jit_solution(3513007119275442974)
XLA Ops:
  0.0 2.6 %collective-permute-start = (f32[1536,128]{1,0:T(8,128)}, f32[1536,128]{1,0:T(8,128)S(1)}, u32[]{:S(2)}, u32[]{:S(2)}) collective-permute-start(f32[1536,128]{1,0:T(8,128)} %bitcast.13), channel_id=1, source_target_pairs={{0,1},{1,0},{2,3},{3,2},{4,5},{5,4},{6,7},{7,6},{8,9},{9,8},{10,11... | collective-permute-start | bytes 2359304 | tf_op jit(solution)/shard_map/ppermute | solution.py:306
  2.6 0.9 slice.18
  3.5 3.4 %collective-permute-start.2 = (f32[192,128]{1,0:T(8,128)S(1)}, f32[192,128]{1,0:T(8,128)S(1)}, u32[]{:S(2)}, u32[]{:S(2)}) collective-permute-start(f32[192,128]{1,0:T(8,128)S(1)} %bitcast.15), channel_id=1, source_target_pairs={{0,33},{1,32},{2,35},{3,34},{4,37},{5,36},{6,39},{7,38},{8,41},{9,... | collective-permute-start | bytes 294920 | tf_op jit(solution)/shard_map/ppermute | solution.py:305
  6.9 3.5 %collective-permute-start.1 = (f32[192,128]{1,0:T(8,128)S(1)}, f32[192,128]{1,0:T(8,128)S(1)}, u32[]{:S(2)}, u32[]{:S(2)}) collective-permute-start(f32[192,128]{1,0:T(8,128)S(1)} %bitcast.16), channel_id=1, source_target_pairs={{0,32},{1,33},{2,34},{3,35},{4,36},{5,37},{6,38},{7,39},{8,40},{9,... | collective-permute-start | bytes 294920 | tf_op jit(solution)/shard_map/ppermute | solution.py:304
  10.5 0.8 broadcast_in_dim.36
  11.3 0.1 broadcast_in_dim.37
  11.3 0.1 pad_add_fusion.k_ref.at_ref
  11.4 0.0 collective-permute-done.2.other_lead_ref
  11.4 1.3 collective-permute-done.1.own_lead_ref
  12.7 0.0 collective-permute-done.other_ref
  12.7 0.1 broadcast_in_dim.38.taps_ref
  12.8 0.0 copy-start
  12.8 1.2 copy-done
  14.0 0.0 copy-start.1
  14.0 1.1 copy-done.1
  15.2 2.7 %shard_map.46 = f32[16,24,512]{2,1,0:T(8,128)S(1)} custom-call(s32[2]{0:T(128)S(1)} %pad_add_fusion.k_ref.at_ref, f32[1536,128]{1,0:T(8,128)S(1)} %bitcast.14, f32[1536,128]{1,0:T(8,128)S(1)} %collective-permute-done.other_ref, f32[192,128]{1,0:T(8,128)S(1)} %collective-permute-done.1.own_lead_ref, f32[192,128]{1,0:T(8,128)S(1)} %collective-permute-done.2.other_lead_ref, ...), custom_call_target="tpu_custom_call" | custom-call | tf_op jit(solution)/shard_map/pallas_call | solution.py:76
  17.8 54.6 %all_to_all.5 = f32[16,24,512]{2,1,0:T(8,128)S(1)} all-to-all(f32[16,24,512]{2,1,0:T(8,128)S(1)} %shard_map.46), channel_id=1, replica_groups=mesh['ta'=16,'aa'=32] {'ta'}, dimensions={0} | all-to-all | bytes 1572864 | tf_op jit(solution)/shard_map/all_to_all | solution.py:308
  72.4 4.6 %collective-permute-start.3 = (f32[384,512]{1,0:T(8,128)S(1)}, f32[384,512]{1,0:T(8,128)}, u32[]{:S(2)}, u32[]{:S(2)}) collective-permute-start(f32[384,512]{1,0:T(8,128)S(1)} %bitcast.9), channel_id=1, source_target_pairs={{8,0},{9,1},{10,2},{11,3},{12,4},{13,5},{14,6},{15,7},{16,8},{17,9... | collective-permute-start | bytes 2359304 | tf_op jit(solution)/shard_map/ppermute | solution.py:118
  77.1 2.5 %collective-permute-start.7 = (f32[384,512]{1,0:T(8,128)S(1)}, f32[384,512]{1,0:T(8,128)S(1)}, u32[]{:S(2)}, u32[]{:S(2)}) collective-permute-start(f32[384,512]{1,0:T(8,128)S(1)} %bitcast.10), channel_id=1, source_target_pairs={{2,0},{3,1},{4,2},{5,3},{6,4},{7,5},{10,8},{11,9},{12,10},{13,11},... | collective-permute-start | bytes 2359304 | tf_op jit(solution)/shard_map/ppermute | solution.py:118
  79.6 12.3 %collective-permute-done.3.refs_1_ = f32[384,512]{1,0:T(8,128)} collective-permute-done((f32[384,512]{1,0:T(8,128)S(1)}, f32[384,512]{1,0:T(8,128)}, u32[]{:S(2)}, u32[]{:S(2)}) %collective-permute-start.3) | collective-permute-done | bytes 786464 | tf_op jit(solution)/shard_map/ppermute | solution.py:118
  91.9 2.1 %collective-permute-start.6 = (f32[384,512]{1,0:T(8,128)}, f32[384,512]{1,0:T(8,128)S(1)}, u32[]{:S(2)}, u32[]{:S(2)}) collective-permute-start(f32[384,512]{1,0:T(8,128)} %collective-permute-done.3.refs_1_), channel_id=1, source_target_pairs={{6,0},{7,1},{0,2},{1,3},{2,4},{3,5},{4,6},{5,7},{14,8},{15,9},{8,1... | collective-permute-start | bytes 2359304 | tf_op jit(solution)/shard_map/ppermute | solution.py:118
  94.0 3.2 %collective-permute-start.5 = (f32[384,512]{1,0:T(8,128)}, f32[384,512]{1,0:T(8,128)S(1)}, u32[]{:S(2)}, u32[]{:S(2)}) collective-permute-start(f32[384,512]{1,0:T(8,128)} %collective-permute-done.3.refs_1_), channel_id=1, source_target_pairs={{2,0},{3,1},{4,2},{5,3},{6,4},{7,5},{0,6},{1,7},{10,8},{11,9},{12,... | collective-permute-start | bytes 2359304 | tf_op jit(solution)/shard_map/ppermute | solution.py:118
  97.2 5.4 %collective-permute-start.4 = (f32[384,512]{1,0:T(8,128)}, f32[384,512]{1,0:T(8,128)}, u32[]{:S(2)}, u32[]{:S(2)}) collective-permute-start(f32[384,512]{1,0:T(8,128)} %collective-permute-done.3.refs_1_), channel_id=1, source_target_pairs={{8,0},{9,1},{10,2},{11,3},{12,4},{13,5},{14,6},{15,7},{16,8},{17,9... | collective-permute-start | bytes 2359304 | tf_op jit(solution)/shard_map/ppermute | solution.py:118
  102.6 0.0 collective-permute-done.7.refs_1_
  102.6 7.6 %collective-permute-done.6.refs_4_ = f32[384,512]{1,0:T(8,128)S(1)} collective-permute-done((f32[384,512]{1,0:T(8,128)}, f32[384,512]{1,0:T(8,128)S(1)}, u32[]{:S(2)}, u32[]{:S(2)}) %collective-permute-start.6) | collective-permute-done | bytes 786464 | tf_op jit(solution)/shard_map/ppermute | solution.py:118
  110.2 3.0 %collective-permute-done.5.refs_3_ = f32[384,512]{1,0:T(8,128)S(1)} collective-permute-done((f32[384,512]{1,0:T(8,128)}, f32[384,512]{1,0:T(8,128)S(1)}, u32[]{:S(2)}, u32[]{:S(2)}) %collective-permute-start.5) | collective-permute-done | bytes 786464 | tf_op jit(solution)/shard_map/ppermute | solution.py:118
  113.2 3.1 %collective-permute-done.4.refs_2_ = f32[384,512]{1,0:T(8,128)} collective-permute-done((f32[384,512]{1,0:T(8,128)}, f32[384,512]{1,0:T(8,128)}, u32[]{:S(2)}, u32[]{:S(2)}) %collective-permute-start.4) | collective-permute-done | bytes 786464 | tf_op jit(solution)/shard_map/ppermute | solution.py:118
  116.3 0.4 broadcast_select_fusion.1
  116.6 3.3 %collective-permute-start.13 = (f32[384,512]{1,0:T(8,128)S(1)}, f32[384,512]{1,0:T(8,128)S(1)}, u32[]{:S(2)}, u32[]{:S(2)}) collective-permute-start(f32[384,512]{1,0:T(8,128)S(1)} %get-tuple-element.17), channel_id=1, source_target_pairs={{6,0},{7,1},{0,2},{1,3},{2,4},{3,5},{4,6},{5,7},{14,8},{15,9},{8,1... | collective-permute-start | bytes 2359304 | tf_op jit(solution)/shard_map/ppermute | solution.py:118
  120.0 5.3 %collective-permute-start.9 = (f32[384,512]{1,0:T(8,128)S(1)}, f32[384,512]{1,0:T(8,128)S(1)}, u32[]{:S(2)}, u32[]{:S(2)}) collective-permute-start(f32[384,512]{1,0:T(8,128)S(1)} %get-tuple-element.18), channel_id=1, source_target_pairs={{10,2},{11,3},{14,6},{15,7},{18,10},{19,11},{22,14},{23,15},{26,18... | collective-permute-start | bytes 2359304 | tf_op jit(solution)/shard_map/ppermute | solution.py:118
  125.3 1.9 %collective-permute-start.8 = (f32[384,512]{1,0:T(8,128)S(1)}, f32[384,512]{1,0:T(8,128)S(1)}, u32[]{:S(2)}, u32[]{:S(2)}) collective-permute-start(f32[384,512]{1,0:T(8,128)S(1)} %get-tuple-element.19), channel_id=1, source_target_pairs={{2,0},{3,1},{4,2},{5,3},{6,4},{7,5},{0,6},{1,7},{10,8},{11,9},{12,... | collective-permute-start | bytes 2359304 | tf_op jit(solution)/shard_map/ppermute | solution.py:118
  127.2 0.3 shard_map.47.left_ref
  127.5 0.7 collective-permute-start.12
  128.3 4.7 %shard_map.48 = (f32[10,2,128,128]{3,2,1,0:T(8,128)S(1)}, f32[10,2,128,128]{3,2,1,0:T(8,128)S(1)}) custom-call(s32[2]{0:T(128)S(1)} %pad_add_fusion.k_ref.at_ref, bf16[2,512,768]{2,1,0:T(8,128)(2,1)S(1)} %shard_map.47.left_ref, f32[384,512]{1,0:T(8,128)S(1)} %bitcast.12, f32[384,512]{1,0:T(8,128)} %collective-permute-done.3.refs_1_, ...), custom_call_target="tpu_custom_call" | custom-call | flops 3019898880 | bytes 5898240 | tf_op jit(solution)/shard_map/pallas_call | solution.py:217
  132.9 6.8 %collective-permute-start.10 = (f32[10,2,128,128]{3,2,1,0:T(8,128)S(1)}, f32[10,2,128,128]{3,2,1,0:T(8,128)S(1)}, u32[]{:S(2)}, u32[]{:S(2)}) collective-permute-start(f32[10,2,128,128]{3,2,1,0:T(8,128)S(1)} %get-tuple-element.13), channel_id=1, source_target_pairs={{0,1},{1,0},{2,3},{3,2},{4,5},{5,4},{6,7},{7,6},{8,9},{9,8},{10,11... | collective-permute-start | bytes 3932168 | tf_op jit(solution)/shard_map/ppermute | solution.py:319
  139.8 0.5 slice.20
  140.9 0.0 collective-permute-done.13.refs_2_
  140.9 0.0 collective-permute-done.9.refs_2_.refs_1_
  140.9 0.1 slice_select_fusion
  141.0 1.3 collective-permute-start.14
  142.3 0.2 collective-permute-done.8.refs_0_
  142.5 2.2 %collective-permute-start.15 = (f32[192,512]{1,0:T(8,128)S(1)}, f32[192,512]{1,0:T(8,128)S(1)}, u32[]{:S(2)}, u32[]{:S(2)}) collective-permute-start(f32[192,512]{1,0:T(8,128)S(1)} %slice.26), channel_id=1, source_target_pairs={{12,4},{13,5},{14,6},{15,7},{20,12},{21,13},{22,14},{23,15},{28,20... | collective-permute-start | bytes 1179656 | tf_op jit(solution)/shard_map/ppermute | solution.py:118
  144.8 2.0 %shard_map.49 = (f32[4,2,128,128]{3,2,1,0:T(8,128)S(1)}, f32[4,2,128,128]{3,2,1,0:T(8,128)S(1)}) custom-call(s32[2]{0:T(128)S(1)} %pad_add_fusion.k_ref.at_ref, bf16[2,512,768]{2,1,0:T(8,128)(2,1)S(1)} %shard_map.47.left_ref, f32[384,512]{1,0:T(8,128)S(1)} %collective-permute-done.8.refs_0_, f32[384,512]{1,0:T(8,128)S(1)} %collective-permute-done.7.refs_1_, ...), custom_call_target="tpu_custom_call" | custom-call | flops 1207959552 | bytes 2359296 | tf_op jit(solution)/shard_map/pallas_call | solution.py:217
  146.7 0.0 copy-start.2
  146.8 7.8 %collective-permute-start.11 = (f32[4,2,128,128]{3,2,1,0:T(8,128)S(1)}, f32[4,2,128,128]{3,2,1,0:T(8,128)S(1)}, u32[]{:S(2)}, u32[]{:S(2)}) collective-permute-start(f32[4,2,128,128]{3,2,1,0:T(8,128)S(1)} %get-tuple-element.14), channel_id=1, source_target_pairs={{0,1},{1,0},{2,3},{3,2},{4,5},{5,4},{6,7},{7,6},{8,9},{9,8},{10,11... | collective-permute-start | bytes 1572872 | tf_op jit(solution)/shard_map/ppermute | solution.py:319
  154.5 0.0 collective-permute-done.12.refs_0_
  154.5 0.0 collective-permute-done.14.refs_3_
  154.5 0.0 collective-permute-done.15.refs_4_
  154.6 2.0 %shard_map.51 = (f32[4,2,128,128]{3,2,1,0:T(8,128)S(1)}, f32[4,2,128,128]{3,2,1,0:T(8,128)S(1)}) custom-call(s32[2]{0:T(128)S(1)} %pad_add_fusion.k_ref.at_ref, bf16[2,512,768]{2,1,0:T(8,128)(2,1)S(1)} %shard_map.47.left_ref, f32[384,512]{1,0:T(8,128)S(1)} %collective-permute-done.12.refs_0_, f32[384,512]{1,0:T(8,128)S(1)} %collective-permute-done.9.refs_2_.refs_1_, ...), custom_call_target="tpu_custom_call" | custom-call | flops 1207959552 | bytes 2359296 | tf_op jit(solution)/shard_map/pallas_call | solution.py:217
  156.6 5.4 %collective-permute-start.16 = (f32[4,2,128,128]{3,2,1,0:T(8,128)S(1)}, f32[4,2,128,128]{3,2,1,0:T(8,128)S(1)}, u32[]{:S(2)}, u32[]{:S(2)}) collective-permute-start(f32[4,2,128,128]{3,2,1,0:T(8,128)S(1)} %get-tuple-element.16), channel_id=1, source_target_pairs={{0,1},{1,0},{2,3},{3,2},{4,5},{5,4},{6,7},{7,6},{8,9},{9,8},{10,11... | collective-permute-start | bytes 1572872 | tf_op jit(solution)/shard_map/ppermute | solution.py:319
  162.0 0.0 copy-done.2
  162.0 0.1 select_reduce_fusion.slot_ref
  162.1 0.0 collective-permute-done.11.refs_3_
  162.1 0.0 collective-permute-done.10.refs_2_
  162.1 2.5 %shard_map.50.refs_0_ = f32[17,2,2,128,128]{4,3,2,1,0:T(8,128)} custom-call(s32[2]{0:T(128)S(1)} %pad_add_fusion.k_ref.at_ref, s32[17]{0:T(128)S(1)} %select_reduce_fusion.slot_ref, f32[10,2,128,128]{3,2,1,0:T(8,128)S(1)} %get-tuple-element.11.refs_0_, f32[4,2,128,128]{3,2,1,0:T(8,128)S(1)} %get-tuple-element.12.refs_1_, ...), custom_call_target="tpu_custom_call" | custom-call | bytes 3670016 | tf_op jit(solution)/shard_map/pallas_call | solution.py:279
  164.7 0.0 collective-permute-done.16.refs_2_
  164.7 1.6 shard_map.52
  (1 shorter events, 0.0 us)
Async XLA Ops:
  0.0 12.7 %collective-permute-start = (f32[1536,128]{1,0:T(8,128)}, f32[1536,128]{1,0:T(8,128)S(1)}, u32[]{:S(2)}, u32[]{:S(2)}) collective-permute-start(f32[1536,128]{1,0:T(8,128)} %bitcast.13), channel_id=1, source_target_pairs={{0,1},{1,0},{2,3},{3,2},{4,5},{5,4},{6,7},{7,6},{8,9},{9,8},{10,11... | collective-permute-start | bytes 2359304 | tf_op jit(solution)/shard_map/ppermute | solution.py:306
  3.5 7.9 %collective-permute-start.2 = (f32[192,128]{1,0:T(8,128)S(1)}, f32[192,128]{1,0:T(8,128)S(1)}, u32[]{:S(2)}, u32[]{:S(2)}) collective-permute-start(f32[192,128]{1,0:T(8,128)S(1)} %bitcast.15), channel_id=1, source_target_pairs={{0,33},{1,32},{2,35},{3,34},{4,37},{5,36},{6,39},{7,38},{8,41},{9,... | collective-permute-start | bytes 294920 | tf_op jit(solution)/shard_map/ppermute | solution.py:305
  6.9 5.8 %collective-permute-start.1 = (f32[192,128]{1,0:T(8,128)S(1)}, f32[192,128]{1,0:T(8,128)S(1)}, u32[]{:S(2)}, u32[]{:S(2)}) collective-permute-start(f32[192,128]{1,0:T(8,128)S(1)} %bitcast.16), channel_id=1, source_target_pairs={{0,32},{1,33},{2,34},{3,35},{4,36},{5,37},{6,38},{7,39},{8,40},{9,... | collective-permute-start | bytes 294920 | tf_op jit(solution)/shard_map/ppermute | solution.py:304
  12.8 1.2 copy-start
  14.0 1.1 copy-start.1
  72.4 19.5 %collective-permute-start.3 = (f32[384,512]{1,0:T(8,128)S(1)}, f32[384,512]{1,0:T(8,128)}, u32[]{:S(2)}, u32[]{:S(2)}) collective-permute-start(f32[384,512]{1,0:T(8,128)S(1)} %bitcast.9), channel_id=1, source_target_pairs={{8,0},{9,1},{10,2},{11,3},{12,4},{13,5},{14,6},{15,7},{16,8},{17,9... | collective-permute-start | bytes 2359304 | tf_op jit(solution)/shard_map/ppermute | solution.py:118
  77.1 25.6 %collective-permute-start.7 = (f32[384,512]{1,0:T(8,128)S(1)}, f32[384,512]{1,0:T(8,128)S(1)}, u32[]{:S(2)}, u32[]{:S(2)}) collective-permute-start(f32[384,512]{1,0:T(8,128)S(1)} %bitcast.10), channel_id=1, source_target_pairs={{2,0},{3,1},{4,2},{5,3},{6,4},{7,5},{10,8},{11,9},{12,10},{13,11},... | collective-permute-start | bytes 2359304 | tf_op jit(solution)/shard_map/ppermute | solution.py:118
  91.9 18.3 %collective-permute-start.6 = (f32[384,512]{1,0:T(8,128)}, f32[384,512]{1,0:T(8,128)S(1)}, u32[]{:S(2)}, u32[]{:S(2)}) collective-permute-start(f32[384,512]{1,0:T(8,128)} %collective-permute-done.3.refs_1_), channel_id=1, source_target_pairs={{6,0},{7,1},{0,2},{1,3},{2,4},{3,5},{4,6},{5,7},{14,8},{15,9},{8,1... | collective-permute-start | bytes 2359304 | tf_op jit(solution)/shard_map/ppermute | solution.py:118
  94.0 19.2 %collective-permute-start.5 = (f32[384,512]{1,0:T(8,128)}, f32[384,512]{1,0:T(8,128)S(1)}, u32[]{:S(2)}, u32[]{:S(2)}) collective-permute-start(f32[384,512]{1,0:T(8,128)} %collective-permute-done.3.refs_1_), channel_id=1, source_target_pairs={{2,0},{3,1},{4,2},{5,3},{6,4},{7,5},{0,6},{1,7},{10,8},{11,9},{12,... | collective-permute-start | bytes 2359304 | tf_op jit(solution)/shard_map/ppermute | solution.py:118
  97.2 19.1 %collective-permute-start.4 = (f32[384,512]{1,0:T(8,128)}, f32[384,512]{1,0:T(8,128)}, u32[]{:S(2)}, u32[]{:S(2)}) collective-permute-start(f32[384,512]{1,0:T(8,128)} %collective-permute-done.3.refs_1_), channel_id=1, source_target_pairs={{8,0},{9,1},{10,2},{11,3},{12,4},{13,5},{14,6},{15,7},{16,8},{17,9... | collective-permute-start | bytes 2359304 | tf_op jit(solution)/shard_map/ppermute | solution.py:118
  116.6 24.3 %collective-permute-start.13 = (f32[384,512]{1,0:T(8,128)S(1)}, f32[384,512]{1,0:T(8,128)S(1)}, u32[]{:S(2)}, u32[]{:S(2)}) collective-permute-start(f32[384,512]{1,0:T(8,128)S(1)} %get-tuple-element.17), channel_id=1, source_target_pairs={{6,0},{7,1},{0,2},{1,3},{2,4},{3,5},{4,6},{5,7},{14,8},{15,9},{8,1... | collective-permute-start | bytes 2359304 | tf_op jit(solution)/shard_map/ppermute | solution.py:118
  120.0 21.0 %collective-permute-start.9 = (f32[384,512]{1,0:T(8,128)S(1)}, f32[384,512]{1,0:T(8,128)S(1)}, u32[]{:S(2)}, u32[]{:S(2)}) collective-permute-start(f32[384,512]{1,0:T(8,128)S(1)} %get-tuple-element.18), channel_id=1, source_target_pairs={{10,2},{11,3},{14,6},{15,7},{18,10},{19,11},{22,14},{23,15},{26,18... | collective-permute-start | bytes 2359304 | tf_op jit(solution)/shard_map/ppermute | solution.py:118
  125.3 17.2 %collective-permute-start.8 = (f32[384,512]{1,0:T(8,128)S(1)}, f32[384,512]{1,0:T(8,128)S(1)}, u32[]{:S(2)}, u32[]{:S(2)}) collective-permute-start(f32[384,512]{1,0:T(8,128)S(1)} %get-tuple-element.19), channel_id=1, source_target_pairs={{2,0},{3,1},{4,2},{5,3},{6,4},{7,5},{0,6},{1,7},{10,8},{11,9},{12,... | collective-permute-start | bytes 2359304 | tf_op jit(solution)/shard_map/ppermute | solution.py:118
  127.5 27.0 %collective-permute-start.12 = (f32[384,512]{1,0:T(8,128)S(1)}, f32[384,512]{1,0:T(8,128)S(1)}, u32[]{:S(2)}, u32[]{:S(2)}) collective-permute-start(f32[384,512]{1,0:T(8,128)S(1)} %collective-permute-done.6.refs_4_), channel_id=1, source_target_pairs={{24,0},{25,1},{0,8},{1,9},{8,16},{9,17},{16,24},{17,25},{56,32},{5... | collective-permute-start | bytes 2359304 | tf_op jit(solution)/shard_map/ppermute | solution.py:118
  132.9 29.2 %collective-permute-start.10 = (f32[10,2,128,128]{3,2,1,0:T(8,128)S(1)}, f32[10,2,128,128]{3,2,1,0:T(8,128)S(1)}, u32[]{:S(2)}, u32[]{:S(2)}) collective-permute-start(f32[10,2,128,128]{3,2,1,0:T(8,128)S(1)} %get-tuple-element.13), channel_id=1, source_target_pairs={{0,1},{1,0},{2,3},{3,2},{4,5},{5,4},{6,7},{7,6},{8,9},{9,8},{10,11... | collective-permute-start | bytes 3932168 | tf_op jit(solution)/shard_map/ppermute | solution.py:319
  141.0 13.5 %collective-permute-start.14 = (f32[192,512]{1,0:T(8,128)S(1)}, f32[192,512]{1,0:T(8,128)S(1)}, u32[]{:S(2)}, u32[]{:S(2)}) collective-permute-start(f32[192,512]{1,0:T(8,128)S(1)} %slice_select_fusion), channel_id=1, source_target_pairs={{2,4},{3,5},{4,6},{5,7},{10,12},{11,13},{12,14},{13,15},{18,20},{1... | collective-permute-start | bytes 1179656 | tf_op jit(solution)/shard_map/ppermute | solution.py:118
  142.5 12.0 %collective-permute-start.15 = (f32[192,512]{1,0:T(8,128)S(1)}, f32[192,512]{1,0:T(8,128)S(1)}, u32[]{:S(2)}, u32[]{:S(2)}) collective-permute-start(f32[192,512]{1,0:T(8,128)S(1)} %slice.26), channel_id=1, source_target_pairs={{12,4},{13,5},{14,6},{15,7},{20,12},{21,13},{22,14},{23,15},{28,20... | collective-permute-start | bytes 1179656 | tf_op jit(solution)/shard_map/ppermute | solution.py:118
  146.7 15.2 %copy-start.2 = (s32[1,17]{1,0:T(1,128)S(1)}, s32[1,17]{1,0:T(1,128)}, u32[]{:S(2)}) copy-start(s32[1,17]{1,0:T(1,128)} %param.6) | copy-start | bytes 208
  146.8 15.4 %collective-permute-start.11 = (f32[4,2,128,128]{3,2,1,0:T(8,128)S(1)}, f32[4,2,128,128]{3,2,1,0:T(8,128)S(1)}, u32[]{:S(2)}, u32[]{:S(2)}) collective-permute-start(f32[4,2,128,128]{3,2,1,0:T(8,128)S(1)} %get-tuple-element.14), channel_id=1, source_target_pairs={{0,1},{1,0},{2,3},{3,2},{4,5},{5,4},{6,7},{7,6},{8,9},{9,8},{10,11... | collective-permute-start | bytes 1572872 | tf_op jit(solution)/shard_map/ppermute | solution.py:319
  156.6 8.1 %collective-permute-start.16 = (f32[4,2,128,128]{3,2,1,0:T(8,128)S(1)}, f32[4,2,128,128]{3,2,1,0:T(8,128)S(1)}, u32[]{:S(2)}, u32[]{:S(2)}) collective-permute-start(f32[4,2,128,128]{3,2,1,0:T(8,128)S(1)} %get-tuple-element.16), channel_id=1, source_target_pairs={{0,1},{1,0},{2,3},{3,2},{4,5},{5,4},{6,7},{7,6},{8,9},{9,8},{10,11... | collective-permute-start | bytes 1572872 | tf_op jit(solution)/shard_map/ppermute | solution.py:319

commit v6 on v5

--- a/solution.py
+++ b/solution.py
@@ -302,7 +302,7 @@
     mate = [(i, i ^ 1) for i in range(n_aa)]
     later = [(t * n_aa + i, (t + 1) * n_aa + i) for t in range(n_ta - 1) for i in range(n_aa)]
     own_lead = lax.ppermute(lead, ("ta", "aa"), later)
-    other_lead = lax.ppermute(lead, ("ta", "aa"), [(s, d ^ 1) for s, d in later])
+    other_lead = lax.ppermute(own_lead, "aa", mate)
     other = lax.ppermute(own, "aa", mate)
     spectra = spectra_of(at, own, other, own_lead, other_lead, taps)
     block = lax.all_to_all(spectra, "ta", split_axis=0, concat_axis=0, tiled=True).reshape(-1, 4 * lanes)

time: 167 us -> 170 us (1.018)
  waiting for transfers between devices: 27.5 us -> 30.4 us
  transfers between devices with their start and end apart: 17 -> 17, of which waited for: 6 -> 7; matrix products, arithmetic and copies ran while one was open for 2% -> 2% of each run, Pallas kernels for 7% -> 7%
where the time goes in v6:
time: 170 us; the launch traced here: 169 us
  starting transfers between devices  60.7 us (36%)
  blocking collectives  56 us (33%)
  waiting for transfers between devices  30.4 us (18%)
  Pallas kernels  15.7 us (9%)
  local copies, waits for them, and re-layouts  4.75 us (3%)
    all_to_all x1, blocking collectives, local(): lax.all_to_all(spectra, 'ta', split_axis=0, concat_axis=0, tiled=True)  56 us
    ppermute x11, starting transfers between devices, moved(): return lax.ppermute(block, 'aa', pairs)  32.6 us
    ppermute x11, waiting for transfers between devices, moved(): return lax.ppermute(block, 'aa', pairs)  27.7 us
    ppermute x3, starting transfers between devices, work(): gots.append(lax.ppermute(leaving, 'aa', mate))  19.3 us
    pallas_call x3, Pallas kernels, correlated(): pl.pallas_call(functools.partial(correlate_kernel, plan), out_shape=(tile...  8.63 us
    pallas_call x2, Pallas kernels, placed(): pl.pallas_call(functools.partial(place_kernel, groups), out_shape=jax.Sha...  4.12 us
    ppermute x1, starting transfers between devices, local(): own_lead = lax.ppermute(lead, ('ta', 'aa'), later)  3.53 us
  transfers between devices with their start and end apart: 17, of which 7 were waited for; matrix products, arithmetic and copies ran while one was open for 2% of the time, Pallas kernels for 7%

profile of v6, /device:TPU:39, one launch (start us, length us, event | category | flops | bytes accessed | tf_op | source)
XLA Modules:
  0.0 169.1 jit_solution(17523388154016492343)
XLA Ops:
  0.0 2.6 %collective-permute-start = (f32[1536,128]{1,0:T(8,128)}, f32[1536,128]{1,0:T(8,128)S(1)}, u32[]{:S(2)}, u32[]{:S(2)}) collective-permute-start(f32[1536,128]{1,0:T(8,128)} %bitcast.13), channel_id=1, source_target_pairs={{0,1},{1,0},{2,3},{3,2},{4,5},{5,4},{6,7},{7,6},{8,9},{9,8},{10,11... | collective-permute-start | bytes 2359304 | tf_op jit(solution)/shard_map/ppermute | solution.py:306
  2.6 0.9 slice.18
  3.5 3.5 %collective-permute-start.1 = (f32[192,128]{1,0:T(8,128)S(1)}, f32[192,128]{1,0:T(8,128)S(1)}, u32[]{:S(2)}, u32[]{:S(2)}) collective-permute-start(f32[192,128]{1,0:T(8,128)S(1)} %bitcast.15), channel_id=1, source_target_pairs={{0,32},{1,33},{2,34},{3,35},{4,36},{5,37},{6,38},{7,39},{8,40},{9,... | collective-permute-start | bytes 294920 | tf_op jit(solution)/shard_map/ppermute | solution.py:304
  7.0 0.8 broadcast_in_dim.36
  7.8 0.1 broadcast_in_dim.37
  7.9 1.9 %collective-permute-done.1.own_lead_ref = f32[192,128]{1,0:T(8,128)S(1)} collective-permute-done((f32[192,128]{1,0:T(8,128)S(1)}, f32[192,128]{1,0:T(8,128)S(1)}, u32[]{:S(2)}, u32[]{:S(2)}) %collective-permute-start.1) | collective-permute-done | bytes 98336 | tf_op jit(solution)/shard_map/ppermute | solution.py:304
  9.8 2.7 %collective-permute-start.2 = (f32[192,128]{1,0:T(8,128)S(1)}, f32[192,128]{1,0:T(8,128)S(1)}, u32[]{:S(2)}, u32[]{:S(2)}) collective-permute-start(f32[192,128]{1,0:T(8,128)S(1)} %collective-permute-done.1.own_lead_ref), channel_id=1, source_target_pairs={{0,1},{1,0},{2,3},{3,2},{4,5},{5,4},{6,7},{7,6},{8,9},{9,8},{10,11... | collective-permute-start | bytes 294920 | tf_op jit(solution)/shard_map/ppermute | solution.py:305
  12.5 0.1 pad_add_fusion.k_ref.at_ref
  12.6 0.8 collective-permute-done.2.other_lead_ref
  13.4 0.0 collective-permute-done.other_ref
  13.4 0.1 broadcast_in_dim.38.taps_ref
  13.5 0.0 copy-start
  13.5 1.2 copy-done
  14.7 0.0 copy-start.1
  14.7 1.1 copy-done.1
  15.9 2.7 %shard_map.46 = f32[16,24,512]{2,1,0:T(8,128)S(1)} custom-call(s32[2]{0:T(128)S(1)} %pad_add_fusion.k_ref.at_ref, f32[1536,128]{1,0:T(8,128)S(1)} %bitcast.14, f32[1536,128]{1,0:T(8,128)S(1)} %collective-permute-done.other_ref, f32[192,128]{1,0:T(8,128)S(1)} %collective-permute-done.1.own_lead_ref, f32[192,128]{1,0:T(8,128)S(1)} %collective-permute-done.2.other_lead_ref, ...), custom_call_target="tpu_custom_call" | custom-call | tf_op jit(solution)/shard_map/pallas_call | solution.py:76
  18.6 56.0 %all_to_all.5 = f32[16,24,512]{2,1,0:T(8,128)S(1)} all-to-all(f32[16,24,512]{2,1,0:T(8,128)S(1)} %shard_map.46), channel_id=1, replica_groups=mesh['ta'=16,'aa'=32] {'ta'}, dimensions={0} | all-to-all | bytes 1572864 | tf_op jit(solution)/shard_map/all_to_all | solution.py:308
  74.6 4.6 %collective-permute-start.3 = (f32[384,512]{1,0:T(8,128)S(1)}, f32[384,512]{1,0:T(8,128)}, u32[]{:S(2)}, u32[]{:S(2)}) collective-permute-start(f32[384,512]{1,0:T(8,128)S(1)} %bitcast.9), channel_id=1, source_target_pairs={{8,0},{9,1},{10,2},{11,3},{12,4},{13,5},{14,6},{15,7},{16,8},{17,9... | collective-permute-start | bytes 2359304 | tf_op jit(solution)/shard_map/ppermute | solution.py:118
  79.2 2.5 %collective-permute-start.7 = (f32[384,512]{1,0:T(8,128)S(1)}, f32[384,512]{1,0:T(8,128)S(1)}, u32[]{:S(2)}, u32[]{:S(2)}) collective-permute-start(f32[384,512]{1,0:T(8,128)S(1)} %bitcast.10), channel_id=1, source_target_pairs={{2,0},{3,1},{4,2},{5,3},{6,4},{7,5},{10,8},{11,9},{12,10},{13,11},... | collective-permute-start | bytes 2359304 | tf_op jit(solution)/shard_map/ppermute | solution.py:118
  81.7 12.7 %collective-permute-done.3.refs_1_ = f32[384,512]{1,0:T(8,128)} collective-permute-done((f32[384,512]{1,0:T(8,128)S(1)}, f32[384,512]{1,0:T(8,128)}, u32[]{:S(2)}, u32[]{:S(2)}) %collective-permute-start.3) | collective-permute-done | bytes 786464 | tf_op jit(solution)/shard_map/ppermute | solution.py:118
  94.4 2.1 %collective-permute-start.6 = (f32[384,512]{1,0:T(8,128)}, f32[384,512]{1,0:T(8,128)S(1)}, u32[]{:S(2)}, u32[]{:S(2)}) collective-permute-start(f32[384,512]{1,0:T(8,128)} %collective-permute-done.3.refs_1_), channel_id=1, source_target_pairs={{6,0},{7,1},{0,2},{1,3},{2,4},{3,5},{4,6},{5,7},{14,8},{15,9},{8,1... | collective-permute-start | bytes 2359304 | tf_op jit(solution)/shard_map/ppermute | solution.py:118
  96.5 3.2 %collective-permute-start.5 = (f32[384,512]{1,0:T(8,128)}, f32[384,512]{1,0:T(8,128)S(1)}, u32[]{:S(2)}, u32[]{:S(2)}) collective-permute-start(f32[384,512]{1,0:T(8,128)} %collective-permute-done.3.refs_1_), channel_id=1, source_target_pairs={{2,0},{3,1},{4,2},{5,3},{6,4},{7,5},{0,6},{1,7},{10,8},{11,9},{12,... | collective-permute-start | bytes 2359304 | tf_op jit(solution)/shard_map/ppermute | solution.py:118
  99.7 5.4 %collective-permute-start.4 = (f32[384,512]{1,0:T(8,128)}, f32[384,512]{1,0:T(8,128)}, u32[]{:S(2)}, u32[]{:S(2)}) collective-permute-start(f32[384,512]{1,0:T(8,128)} %collective-permute-done.3.refs_1_), channel_id=1, source_target_pairs={{8,0},{9,1},{10,2},{11,3},{12,4},{13,5},{14,6},{15,7},{16,8},{17,9... | collective-permute-start | bytes 2359304 | tf_op jit(solution)/shard_map/ppermute | solution.py:118
  105.1 0.0 collective-permute-done.7.refs_1_
  105.2 8.0 %collective-permute-done.6.refs_4_ = f32[384,512]{1,0:T(8,128)S(1)} collective-permute-done((f32[384,512]{1,0:T(8,128)}, f32[384,512]{1,0:T(8,128)S(1)}, u32[]{:S(2)}, u32[]{:S(2)}) %collective-permute-start.6) | collective-permute-done | bytes 786464 | tf_op jit(solution)/shard_map/ppermute | solution.py:118
  113.1 2.9 %collective-permute-done.5.refs_3_ = f32[384,512]{1,0:T(8,128)S(1)} collective-permute-done((f32[384,512]{1,0:T(8,128)}, f32[384,512]{1,0:T(8,128)S(1)}, u32[]{:S(2)}, u32[]{:S(2)}) %collective-permute-start.5) | collective-permute-done | bytes 786464 | tf_op jit(solution)/shard_map/ppermute | solution.py:118
  116.1 3.1 %collective-permute-done.4.refs_2_ = f32[384,512]{1,0:T(8,128)} collective-permute-done((f32[384,512]{1,0:T(8,128)}, f32[384,512]{1,0:T(8,128)}, u32[]{:S(2)}, u32[]{:S(2)}) %collective-permute-start.4) | collective-permute-done | bytes 786464 | tf_op jit(solution)/shard_map/ppermute | solution.py:118
  119.2 0.4 broadcast_select_fusion.1
  119.5 3.3 %collective-permute-start.13 = (f32[384,512]{1,0:T(8,128)S(1)}, f32[384,512]{1,0:T(8,128)S(1)}, u32[]{:S(2)}, u32[]{:S(2)}) collective-permute-start(f32[384,512]{1,0:T(8,128)S(1)} %get-tuple-element.17), channel_id=1, source_target_pairs={{6,0},{7,1},{0,2},{1,3},{2,4},{3,5},{4,6},{5,7},{14,8},{15,9},{8,1... | collective-permute-start | bytes 2359304 | tf_op jit(solution)/shard_map/ppermute | solution.py:118
  122.9 5.3 %collective-permute-start.9 = (f32[384,512]{1,0:T(8,128)S(1)}, f32[384,512]{1,0:T(8,128)S(1)}, u32[]{:S(2)}, u32[]{:S(2)}) collective-permute-start(f32[384,512]{1,0:T(8,128)S(1)} %get-tuple-element.18), channel_id=1, source_target_pairs={{10,2},{11,3},{14,6},{15,7},{18,10},{19,11},{22,14},{23,15},{26,18... | collective-permute-start | bytes 2359304 | tf_op jit(solution)/shard_map/ppermute | solution.py:118
  128.2 1.9 %collective-permute-start.8 = (f32[384,512]{1,0:T(8,128)S(1)}, f32[384,512]{1,0:T(8,128)S(1)}, u32[]{:S(2)}, u32[]{:S(2)}) collective-permute-start(f32[384,512]{1,0:T(8,128)S(1)} %get-tuple-element.19), channel_id=1, source_target_pairs={{2,0},{3,1},{4,2},{5,3},{6,4},{7,5},{0,6},{1,7},{10,8},{11,9},{12,... | collective-permute-start | bytes 2359304 | tf_op jit(solution)/shard_map/ppermute | solution.py:118
  130.1 0.3 shard_map.47.left_ref
  130.4 0.7 collective-permute-start.12
  131.1 4.7 %shard_map.48 = (f32[10,2,128,128]{3,2,1,0:T(8,128)S(1)}, f32[10,2,128,128]{3,2,1,0:T(8,128)S(1)}) custom-call(s32[2]{0:T(128)S(1)} %pad_add_fusion.k_ref.at_ref, bf16[2,512,768]{2,1,0:T(8,128)(2,1)S(1)} %shard_map.47.left_ref, f32[384,512]{1,0:T(8,128)S(1)} %bitcast.12, f32[384,512]{1,0:T(8,128)} %collective-permute-done.3.refs_1_, ...), custom_call_target="tpu_custom_call" | custom-call | flops 3019898880 | bytes 5898240 | tf_op jit(solution)/shard_map/pallas_call | solution.py:217
  135.8 6.5 %collective-permute-start.10 = (f32[10,2,128,128]{3,2,1,0:T(8,128)S(1)}, f32[10,2,128,128]{3,2,1,0:T(8,128)S(1)}, u32[]{:S(2)}, u32[]{:S(2)}) collective-permute-start(f32[10,2,128,128]{3,2,1,0:T(8,128)S(1)} %get-tuple-element.13), channel_id=1, source_target_pairs={{0,1},{1,0},{2,3},{3,2},{4,5},{5,4},{6,7},{7,6},{8,9},{9,8},{10,11... | collective-permute-start | bytes 3932168 | tf_op jit(solution)/shard_map/ppermute | solution.py:319
  142.3 0.5 slice.20
  143.4 0.0 collective-permute-done.13.refs_2_
  143.5 0.0 collective-permute-done.9.refs_2_.refs_1_
  143.5 0.1 slice_select_fusion
  143.5 1.3 collective-permute-start.14
  144.8 1.0 collective-permute-done.8.refs_0_
  145.8 2.2 %collective-permute-start.15 = (f32[192,512]{1,0:T(8,128)S(1)}, f32[192,512]{1,0:T(8,128)S(1)}, u32[]{:S(2)}, u32[]{:S(2)}) collective-permute-start(f32[192,512]{1,0:T(8,128)S(1)} %slice.26), channel_id=1, source_target_pairs={{12,4},{13,5},{14,6},{15,7},{20,12},{21,13},{22,14},{23,15},{28,20... | collective-permute-start | bytes 1179656 | tf_op jit(solution)/shard_map/ppermute | solution.py:118
  148.0 2.0 %shard_map.49 = (f32[4,2,128,128]{3,2,1,0:T(8,128)S(1)}, f32[4,2,128,128]{3,2,1,0:T(8,128)S(1)}) custom-call(s32[2]{0:T(128)S(1)} %pad_add_fusion.k_ref.at_ref, bf16[2,512,768]{2,1,0:T(8,128)(2,1)S(1)} %shard_map.47.left_ref, f32[384,512]{1,0:T(8,128)S(1)} %collective-permute-done.8.refs_0_, f32[384,512]{1,0:T(8,128)S(1)} %collective-permute-done.7.refs_1_, ...), custom_call_target="tpu_custom_call" | custom-call | flops 1207959552 | bytes 2359296 | tf_op jit(solution)/shard_map/pallas_call | solution.py:217
  150.0 0.0 copy-start.2
  150.0 7.4 %collective-permute-start.11 = (f32[4,2,128,128]{3,2,1,0:T(8,128)S(1)}, f32[4,2,128,128]{3,2,1,0:T(8,128)S(1)}, u32[]{:S(2)}, u32[]{:S(2)}) collective-permute-start(f32[4,2,128,128]{3,2,1,0:T(8,128)S(1)} %get-tuple-element.14), channel_id=1, source_target_pairs={{0,1},{1,0},{2,3},{3,2},{4,5},{5,4},{6,7},{7,6},{8,9},{9,8},{10,11... | collective-permute-start | bytes 1572872 | tf_op jit(solution)/shard_map/ppermute | solution.py:319
  157.4 0.0 collective-permute-done.12.refs_0_
  157.4 0.0 collective-permute-done.14.refs_3_
  157.4 0.0 collective-permute-done.15.refs_4_
  157.4 2.0 %shard_map.51 = (f32[4,2,128,128]{3,2,1,0:T(8,128)S(1)}, f32[4,2,128,128]{3,2,1,0:T(8,128)S(1)}) custom-call(s32[2]{0:T(128)S(1)} %pad_add_fusion.k_ref.at_ref, bf16[2,512,768]{2,1,0:T(8,128)(2,1)S(1)} %shard_map.47.left_ref, f32[384,512]{1,0:T(8,128)S(1)} %collective-permute-done.12.refs_0_, f32[384,512]{1,0:T(8,128)S(1)} %collective-permute-done.9.refs_2_.refs_1_, ...), custom_call_target="tpu_custom_call" | custom-call | flops 1207959552 | bytes 2359296 | tf_op jit(solution)/shard_map/pallas_call | solution.py:217
  159.4 5.4 %collective-permute-start.16 = (f32[4,2,128,128]{3,2,1,0:T(8,128)S(1)}, f32[4,2,128,128]{3,2,1,0:T(8,128)S(1)}, u32[]{:S(2)}, u32[]{:S(2)}) collective-permute-start(f32[4,2,128,128]{3,2,1,0:T(8,128)S(1)} %get-tuple-element.16), channel_id=1, source_target_pairs={{0,1},{1,0},{2,3},{3,2},{4,5},{5,4},{6,7},{7,6},{8,9},{9,8},{10,11... | collective-permute-start | bytes 1572872 | tf_op jit(solution)/shard_map/ppermute | solution.py:319
  164.9 0.0 copy-done.2
  164.9 0.1 select_reduce_fusion.slot_ref
  165.0 0.0 collective-permute-done.11.refs_3_
  165.0 0.0 collective-permute-done.10.refs_2_
  165.0 2.5 %shard_map.50.refs_0_ = f32[17,2,2,128,128]{4,3,2,1,0:T(8,128)} custom-call(s32[2]{0:T(128)S(1)} %pad_add_fusion.k_ref.at_ref, s32[17]{0:T(128)S(1)} %select_reduce_fusion.slot_ref, f32[10,2,128,128]{3,2,1,0:T(8,128)S(1)} %get-tuple-element.11.refs_0_, f32[4,2,128,128]{3,2,1,0:T(8,128)S(1)} %get-tuple-element.12.refs_1_, ...), custom_call_target="tpu_custom_call" | custom-call | bytes 3670016 | tf_op jit(solution)/shard_map/pallas_call | solution.py:279
  167.5 0.0 collective-permute-done.16.refs_2_
  167.6 1.6 shard_map.52
  (1 shorter events, 0.0 us)
Async XLA Ops:
  0.0 13.4 %collective-permute-start = (f32[1536,128]{1,0:T(8,128)}, f32[1536,128]{1,0:T(8,128)S(1)}, u32[]{:S(2)}, u32[]{:S(2)}) collective-permute-start(f32[1536,128]{1,0:T(8,128)} %bitcast.13), channel_id=1, source_target_pairs={{0,1},{1,0},{2,3},{3,2},{4,5},{5,4},{6,7},{7,6},{8,9},{9,8},{10,11... | collective-permute-start | bytes 2359304 | tf_op jit(solution)/shard_map/ppermute | solution.py:306
  3.5 6.3 %collective-permute-start.1 = (f32[192,128]{1,0:T(8,128)S(1)}, f32[192,128]{1,0:T(8,128)S(1)}, u32[]{:S(2)}, u32[]{:S(2)}) collective-permute-start(f32[192,128]{1,0:T(8,128)S(1)} %bitcast.15), channel_id=1, source_target_pairs={{0,32},{1,33},{2,34},{3,35},{4,36},{5,37},{6,38},{7,39},{8,40},{9,... | collective-permute-start | bytes 294920 | tf_op jit(solution)/shard_map/ppermute | solution.py:304
  9.8 3.6 %collective-permute-start.2 = (f32[192,128]{1,0:T(8,128)S(1)}, f32[192,128]{1,0:T(8,128)S(1)}, u32[]{:S(2)}, u32[]{:S(2)}) collective-permute-start(f32[192,128]{1,0:T(8,128)S(1)} %collective-permute-done.1.own_lead_ref), channel_id=1, source_target_pairs={{0,1},{1,0},{2,3},{3,2},{4,5},{5,4},{6,7},{7,6},{8,9},{9,8},{10,11... | collective-permute-start | bytes 294920 | tf_op jit(solution)/shard_map/ppermute | solution.py:305
  13.5 1.2 copy-start
  14.7 1.1 copy-start.1
  74.6 19.9 %collective-permute-start.3 = (f32[384,512]{1,0:T(8,128)S(1)}, f32[384,512]{1,0:T(8,128)}, u32[]{:S(2)}, u32[]{:S(2)}) collective-permute-start(f32[384,512]{1,0:T(8,128)S(1)} %bitcast.9), channel_id=1, source_target_pairs={{8,0},{9,1},{10,2},{11,3},{12,4},{13,5},{14,6},{15,7},{16,8},{17,9... | collective-permute-start | bytes 2359304 | tf_op jit(solution)/shard_map/ppermute | solution.py:118
  79.2 25.9 %collective-permute-start.7 = (f32[384,512]{1,0:T(8,128)S(1)}, f32[384,512]{1,0:T(8,128)S(1)}, u32[]{:S(2)}, u32[]{:S(2)}) collective-permute-start(f32[384,512]{1,0:T(8,128)S(1)} %bitcast.10), channel_id=1, source_target_pairs={{2,0},{3,1},{4,2},{5,3},{6,4},{7,5},{10,8},{11,9},{12,10},{13,11},... | collective-permute-start | bytes 2359304 | tf_op jit(solution)/shard_map/ppermute | solution.py:118
  94.4 18.7 %collective-permute-start.6 = (f32[384,512]{1,0:T(8,128)}, f32[384,512]{1,0:T(8,128)S(1)}, u32[]{:S(2)}, u32[]{:S(2)}) collective-permute-start(f32[384,512]{1,0:T(8,128)} %collective-permute-done.3.refs_1_), channel_id=1, source_target_pairs={{6,0},{7,1},{0,2},{1,3},{2,4},{3,5},{4,6},{5,7},{14,8},{15,9},{8,1... | collective-permute-start | bytes 2359304 | tf_op jit(solution)/shard_map/ppermute | solution.py:118
  96.5 19.6 %collective-permute-start.5 = (f32[384,512]{1,0:T(8,128)}, f32[384,512]{1,0:T(8,128)S(1)}, u32[]{:S(2)}, u32[]{:S(2)}) collective-permute-start(f32[384,512]{1,0:T(8,128)} %collective-permute-done.3.refs_1_), channel_id=1, source_target_pairs={{2,0},{3,1},{4,2},{5,3},{6,4},{7,5},{0,6},{1,7},{10,8},{11,9},{12,... | collective-permute-start | bytes 2359304 | tf_op jit(solution)/shard_map/ppermute | solution.py:118
  99.7 19.5 %collective-permute-start.4 = (f32[384,512]{1,0:T(8,128)}, f32[384,512]{1,0:T(8,128)}, u32[]{:S(2)}, u32[]{:S(2)}) collective-permute-start(f32[384,512]{1,0:T(8,128)} %collective-permute-done.3.refs_1_), channel_id=1, source_target_pairs={{8,0},{9,1},{10,2},{11,3},{12,4},{13,5},{14,6},{15,7},{16,8},{17,9... | collective-permute-start | bytes 2359304 | tf_op jit(solution)/shard_map/ppermute | solution.py:118
  119.5 23.9 %collective-permute-start.13 = (f32[384,512]{1,0:T(8,128)S(1)}, f32[384,512]{1,0:T(8,128)S(1)}, u32[]{:S(2)}, u32[]{:S(2)}) collective-permute-start(f32[384,512]{1,0:T(8,128)S(1)} %get-tuple-element.17), channel_id=1, source_target_pairs={{6,0},{7,1},{0,2},{1,3},{2,4},{3,5},{4,6},{5,7},{14,8},{15,9},{8,1... | collective-permute-start | bytes 2359304 | tf_op jit(solution)/shard_map/ppermute | solution.py:118
  122.9 20.6 %collective-permute-start.9 = (f32[384,512]{1,0:T(8,128)S(1)}, f32[384,512]{1,0:T(8,128)S(1)}, u32[]{:S(2)}, u32[]{:S(2)}) collective-permute-start(f32[384,512]{1,0:T(8,128)S(1)} %get-tuple-element.18), channel_id=1, source_target_pairs={{10,2},{11,3},{14,6},{15,7},{18,10},{19,11},{22,14},{23,15},{26,18... | collective-permute-start | bytes 2359304 | tf_op jit(solution)/shard_map/ppermute | solution.py:118
  128.2 17.6 %collective-permute-start.8 = (f32[384,512]{1,0:T(8,128)S(1)}, f32[384,512]{1,0:T(8,128)S(1)}, u32[]{:S(2)}, u32[]{:S(2)}) collective-permute-start(f32[384,512]{1,0:T(8,128)S(1)} %get-tuple-element.19), channel_id=1, source_target_pairs={{2,0},{3,1},{4,2},{5,3},{6,4},{7,5},{0,6},{1,7},{10,8},{11,9},{12,... | collective-permute-start | bytes 2359304 | tf_op jit(solution)/shard_map/ppermute | solution.py:118
  130.4 27.0 %collective-permute-start.12 = (f32[384,512]{1,0:T(8,128)S(1)}, f32[384,512]{1,0:T(8,128)S(1)}, u32[]{:S(2)}, u32[]{:S(2)}) collective-permute-start(f32[384,512]{1,0:T(8,128)S(1)} %collective-permute-done.6.refs_4_), channel_id=1, source_target_pairs={{24,0},{25,1},{0,8},{1,9},{8,16},{9,17},{16,24},{17,25},{56,32},{5... | collective-permute-start | bytes 2359304 | tf_op jit(solution)/shard_map/ppermute | solution.py:118
  135.8 29.2 %collective-permute-start.10 = (f32[10,2,128,128]{3,2,1,0:T(8,128)S(1)}, f32[10,2,128,128]{3,2,1,0:T(8,128)S(1)}, u32[]{:S(2)}, u32[]{:S(2)}) collective-permute-start(f32[10,2,128,128]{3,2,1,0:T(8,128)S(1)} %get-tuple-element.13), channel_id=1, source_target_pairs={{0,1},{1,0},{2,3},{3,2},{4,5},{5,4},{6,7},{7,6},{8,9},{9,8},{10,11... | collective-permute-start | bytes 3932168 | tf_op jit(solution)/shard_map/ppermute | solution.py:319
  143.5 13.9 %collective-permute-start.14 = (f32[192,512]{1,0:T(8,128)S(1)}, f32[192,512]{1,0:T(8,128)S(1)}, u32[]{:S(2)}, u32[]{:S(2)}) collective-permute-start(f32[192,512]{1,0:T(8,128)S(1)} %slice_select_fusion), channel_id=1, source_target_pairs={{2,4},{3,5},{4,6},{5,7},{10,12},{11,13},{12,14},{13,15},{18,20},{1... | collective-permute-start | bytes 1179656 | tf_op jit(solution)/shard_map/ppermute | solution.py:118
  145.8 11.6 %collective-permute-start.15 = (f32[192,512]{1,0:T(8,128)S(1)}, f32[192,512]{1,0:T(8,128)S(1)}, u32[]{:S(2)}, u32[]{:S(2)}) collective-permute-start(f32[192,512]{1,0:T(8,128)S(1)} %slice.26), channel_id=1, source_target_pairs={{12,4},{13,5},{14,6},{15,7},{20,12},{21,13},{22,14},{23,15},{28,20... | collective-permute-start | bytes 1179656 | tf_op jit(solution)/shard_map/ppermute | solution.py:118
  150.0 14.9 %copy-start.2 = (s32[1,17]{1,0:T(1,128)S(1)}, s32[1,17]{1,0:T(1,128)}, u32[]{:S(2)}) copy-start(s32[1,17]{1,0:T(1,128)} %param.6) | copy-start | bytes 208
  150.0 15.0 %collective-permute-start.11 = (f32[4,2,128,128]{3,2,1,0:T(8,128)S(1)}, f32[4,2,128,128]{3,2,1,0:T(8,128)S(1)}, u32[]{:S(2)}, u32[]{:S(2)}) collective-permute-start(f32[4,2,128,128]{3,2,1,0:T(8,128)S(1)} %get-tuple-element.14), channel_id=1, source_target_pairs={{0,1},{1,0},{2,3},{3,2},{4,5},{5,4},{6,7},{7,6},{8,9},{9,8},{10,11... | collective-permute-start | bytes 1572872 | tf_op jit(solution)/shard_map/ppermute | solution.py:319
  159.4 8.1 %collective-permute-start.16 = (f32[4,2,128,128]{3,2,1,0:T(8,128)S(1)}, f32[4,2,128,128]{3,2,1,0:T(8,128)S(1)}, u32[]{:S(2)}, u32[]{:S(2)}) collective-permute-start(f32[4,2,128,128]{3,2,1,0:T(8,128)S(1)} %get-tuple-element.16), channel_id=1, source_target_pairs={{0,1},{1,0},{2,3},{3,2},{4,5},{5,4},{6,7},{7,6},{8,9},{9,8},{10,11... | collective-permute-start | bytes 1572872 | tf_op jit(solution)/shard_map/ppermute | solution.py:319
